TPU v7x, 32 devices: a whole 2x2x4 slice. The times are simulated.
32 devices in a mesh: seq: 8 (over z, x), head: 4 (over y, core).
Axes of the slice: x: 2, y: 2, z: 4, core: 2. Of those that a mesh axis runs over, the one named last changes fastest.
Arguments:
- queries: bfloat16 [4096, 4096], P('seq', 'head'), may hold values from -6 to 6
- keys: bfloat16 [4096, 1024], P('seq', 'head'), may hold values from -6 to 6
- values: bfloat16 [4096, 1024], P('seq', 'head'), may hold values from -6 to 6
- output_gradient: bfloat16 [4096, 4096], P('seq', 'head'), may hold values from -6 to 6
- doc_lengths: int32 [32], P(('seq', 'head')), may hold values from 1 to 512, 4096 in all
Outputs:
- grad_queries: bfloat16 [4096, 4096], P('seq', 'head')
- key_gradient: bfloat16 [4096, 1024], P('seq', 'head')
- value_gradient: bfloat16 [4096, 1024], P('seq', 'head')
Inputs may be any that keep to these rules, and one draw needn't show every extreme that they name: `doc_lengths`: the lengths sum to 4096; no document holds more than 512 tokens, and one holds exactly 512.
All inputs are finite; a program needn't handle non-finite values. No bound on the sum of `doc_lengths` on one device may be relied on, other than what follows from the above.
Results may differ from a plain program's by a relative error of at most 0.012.
Values may be sent and summed in bfloat16 or wider, within the bound.
No kernel may reach another device: no remote copies, remote signals or barrier semaphores. Data moves between devices by JAX's collectives and lax.ppermute only.
A program may use at most 64 MiB of HBM per device.

v0:
```python
import jax
import jax.numpy as jnp
from jax import lax
from jax.sharding import PartitionSpec as P

HEAD_WIDTH = 128


def shifted(value, axis, steps):
    count = lax.axis_size(axis)
    first, last = (max(0, -steps), min(count, count - steps))
    return lax.ppermute(value, axis, [(source, source + steps) for source in range(first, last)])


def doc_starts(lengths, positions):
    ends = jnp.cumsum(lengths, dtype=jnp.int32)
    starts = ends - lengths
    reached = starts[None, :] <= positions[:, None]
    return jnp.max(jnp.where(reached, starts[None, :], jnp.int32(0)), axis=1)


def window_mask(query_pos, query_start, key_pos):
    return (key_pos[None, :] >= query_start[:, None]) & (key_pos[None, :] <= query_pos[:, None])


def masked_scores(query_block, key_rows, allowed):
    raw = jnp.einsum("qgha,kga->ghqk", query_block, key_rows, preferred_element_type=jnp.float32)
    return jnp.where(allowed[None, None], raw * HEAD_WIDTH ** (-0.5), -jnp.inf)


def mixed_values(weights, value_rows):
    return jnp.einsum("ghqk,kga->qgha", weights, value_rows, preferred_element_type=jnp.float32)


def row_delta(grad_block, out):
    return jnp.sum(grad_block.astype(jnp.float32) * out, axis=-1)


def key_grads(prob, weights, delta, query_block, grad_block, key_rows, value_rows):
    dprob = jnp.einsum("qgha,kga->ghqk", grad_block, value_rows, preferred_element_type=jnp.float32)
    dscore = (
        prob * (dprob - jnp.transpose(delta, (1, 2, 0))[..., None]) * HEAD_WIDTH ** (-0.5)
    ).astype(jnp.bfloat16)
    grad_q = jnp.einsum("ghqk,kga->qgha", dscore, key_rows, preferred_element_type=jnp.float32)
    grad_k = jnp.einsum("ghqk,qgha->kga", dscore, query_block, preferred_element_type=jnp.float32)
    grad_v = jnp.einsum("ghqk,qgha->kga", weights, grad_block, preferred_element_type=jnp.float32)
    return (grad_q, grad_k, grad_v)


def body(queries, keys, values, output_gradient, doc_lengths):
    rows = queries.shape[0]
    kv_heads = keys.shape[1] // HEAD_WIDTH
    heads_per_group = queries.shape[1] // keys.shape[1]
    lengths = lax.all_gather(doc_lengths, ("seq", "head"), axis=0, tiled=True)
    first = lax.axis_index("seq") * rows
    own_pos = first + jnp.arange(rows, dtype=jnp.int32)
    prev_pos = own_pos - rows
    own_start = doc_starts(lengths, own_pos)
    prev_keys, prev_values = shifted((keys, values), "seq", 1)
    key_own = keys.reshape(rows, kv_heads, HEAD_WIDTH)
    value_own = values.reshape(rows, kv_heads, HEAD_WIDTH)
    key_prev = prev_keys.reshape(rows, kv_heads, HEAD_WIDTH)
    value_prev = prev_values.reshape(rows, kv_heads, HEAD_WIDTH)
    block = min(rows, 512)
    count = rows // block
    inputs = (
        queries.reshape(count, block, kv_heads, heads_per_group, HEAD_WIDTH),
        output_gradient.reshape(count, block, kv_heads, heads_per_group, HEAD_WIDTH),
        own_pos.reshape(count, block),
        own_start.reshape(count, block),
    )
    key_both = jnp.concatenate([key_prev, key_own], axis=0)
    value_both = jnp.concatenate([value_prev, value_own], axis=0)
    pos_both = jnp.concatenate([prev_pos, own_pos])

    def joint_step(carry, blk):
        query_block, grad_block, query_pos, query_start = blk
        scores = masked_scores(query_block, key_both, window_mask(query_pos, query_start, pos_both))
        expo = jnp.exp(scores - jnp.max(scores, axis=-1, keepdims=True))
        prob = expo / jnp.sum(expo, axis=-1, keepdims=True)
        weights = prob.astype(jnp.bfloat16)
        delta = row_delta(grad_block, mixed_values(weights, value_both))
        grad_q, grad_k, grad_v = key_grads(
            prob, weights, delta, query_block, grad_block, key_both, value_both
        )
        return ((carry[0] + grad_k, carry[1] + grad_v), grad_q)

    zero_both = jnp.zeros((2 * rows, kv_heads, HEAD_WIDTH), jnp.float32)
    (dk_all, dv_all), grad_q_blocks = lax.scan(joint_step, (zero_both, zero_both), inputs)
    send_keys, own_dk = (dk_all[:rows], dk_all[rows:])
    send_values, own_dv = (dv_all[:rows], dv_all[rows:])
    back_keys, back_values = (
        shifted(send_keys.astype(jnp.bfloat16), "seq", -1).astype(send_keys.dtype),
        shifted(send_values.astype(jnp.bfloat16), "seq", -1).astype(send_values.dtype),
    )
    grad_queries = grad_q_blocks.reshape(rows, kv_heads * heads_per_group * HEAD_WIDTH).astype(
        jnp.bfloat16
    )
    key_gradient = (own_dk + back_keys).reshape(rows, kv_heads * HEAD_WIDTH).astype(jnp.bfloat16)
    value_gradient = (
        (own_dv + back_values).reshape(rows, kv_heads * HEAD_WIDTH).astype(jnp.bfloat16)
    )
    return (grad_queries, key_gradient, value_gradient)


def solution(mesh):
    in_specs = (
        P("seq", "head"),
        P("seq", "head"),
        P("seq", "head"),
        P("seq", "head"),
        P(("seq", "head")),
    )
    out_specs = (P("seq", "head"), P("seq", "head"), P("seq", "head"))
    return jax.shard_map(body, mesh=mesh, in_specs=in_specs, out_specs=out_specs, check_vma=False)
```

profile of v0, /device:TPU:0, one launch (start us, length us, event | category | flops | bytes accessed | tf_op | source)
XLA Modules:
  0.0 113.5 jit_solution(9949465057944922737)
XLA Ops:
  0.6 1.1 copy.44
  1.7 4.9 %collective-permute-start = (bf16[512,256]{0,1:T(8,128)(2,1)S(1)}, bf16[512,256]{0,1:T(8,128)(2,1)S(1)}, u32[]{:S(2)}, u32[]{:S(2)}) collective-permute-start(bf16[512,256]{0,1:T(8,128)(2,1)S(1)} %copy.44), channel_id=1, source_target_pairs={{0,4},{4,8},{8,12},{12,16},{16,20},{20,24},{24,28},{1,5},{5,9},{9,... | collective-permute-start | bytes 786440 | tf_op jit(solution)/shard_map/ppermute | solution.py:12
  6.6 1.8 %copy.50 = bf16[512,256]{0,1:T(8,128)(2,1)} copy(bf16[512,256]{1,0:T(8,128)(2,1)} %param.7) | data formatting | bytes 524288 | tf_op args[2]
  8.4 4.2 %collective-permute-start.1 = (bf16[512,256]{0,1:T(8,128)(2,1)}, bf16[512,256]{0,1:T(8,128)(2,1)}, u32[]{:S(2)}, u32[]{:S(2)}) collective-permute-start(bf16[512,256]{0,1:T(8,128)(2,1)} %copy.50), channel_id=1, source_target_pairs={{0,4},{4,8},{8,12},{12,16},{16,20},{20,24},{24,28},{1,5},{5,9},{9,... | collective-permute-start | bytes 786440 | tf_op jit(solution)/shard_map/ppermute | solution.py:12
  13.3 40.6 %all-reduce = s32[32]{0:T(128)S(1)} all-reduce(s32[32]{0:T(128)S(1)} %dynamic-update-slice), channel_id=1, replica_groups=mesh['seq'=8,'head'=4] {'seq','head'}, use_global_device_ids=true, to_apply=%add | all-reduce | flops 32 | bytes 256
  54.5 1.5 %copy.81 = bf16[512,1024]{0,1:T(8,128)(2,1)S(1)} copy(bf16[512,1024]{1,0:T(8,128)(2,1)} %param.5) | data formatting | bytes 2097152 | tf_op jit(solution)/shard_map/while/body/jit(dynamic_index_in_dim)/squeeze | solution.py:89
  56.0 1.5 %copy.54 = bf16[512,1024]{0,1:T(8,128)(2,1)S(1)} copy(bf16[512,1024]{1,0:T(8,128)(2,1)} %param.8) | data formatting | bytes 2097152 | tf_op args[3]
  57.6 1.8 %copy.53 = bf16[512,2,128]{2,0,1:T(8,128)(2,1)} copy(bf16[512,2,128]{0,2,1:T(8,128)(2,1)} %bitcast.8) | data formatting | bytes 524288 | tf_op jit(solution)/shard_map/reshape | solution.py:61
  60.0 9.3 %fusion.24 = (f32[2,4,512]{2,1,0:T(4,128)S(1)}, f32[2,4,512,1024]{2,3,1,0:T(8,128)}) fusion(pred[512,1024]{0,1:T(8,128)(4,1)S(1)} %compare_and_fusion, bf16[512,2,4,128]{0,3,2,1:T(8,128)(2,1)S(1)} %bitcast.85, bf16[512,2,128]{2,0,1:T(8,128)(2,1)S(1)} %copy.47, bf16[512,2,128]{2,0,1:T(8,128)(2,1)S(1)} %copy.46), kind=kOutput, calls=%fused_computation.40 | convolution fusion | flops 1091568640 | bytes 18890752 | tf_op jit(solution)/shard_map/while/body/eval_jaxpr/sub | solution.py:79
  69.3 6.7 %fusion.8 = bf16[2,4,512,1024]{2,3,1,0:T(8,128)(2,1)S(1)} fusion(f32[2,4,512,1024]{2,3,1,0:T(8,128)} %get-tuple-element.46, f32[2,4,512]{2,1,0:T(4,128)S(1)} %get-tuple-element.45), kind=kLoop, calls=%fused_computation.12 | loop fusion | flops 8388608 | bytes 25182208 | tf_op jit(solution)/shard_map/while/body/eval_jaxpr/convert_element_type | solution.py:81
  76.1 3.2 %copy-done = bf16[2,4,512,1024]{2,3,1,0:T(8,128)(2,1)} copy-done((bf16[2,4,512,1024]{2,3,1,0:T(8,128)(2,1)}, bf16[2,4,512,1024]{2,3,1,0:T(8,128)(2,1)S(1)}, u32[]{:S(2)}) %copy-start) | copy-done | bytes 8388632
  79.3 2.8 %convolution_bitcast_fusion = f32[1024,2,128]{0,2,1:T(8,128)S(1)} fusion(bf16[2,4,512,1024]{2,3,1,0:T(8,128)(2,1)S(1)} %fusion.8, bf16[512,2,4,128]{0,3,2,1:T(8,128)(2,1)S(1)} %bitcast.82), kind=kOutput, calls=%fused_computation.18 | convolution fusion | flops 1073741824 | bytes 10485760 | tf_op jit(solution)/shard_map/while/body/eval_jaxpr/ghqk,qgha->kga/dot_general | solution.py:46
  82.8 1.3 %collective-permute-start.3 = (bf16[512,2,128]{0,2,1:T(8,128)(2,1)}, bf16[512,2,128]{0,2,1:T(8,128)(2,1)}, u32[]{:S(2)}, u32[]{:S(2)}) collective-permute-start(bf16[512,2,128]{0,2,1:T(8,128)(2,1)} %slice.30), channel_id=1, source_target_pairs={{4,0},{8,4},{12,8},{16,12},{20,16},{24,20},{28,24},{5,1},{9,5},{13... | collective-permute-start | bytes 786440 | tf_op jit(solution)/shard_map/ppermute | solution.py:12
  84.1 1.8 %copy.52 = bf16[512,2,128]{2,0,1:T(8,128)(2,1)} copy(bf16[512,2,128]{0,2,1:T(8,128)(2,1)} %bitcast.7) | data formatting | bytes 524288 | tf_op jit(solution)/shard_map/reshape | solution.py:63
  85.9 4.9 %fusion.9 = f32[512,2,4]{0,2,1:T(4,128)S(1)} fusion(bf16[512,2,4,128]{0,3,2,1:T(8,128)(2,1)S(1)} %bitcast.83, bf16[2,4,512,1024]{2,3,1,0:T(8,128)(2,1)} %copy-done, bf16[512,2,128]{2,0,1:T(8,128)(2,1)} %copy.53, bf16[512,2,128]{2,0,1:T(8,128)(2,1)} %copy.52), kind=kOutput, calls=%fused_computation.14 | convolution fusion | flops 1076359168 | bytes 9977856 | tf_op jit(solution)/shard_map/while/body/eval_jaxpr/ghqk,kga->qgha/dot_general | solution.py:32
  90.8 7.2 %fusion.3 = bf16[2,4,512,1024]{2,3,1,0:T(8,128)(2,1)S(1)} fusion(f32[2,4,512]{2,1,0:T(4,128)S(1)} %bitcast.92, f32[2,4,512,1024]{2,3,1,0:T(8,128)} %get-tuple-element.46, f32[2,4,512]{2,1,0:T(4,128)S(1)} %get-tuple-element.45, bf16[512,2,4,128]{0,3,2,1:T(8,128)(2,1)S(1)} %bitcast.84, bf16[512,2,128]{2,0,1:T(8,128)(2,1)S(1)} %copy-done.3, ...), kind=kOutput, calls=%fused_computation.4 | convolution fusion | flops 1095761920 | bytes 26771456 | tf_op jit(solution)/shard_map/while/body/eval_jaxpr/qgha,kga->ghqk/dot_general | solution.py:40
  98.1 2.8 %convolution_bitcast_fusion.1 = f32[1024,2,128]{0,2,1:T(8,128)S(1)} fusion(bf16[2,4,512,1024]{2,3,1,0:T(8,128)(2,1)S(1)} %fusion.3, bf16[512,2,4,128]{0,3,2,1:T(8,128)(2,1)S(1)} %bitcast.86), kind=kOutput, calls=%fused_computation.19 | convolution fusion | flops 1073741824 | bytes 10485760 | tf_op jit(solution)/shard_map/while/body/eval_jaxpr/ghqk,qgha->kga/dot_general | solution.py:45
  101.6 1.3 %collective-permute-start.2 = (bf16[512,2,128]{0,2,1:T(8,128)(2,1)}, bf16[512,2,128]{0,2,1:T(8,128)(2,1)}, u32[]{:S(2)}, u32[]{:S(2)}) collective-permute-start(bf16[512,2,128]{0,2,1:T(8,128)(2,1)} %slice.31), channel_id=1, source_target_pairs={{4,0},{8,4},{12,8},{16,12},{20,16},{24,20},{28,24},{5,1},{9,5},{13... | collective-permute-start | bytes 786440 | tf_op jit(solution)/shard_map/ppermute | solution.py:12
  102.9 1.3 %convolution_convert_fusion = bf16[2,128,4,512]{3,1,2,0:T(8,128)(2,1)S(1)} fusion(bf16[2,4,512,1024]{2,3,1,0:T(8,128)(2,1)S(1)} %fusion.3, bf16[512,2,128]{2,0,1:T(8,128)(2,1)S(1)} %copy.47, bf16[512,2,128]{2,0,1:T(8,128)(2,1)S(1)} %copy-done.2), kind=kOutput, calls=%fused_computation.17 | convolution fusion | flops 1075314688 | bytes 9961472 | tf_op jit(solution)/shard_map/while/body/eval_jaxpr/ghqk,kga->qgha/dot_general | solution.py:44
  104.2 1.3 %copy.63 = bf16[512,1024]{1,0:T(8,128)(2,1)} copy(bf16[512,1024]{0,1:T(8,128)(2,1)S(1)} %bitcast.87) | data formatting | bytes 2097152
  105.5 1.0 fusion.12
  106.6 0.8 copy.65
  107.4 4.3 %collective-permute-done.2 = bf16[512,2,128]{0,2,1:T(8,128)(2,1)} collective-permute-done((bf16[512,2,128]{0,2,1:T(8,128)(2,1)}, bf16[512,2,128]{0,2,1:T(8,128)(2,1)}, u32[]{:S(2)}, u32[]{:S(2)}) %collective-permute-start.2) | collective-permute-done | bytes 262176 | tf_op jit(solution)/shard_map/ppermute | solution.py:12
  111.7 1.0 fusion.13
  (28 shorter events, 3.6 us)
Async XLA Ops:
  1.7 58.1 %collective-permute-start = (bf16[512,256]{0,1:T(8,128)(2,1)S(1)}, bf16[512,256]{0,1:T(8,128)(2,1)S(1)}, u32[]{:S(2)}, u32[]{:S(2)}) collective-permute-start(bf16[512,256]{0,1:T(8,128)(2,1)S(1)} %copy.44), channel_id=1, source_target_pairs={{0,4},{4,8},{8,12},{12,16},{16,20},{20,24},{24,28},{1,5},{5,9},{9,... | collective-permute-start | bytes 786440 | tf_op jit(solution)/shard_map/ppermute | solution.py:12
  8.4 75.7 %collective-permute-start.1 = (bf16[512,256]{0,1:T(8,128)(2,1)}, bf16[512,256]{0,1:T(8,128)(2,1)}, u32[]{:S(2)}, u32[]{:S(2)}) collective-permute-start(bf16[512,256]{0,1:T(8,128)(2,1)} %copy.50), channel_id=1, source_target_pairs={{0,4},{4,8},{8,12},{12,16},{16,20},{20,24},{24,28},{1,5},{5,9},{9,... | collective-permute-start | bytes 786440 | tf_op jit(solution)/shard_map/ppermute | solution.py:12
  60.0 9.3 %copy-start.1 = (bf16[512,2,128]{2,0,1:T(8,128)(2,1)}, bf16[512,2,128]{2,0,1:T(8,128)(2,1)S(1)}, u32[]{:S(2)}) copy-start(bf16[512,2,128]{2,0,1:T(8,128)(2,1)S(1)} %copy.46) | copy-start | bytes 786436
  76.0 3.2 %copy-start = (bf16[2,4,512,1024]{2,3,1,0:T(8,128)(2,1)}, bf16[2,4,512,1024]{2,3,1,0:T(8,128)(2,1)S(1)}, u32[]{:S(2)}) copy-start(bf16[2,4,512,1024]{2,3,1,0:T(8,128)(2,1)S(1)} %fusion.8) | copy-start | bytes 25165828
  82.8 22.8 %collective-permute-start.3 = (bf16[512,2,128]{0,2,1:T(8,128)(2,1)}, bf16[512,2,128]{0,2,1:T(8,128)(2,1)}, u32[]{:S(2)}, u32[]{:S(2)}) collective-permute-start(bf16[512,2,128]{0,2,1:T(8,128)(2,1)} %slice.30), channel_id=1, source_target_pairs={{4,0},{8,4},{12,8},{16,12},{20,16},{24,20},{28,24},{5,1},{9,5},{13... | collective-permute-start | bytes 786440 | tf_op jit(solution)/shard_map/ppermute | solution.py:12
  85.9 5.0 %copy-start.3 = (bf16[512,2,128]{2,0,1:T(8,128)(2,1)S(1)}, bf16[512,2,128]{2,0,1:T(8,128)(2,1)}, u32[]{:S(2)}) copy-start(bf16[512,2,128]{2,0,1:T(8,128)(2,1)} %copy.53) | copy-start | bytes 786436
  85.9 5.0 %copy-start.4 = (bf16[512,2,128]{2,0,1:T(8,128)(2,1)S(1)}, bf16[512,2,128]{2,0,1:T(8,128)(2,1)}, u32[]{:S(2)}) copy-start(bf16[512,2,128]{2,0,1:T(8,128)(2,1)} %copy.52) | copy-start | bytes 786436
  98.1 4.8 %copy-start.2 = (bf16[512,2,128]{2,0,1:T(8,128)(2,1)S(1)}, bf16[512,2,128]{2,0,1:T(8,128)(2,1)}, u32[]{:S(2)}) copy-start(bf16[512,2,128]{2,0,1:T(8,128)(2,1)} %copy-done.1) | copy-start | bytes 786436
  101.6 10.1 %collective-permute-start.2 = (bf16[512,2,128]{0,2,1:T(8,128)(2,1)}, bf16[512,2,128]{0,2,1:T(8,128)(2,1)}, u32[]{:S(2)}, u32[]{:S(2)}) collective-permute-start(bf16[512,2,128]{0,2,1:T(8,128)(2,1)} %slice.31), channel_id=1, source_target_pairs={{4,0},{8,4},{12,8},{16,12},{20,16},{24,20},{28,24},{5,1},{9,5},{13... | collective-permute-start | bytes 786440 | tf_op jit(solution)/shard_map/ppermute | solution.py:12
where the time goes:
time: 114 us
  blocking collectives  40.6 us (36%)
  matrix products  28.3 us (25%)
  local copies, waits for them, and re-layouts  17.7 us (16%)
  starting transfers between devices  11.6 us (10%)
  other arithmetic  9.55 us (8%)
  waiting for transfers between devices  4.27 us (4%)
  between operations  1.51 us (1%)
    unnamed x1, blocking collectives  40.6 us
    ppermute x4, starting transfers between devices, shifted(): lax.ppermute(value, axis, [(source, source + steps) for source in range(f...  11.6 us
    unnamed x18, local copies, waits for them, and re-layouts  10.7 us
    sub x1, matrix products, joint_step(): expo = jnp.exp(scores - jnp.max(scores, axis=-1, keepdims=True))  9.26 us
    dot_general x1, matrix products, key_grads(): jnp.einsum('qgha,kga->ghqk', grad_block, value_rows, preferred_element_ty...  7.23 us
    convert_element_type x1, other arithmetic, joint_step(): weights = prob.astype(jnp.bfloat16)  6.75 us
    dot_general x1, matrix products, mixed_values(): jnp.einsum('ghqk,kga->qgha', weights, value_rows, preferred_element_type=...  4.95 us
    ppermute x4, waiting for transfers between devices, shifted(): lax.ppermute(value, axis, [(source, source + steps) for source in range(f...  4.27 us
  transfers between devices with their start and end apart: 4, of which 1 were waited for; matrix products, arithmetic and copies ran while one was open for 43% of the time, Pallas kernels for 0%

commit v1 on v0

v1 whole, which is shorter than its diff:
```python
import functools

import jax
import jax.numpy as jnp
from jax import lax
from jax.experimental import pallas as pl
from jax.experimental.pallas import tpu as pltpu
from jax.sharding import PartitionSpec as P

HEAD_WIDTH = 128
BLOCK = 128
SCALE = HEAD_WIDTH ** (-0.5)
LOG2E = 1.4426950408889634
NT = (((1,), (1,)), ((), ()))
NN = (((1,), (0,)), ((), ()))
TN = (((0,), (0,)), ((), ()))


def dot(a, b, dims):
    return lax.dot_general(a, b, dims, preferred_element_type=jnp.float32)


def shifted(value, axis, steps):
    count = lax.axis_size(axis)
    first, last = (max(0, -steps), min(count, count - steps))
    return lax.ppermute(value, axis, [(source, source + steps) for source in range(first, last)])


def summed_everywhere(value, axes):
    for axis in axes:
        count = lax.axis_size(axis)
        if count & (count - 1):
            value = lax.psum(value, axis)
            continue
        step = 1
        while step < count:
            value = value + lax.ppermute(value, axis, [(s, s ^ step) for s in range(count)])
            step *= 2
    return value


def gathered_lengths(doc_lengths):
    own = doc_lengths.shape[0]
    place = lax.axis_index("seq") * lax.axis_size("head") + lax.axis_index("head")
    docs = own * lax.axis_size("seq") * lax.axis_size("head")
    row = jnp.zeros((1, docs), jnp.int32)
    row = lax.dynamic_update_slice(row, doc_lengths.reshape(1, own), (0, place * own))
    return summed_everywhere(row, ("head", "seq"))


def start_row(lengths, first, rows):
    docs = lengths.shape[1]
    before = lax.broadcasted_iota(jnp.int32, (docs, docs), 1) < lax.broadcasted_iota(
        jnp.int32, (docs, docs), 0
    )
    starts = jnp.sum(
        jnp.where(before, jnp.broadcast_to(lengths, (docs, docs)), 0), axis=1, keepdims=True
    )
    starts = jnp.broadcast_to(starts - first, (docs, rows))
    own = lax.broadcasted_iota(jnp.int32, (docs, rows), 1)
    return jnp.max(jnp.where(starts <= own, starts, -first), axis=0, keepdims=True)


def heads_stacked(ref, rows, heads):
    return jnp.concatenate(
        [ref[rows, h * HEAD_WIDTH : (h + 1) * HEAD_WIDTH] for h in range(heads)], axis=0
    )


def masked(scores, start, query, first_key, diagonal):
    keys = scores.shape[0]
    key = first_key + lax.broadcasted_iota(jnp.int32, (keys, BLOCK), 0)
    allowed = key >= start
    if diagonal:
        allowed = allowed & (key <= query)
    return jnp.concatenate(
        [
            jnp.where(allowed, scores[:, c : c + BLOCK], -jnp.inf)
            for c in range(0, scores.shape[1], BLOCK)
        ],
        axis=1,
    )


def block_scores(i, rows, heads, q_ref, k_ref, pk_ref, start):
    at = slice(i * BLOCK, (i + 1) * BLOCK)
    query_rows = heads_stacked(q_ref, at, heads)
    query = i * BLOCK + lax.broadcasted_iota(jnp.int32, (1, BLOCK), 1)
    start = start[:, at]
    prev = masked(dot(pk_ref[i * BLOCK :, :], query_rows, NT), start, query, i * BLOCK - rows, False)
    own = masked(dot(k_ref[: (i + 1) * BLOCK, :], query_rows, NT), start, query, 0, True)
    return query_rows, prev, own


def prev_kernel(
    first_ref, len_ref, q_ref, g_ref, k_ref, v_ref, pk_ref, pv_ref,
    send_ref, stat_ref, start_ref, dk_ref, dv_ref,
):
    rows, width = q_ref.shape
    heads = width // HEAD_WIDTH
    first = first_ref[0]
    start = start_row(len_ref[...], first, rows)
    start_ref[...] = start
    for i in range(rows // BLOCK):
        at = slice(i * BLOCK, (i + 1) * BLOCK)
        query_rows, prev, own = block_scores(i, rows, heads, q_ref, k_ref, pk_ref, start)
        grad_rows = heads_stacked(g_ref, at, heads)
        top = jnp.maximum(
            jnp.max(prev, axis=0, keepdims=True), jnp.max(own, axis=0, keepdims=True)
        )
        prev = jnp.exp2((prev - top) * (SCALE * LOG2E))
        own = jnp.exp2((own - top) * (SCALE * LOG2E))
        total = jnp.sum(prev, axis=0, keepdims=True) + jnp.sum(own, axis=0, keepdims=True)
        inverse = 1.0 / total
        dprev = dot(pv_ref[i * BLOCK :, :], grad_rows, NT)
        down = dot(v_ref[: (i + 1) * BLOCK, :], grad_rows, NT)
        delta = inverse * (
            jnp.sum(prev * dprev, axis=0, keepdims=True) + jnp.sum(own * down, axis=0, keepdims=True)
        )
        prob = prev * inverse
        dscore = (prob * (dprev - delta)).astype(jnp.bfloat16)
        dv = dot(prob.astype(jnp.bfloat16), grad_rows, NN)
        dk = dot(dscore, query_rows, NN)
        if i == 0:
            dv_ref[...] = dv
            dk_ref[...] = dk
        else:
            dv_ref[i * BLOCK :, :] += dv
            dk_ref[i * BLOCK :, :] += dk
        stat_ref[i, 0:1, :] = top
        stat_ref[i, 1:2, :] = inverse
        stat_ref[i, 2:3, :] = delta
    send_ref[:, :HEAD_WIDTH] = (dk_ref[...] * SCALE).astype(jnp.bfloat16)
    send_ref[:, HEAD_WIDTH:] = dv_ref[...].astype(jnp.bfloat16)


def own_kernel(
    q_ref, g_ref, k_ref, v_ref, pk_ref, pv_ref, stat_ref, start_ref,
    dq_ref, keep_ref, dk_ref, dv_ref,
):
    rows, width = q_ref.shape
    heads = width // HEAD_WIDTH
    start = start_ref[...]
    for i in reversed(range(rows // BLOCK)):
        at = slice(i * BLOCK, (i + 1) * BLOCK)
        query_rows, prev, own = block_scores(i, rows, heads, q_ref, k_ref, pk_ref, start)
        grad_rows = heads_stacked(g_ref, at, heads)
        top, inverse, delta = (stat_ref[i, n : n + 1, :] for n in range(3))
        prev = jnp.exp2((prev - top) * (SCALE * LOG2E)) * inverse
        own = jnp.exp2((own - top) * (SCALE * LOG2E)) * inverse
        dprev = dot(pv_ref[i * BLOCK :, :], grad_rows, NT)
        down = dot(v_ref[: (i + 1) * BLOCK, :], grad_rows, NT)
        dprev = (prev * (dprev - delta)).astype(jnp.bfloat16)
        down = (own * (down - delta)).astype(jnp.bfloat16)
        dv = dot(own.astype(jnp.bfloat16), grad_rows, NN)
        dk = dot(down, query_rows, NN)
        if i == rows // BLOCK - 1:
            dv_ref[...] = dv
            dk_ref[...] = dk
        else:
            dv_ref[: (i + 1) * BLOCK, :] += dv
            dk_ref[: (i + 1) * BLOCK, :] += dk
        dq = dot(pk_ref[i * BLOCK :, :], dprev, TN) + dot(k_ref[: (i + 1) * BLOCK, :], down, TN)
        for h in range(heads):
            dq_ref[at, h * HEAD_WIDTH : (h + 1) * HEAD_WIDTH] = (
                jnp.transpose(dq[:, h * BLOCK : (h + 1) * BLOCK]) * SCALE
            ).astype(jnp.bfloat16)
    keep_ref[:, :HEAD_WIDTH] = dk_ref[...] * SCALE
    keep_ref[:, HEAD_WIDTH:] = dv_ref[...]


def sum_kernel(kv_heads, *refs):
    keep, back = refs[:kv_heads], refs[kv_heads : 2 * kv_heads]
    dk_ref, dv_ref = refs[2 * kv_heads :]
    for h in range(kv_heads):
        at = slice(h * HEAD_WIDTH, (h + 1) * HEAD_WIDTH)
        total = keep[h][...] + back[h][...].astype(jnp.float32)
        dk_ref[:, at] = total[:, :HEAD_WIDTH].astype(jnp.bfloat16)
        dv_ref[:, at] = total[:, HEAD_WIDTH:].astype(jnp.bfloat16)


def column(shape, g):
    return pl.BlockSpec(shape, lambda n: (0, g))


def whole(shape):
    return pl.BlockSpec(shape, lambda n: (0,) * len(shape))


def body(queries, keys, values, output_gradient, doc_lengths):
    rows = queries.shape[0]
    kv_heads = keys.shape[1] // HEAD_WIDTH
    heads = queries.shape[1] // keys.shape[1]
    width = heads * HEAD_WIDTH
    blocks = rows // BLOCK
    prev_keys = shifted(keys, "seq", 1)
    prev_values = shifted(values, "seq", 1)
    lengths = gathered_lengths(doc_lengths)
    first = (lax.axis_index("seq") * rows).astype(jnp.int32).reshape(1)
    params = pltpu.CompilerParams(vmem_limit_bytes=48 * 1024 * 1024)
    pair = (rows, 2 * HEAD_WIDTH)
    stat = (blocks, 8, heads * BLOCK)
    operands = (queries, output_gradient, keys, values, prev_keys, prev_values)
    scratch = [pltpu.VMEM((rows, HEAD_WIDTH), jnp.float32)] * 2

    def columns(g):
        return [column((rows, width), g)] * 2 + [column((rows, HEAD_WIDTH), g)] * 4

    sends, stats = [], []
    for g in range(kv_heads):
        send, *stat_g = pl.pallas_call(
            prev_kernel,
            grid=(1,),
            out_shape=(
                jax.ShapeDtypeStruct(pair, jnp.bfloat16),
                jax.ShapeDtypeStruct(stat, jnp.float32),
                jax.ShapeDtypeStruct((1, rows), jnp.int32),
            ),
            in_specs=[pl.BlockSpec(memory_space=pltpu.SMEM), whole(lengths.shape)] + columns(g),
            out_specs=(whole(pair), whole(stat), whole((1, rows))),
            scratch_shapes=scratch,
            compiler_params=params,
            name="prev_grads",
        )(first, lengths, *operands)
        sends.append(send)
        stats.append(stat_g)
    backs = [shifted(send, "seq", -1) for send in sends]
    grads, keeps = [], []
    for g in range(kv_heads):
        aliases = {} if g == 0 else {8: 0}

        def own_call(*refs, g=g):
            return own_kernel(*(refs if g == 0 else refs[:8] + refs[9:]))

        dq, keep = pl.pallas_call(
            own_call,
            grid=(1,),
            out_shape=(
                jax.ShapeDtypeStruct(queries.shape, jnp.bfloat16),
                jax.ShapeDtypeStruct(pair, jnp.float32),
            ),
            in_specs=columns(g)
            + [whole(stat), whole((1, rows))]
            + ([] if g == 0 else [pl.BlockSpec(memory_space=pl.ANY)]),
            out_specs=(column((rows, width), g), whole(pair)),
            scratch_shapes=scratch,
            input_output_aliases=aliases,
            compiler_params=params,
            name="own_grads",
        )(*operands, *stats[g], *([] if g == 0 else [grads[-1]]))
        grads.append(dq)
        keeps.append(keep)
    key_gradient, value_gradient = pl.pallas_call(
        functools.partial(sum_kernel, kv_heads),
        out_shape=(
            jax.ShapeDtypeStruct(keys.shape, jnp.bfloat16),
            jax.ShapeDtypeStruct(values.shape, jnp.bfloat16),
        ),
        compiler_params=params,
        name="sums",
    )(*keeps, *backs)
    return (grads[-1], key_gradient, value_gradient)


def solution(mesh):
    in_specs = (
        P("seq", "head"),
        P("seq", "head"),
        P("seq", "head"),
        P("seq", "head"),
        P(("seq", "head")),
    )
    out_specs = (P("seq", "head"), P("seq", "head"), P("seq", "head"))
    return jax.shard_map(body, mesh=mesh, in_specs=in_specs, out_specs=out_specs, check_vma=False)
```

time: 114 us -> 53 us (0.46)
  the two profiles are of different devices: /device:TPU:0 before, /device:TPU:26 now
where the time goes in v1:
time: 53 us; the launch traced here: 52.6 us
  starting transfers between devices  18.6 us (35%)
  Pallas kernels  16.2 us (31%)
  waiting for transfers between devices  10.6 us (20%)
  local copies, waits for them, and re-layouts  5.24 us (10%)
  between operations  1.43 us (3%)
  other arithmetic  0.6 us (1%)
    ppermute x5, waiting for transfers between devices, summed_everywhere(): lax.ppermute(value, axis, [(s, s ^ step) for s in range(count)])  10.6 us
    ppermute x4, starting transfers between devices, shifted(): lax.ppermute(value, axis, [(source, source + steps) for source in range(f...  10.1 us
    ppermute x5, starting transfers between devices, summed_everywhere(): lax.ppermute(value, axis, [(s, s ^ step) for s in range(count)])  8.54 us
    pallas_call x2, Pallas kernels, body(): pl.pallas_call(own_call, grid=(1,), out_shape=(jax.ShapeDtypeStruct(queri...  7.66 us
    pallas_call x2, Pallas kernels, body(): pl.pallas_call(prev_kernel, grid=(1,), out_shape=(jax.ShapeDtypeStruct(pa...  7.61 us
    unnamed x16, local copies, waits for them, and re-layouts  4.37 us
  transfers between devices with their start and end apart: 9, of which 5 were waited for; matrix products, arithmetic and copies ran while one was open for 3% of the time, Pallas kernels for 22%

profile of v1, /device:TPU:26, one launch (start us, length us, event | category | flops | bytes accessed | tf_op | source)
XLA Modules:
  0.0 52.6 jit_solution(7105287574663247211)
XLA Ops:
  0.6 1.3 %collective-permute-start = (bf16[512,256]{1,0:T(8,128)(2,1)}, bf16[512,256]{1,0:T(8,128)(2,1)S(1)}, u32[]{:S(2)}, u32[]{:S(2)}) collective-permute-start(bf16[512,256]{1,0:T(8,128)(2,1)} %refs_2_.3), channel_id=1, source_target_pairs={{0,4},{4,8},{8,12},{12,16},{16,20},{20,24},{24,28},{1,5},{5,9},{9,... | collective-permute-start | bytes 786440 | tf_op jit(solution)/shard_map/ppermute | solution.py:26
  1.9 1.3 %collective-permute-start.1 = (bf16[512,256]{1,0:T(8,128)(2,1)}, bf16[512,256]{1,0:T(8,128)(2,1)S(1)}, u32[]{:S(2)}, u32[]{:S(2)}) collective-permute-start(bf16[512,256]{1,0:T(8,128)(2,1)} %refs_3_.3), channel_id=1, source_target_pairs={{0,4},{4,8},{8,12},{12,16},{16,20},{20,24},{24,28},{1,5},{5,9},{9,... | collective-permute-start | bytes 786440 | tf_op jit(solution)/shard_map/ppermute | solution.py:26
  4.1 1.1 %collective-permute-done.2 = s32[1,32]{1,0:T(1,128)S(1)} collective-permute-done((s32[1,32]{1,0:T(1,128)S(1)}, s32[1,32]{1,0:T(1,128)S(1)}, u32[]{:S(2)}, u32[]{:S(2)}) %collective-permute-start.2) | collective-permute-done | bytes 160 | tf_op jit(solution)/shard_map/ppermute | solution.py:37
  5.2 0.6 %fusion = s32[1,1]{1,0:T(1,128)} fusion(s32[1,1]{1,0:T(1,128)} %bitcast.3, s32[1,32]{1,0:T(1,128)S(1)} %collective-permute-done.2, s32[]{:T(128)S(6)} %select_n.3), kind=kLoop, calls=%fused_computation.1 | loop fusion | flops 1 | bytes 16 | tf_op jit(solution)/shard_map/dynamic_update_slice | solution.py:47
  5.8 0.8 %add.24 = s32[1,32]{1,0:T(1,128)S(1)} dynamic-update-slice(s32[1,32]{1,0:T(1,128)S(1)} %collective-permute-done.2, s32[1,1]{1,0:T(1,128)} %fusion, s32[]{:T(128)} %constant.5.clone.1, s32[]{:T(128)S(6)} %select_n.3) | dynamic-update-slice | bytes 12 | tf_op jit(solution)/shard_map/add | solution.py:37
  6.5 1.6 %collective-permute-start.3 = (s32[1,32]{1,0:T(1,128)S(1)}, s32[1,32]{1,0:T(1,128)S(1)}, u32[]{:S(2)}, u32[]{:S(2)}) collective-permute-start(s32[1,32]{1,0:T(1,128)S(1)} %add.24), channel_id=1, source_target_pairs={{0,2},{1,3},{2,0},{3,1},{4,6},{5,7},{6,4},{7,5},{8,10},{9,11},{10,... | collective-permute-start | bytes 392 | tf_op jit(solution)/shard_map/ppermute | solution.py:37
  8.1 2.0 %collective-permute-done.3 = s32[1,32]{1,0:T(1,128)S(1)} collective-permute-done((s32[1,32]{1,0:T(1,128)S(1)}, s32[1,32]{1,0:T(1,128)S(1)}, u32[]{:S(2)}, u32[]{:S(2)}) %collective-permute-start.3) | collective-permute-done | bytes 160 | tf_op jit(solution)/shard_map/ppermute | solution.py:37
  10.1 3.3 %collective-permute-start.4 = (s32[1,32]{1,0:T(1,128)S(1)}, s32[1,32]{1,0:T(1,128)S(1)}, u32[]{:S(2)}, u32[]{:S(2)}) collective-permute-start(s32[1,32]{1,0:T(1,128)S(1)} %add.25), channel_id=1, source_target_pairs={{0,4},{4,0},{8,12},{12,8},{16,20},{20,16},{24,28},{28,24},{1,5},{5... | collective-permute-start | bytes 392 | tf_op jit(solution)/shard_map/ppermute | solution.py:37
  13.4 3.1 %collective-permute-done.4 = s32[1,32]{1,0:T(1,128)S(1)} collective-permute-done((s32[1,32]{1,0:T(1,128)S(1)}, s32[1,32]{1,0:T(1,128)S(1)}, u32[]{:S(2)}, u32[]{:S(2)}) %collective-permute-start.4) | collective-permute-done | bytes 160 | tf_op jit(solution)/shard_map/ppermute | solution.py:37
  16.5 1.9 %collective-permute-start.5 = (s32[1,32]{1,0:T(1,128)S(1)}, s32[1,32]{1,0:T(1,128)S(1)}, u32[]{:S(2)}, u32[]{:S(2)}) collective-permute-start(s32[1,32]{1,0:T(1,128)S(1)} %add.26), channel_id=1, source_target_pairs={{0,8},{4,12},{8,0},{12,4},{16,24},{20,28},{24,16},{28,20},{1,9},{5... | collective-permute-start | bytes 392 | tf_op jit(solution)/shard_map/ppermute | solution.py:37
  18.4 1.7 %collective-permute-done.5 = s32[1,32]{1,0:T(1,128)S(1)} collective-permute-done((s32[1,32]{1,0:T(1,128)S(1)}, s32[1,32]{1,0:T(1,128)S(1)}, u32[]{:S(2)}, u32[]{:S(2)}) %collective-permute-start.5) | collective-permute-done | bytes 160 | tf_op jit(solution)/shard_map/ppermute | solution.py:37
  20.0 1.8 %collective-permute-start.6 = (s32[1,32]{1,0:T(1,128)S(1)}, s32[1,32]{1,0:T(1,128)S(1)}, u32[]{:S(2)}, u32[]{:S(2)}) collective-permute-start(s32[1,32]{1,0:T(1,128)S(1)} %add.27), channel_id=1, source_target_pairs={{0,16},{4,20},{8,24},{12,28},{16,0},{20,4},{24,8},{28,12},{1,17},{... | collective-permute-start | bytes 392 | tf_op jit(solution)/shard_map/ppermute | solution.py:37
  21.8 2.7 %collective-permute-done.6 = s32[1,32]{1,0:T(1,128)S(1)} collective-permute-done((s32[1,32]{1,0:T(1,128)S(1)}, s32[1,32]{1,0:T(1,128)S(1)}, u32[]{:S(2)}, u32[]{:S(2)}) %collective-permute-start.6) | collective-permute-done | bytes 160 | tf_op jit(solution)/shard_map/ppermute | solution.py:37
  24.5 1.2 %copy-done = bf16[512,1024]{1,0:T(8,128)(2,1)S(1)} copy-done((bf16[512,1024]{1,0:T(8,128)(2,1)S(1)}, bf16[512,1024]{1,0:T(8,128)(2,1)}, u32[]{:S(2)}) %copy-start) | copy-done | bytes 1048600
  25.7 1.2 %copy-done.2 = bf16[512,1024]{1,0:T(8,128)(2,1)S(1)} copy-done((bf16[512,1024]{1,0:T(8,128)(2,1)S(1)}, bf16[512,1024]{1,0:T(8,128)(2,1)}, u32[]{:S(2)}) %copy-start.2) | copy-done | bytes 1048600
  26.9 0.9 %copy-done.4 = bf16[512,256]{1,0:T(8,128)(2,1)S(1)} copy-done((bf16[512,256]{1,0:T(8,128)(2,1)S(1)}, bf16[512,256]{1,0:T(8,128)(2,1)}, u32[]{:S(2)}) %copy-start.4) | copy-done | bytes 262168
  27.9 0.9 %copy-done.6 = bf16[512,256]{1,0:T(8,128)(2,1)S(1)} copy-done((bf16[512,256]{1,0:T(8,128)(2,1)S(1)}, bf16[512,256]{1,0:T(8,128)(2,1)}, u32[]{:S(2)}) %copy-start.6) | copy-done | bytes 262168
  28.8 3.8 %prev_grads.3 = (bf16[512,256]{1,0:T(8,128)(2,1)S(1)}, f32[4,8,512]{2,1,0:T(8,128)S(1)}, s32[1,512]{1,0:T(1,128)S(1)}) custom-call(s32[1]{0:T(128)} %bitcast.first_ref, s32[1,32]{1,0:T(1,128)S(1)} %add.28.len_ref, bf16[512,1024]{1,0:T(8,128)(2,1)S(1)} %copy-done, bf16[512,1024]{1,0:T(8,128)(2,1)S(1)} %copy-done.2, bf16[512,256]{1,0:T(8,128)(2,1)S(1)} %copy-done.4, ...), custom_call_target="tpu_custom_call" | custom-call | tf_op jit(solution)/shard_map/prev_grads/pallas_call | solution.py:211
  32.7 2.5 %collective-permute-start.7 = (bf16[512,256]{1,0:T(8,128)(2,1)S(1)}, bf16[512,256]{1,0:T(8,128)(2,1)S(1)}, u32[]{:S(2)}, u32[]{:S(2)}) collective-permute-start(bf16[512,256]{1,0:T(8,128)(2,1)S(1)} %get-tuple-element.23), channel_id=1, source_target_pairs={{4,0},{8,4},{12,8},{16,12},{20,16},{24,20},{28,24},{5,1},{9,5},{13... | collective-permute-start | bytes 786440 | tf_op jit(solution)/shard_map/ppermute | solution.py:26
  35.2 3.8 %prev_grads.2 = (bf16[512,256]{1,0:T(8,128)(2,1)S(1)}, f32[4,8,512]{2,1,0:T(8,128)S(1)}, s32[1,512]{1,0:T(1,128)S(1)}) custom-call(s32[1]{0:T(128)} %bitcast.first_ref, s32[1,32]{1,0:T(1,128)S(1)} %add.28.len_ref, bf16[512,1024]{1,0:T(8,128)(2,1)S(1)} %copy-done, bf16[512,1024]{1,0:T(8,128)(2,1)S(1)} %copy-done.2, bf16[512,256]{1,0:T(8,128)(2,1)S(1)} %copy-done.4, ...), custom_call_target="tpu_custom_call" | custom-call | tf_op jit(solution)/shard_map/prev_grads/pallas_call | solution.py:211
  39.0 5.0 %collective-permute-start.8 = (bf16[512,256]{1,0:T(8,128)(2,1)S(1)}, bf16[512,256]{1,0:T(8,128)(2,1)S(1)}, u32[]{:S(2)}, u32[]{:S(2)}) collective-permute-start(bf16[512,256]{1,0:T(8,128)(2,1)S(1)} %get-tuple-element.24), channel_id=1, source_target_pairs={{4,0},{8,4},{12,8},{16,12},{20,16},{24,20},{28,24},{5,1},{9,5},{13... | collective-permute-start | bytes 786440 | tf_op jit(solution)/shard_map/ppermute | solution.py:26
  44.0 3.8 %own_grads.2 = (bf16[512,1024]{1,0:T(8,128)(2,1)}, f32[512,256]{1,0:T(8,128)S(1)}) custom-call(bf16[512,1024]{1,0:T(8,128)(2,1)S(1)} %copy-done.1, bf16[512,1024]{1,0:T(8,128)(2,1)S(1)} %copy-done.3, bf16[512,256]{1,0:T(8,128)(2,1)S(1)} %copy-done.5, bf16[512,256]{1,0:T(8,128)(2,1)S(1)} %copy-done.7, ...), custom_call_target="tpu_custom_call" | custom-call | tf_op jit(solution)/shard_map/own_grads/pallas_call | solution.py:235
  47.9 3.8 %own_grads.3 = (bf16[512,1024]{1,0:T(8,128)(2,1)}, f32[512,256]{1,0:T(8,128)S(1)}) custom-call(bf16[512,1024]{1,0:T(8,128)(2,1)S(1)} %copy-done.1, bf16[512,1024]{1,0:T(8,128)(2,1)S(1)} %copy-done.3, bf16[512,256]{1,0:T(8,128)(2,1)S(1)} %copy-done.5, bf16[512,256]{1,0:T(8,128)(2,1)S(1)} %copy-done.7, ...), custom_call_target="tpu_custom_call", output_to_operand_aliasing={{0}: (8, {})} | custom-call | tf_op jit(solution)/shard_map/own_grads/pallas_call | solution.py:235
  51.7 0.9 %sums.1 = (bf16[512,256]{1,0:T(8,128)(2,1)}, bf16[512,256]{1,0:T(8,128)(2,1)}) custom-call(f32[512,256]{1,0:T(8,128)S(1)} %get-tuple-element.21.refs_0_, f32[512,256]{1,0:T(8,128)S(1)} %get-tuple-element.22.refs_1_, bf16[512,256]{1,0:T(8,128)(2,1)S(1)} %collective-permute-done.7.refs_2_, bf16[512,256]{1,0:T(8,128)(2,1)S(1)} %collective-permute-done.8.refs_3_), custom_call_target="tpu_custom_call" | custom-call | tf_op jit(solution)/shard_map/sums/pallas_call | solution.py:253
  (23 shorter events, 0.2 us)
Async XLA Ops:
  0.6 23.8 %collective-permute-start = (bf16[512,256]{1,0:T(8,128)(2,1)}, bf16[512,256]{1,0:T(8,128)(2,1)S(1)}, u32[]{:S(2)}, u32[]{:S(2)}) collective-permute-start(bf16[512,256]{1,0:T(8,128)(2,1)} %refs_2_.3), channel_id=1, source_target_pairs={{0,4},{4,8},{8,12},{12,16},{16,20},{20,24},{24,28},{1,5},{5,9},{9,... | collective-permute-start | bytes 786440 | tf_op jit(solution)/shard_map/ppermute | solution.py:26
  1.9 22.5 %collective-permute-start.1 = (bf16[512,256]{1,0:T(8,128)(2,1)}, bf16[512,256]{1,0:T(8,128)(2,1)S(1)}, u32[]{:S(2)}, u32[]{:S(2)}) collective-permute-start(bf16[512,256]{1,0:T(8,128)(2,1)} %refs_3_.3), channel_id=1, source_target_pairs={{0,4},{4,8},{8,12},{12,16},{16,20},{20,24},{24,28},{1,5},{5,9},{9,... | collective-permute-start | bytes 786440 | tf_op jit(solution)/shard_map/ppermute | solution.py:26
  4.0 1.2 %collective-permute-start.2 = (s32[1,32]{1,0:T(1,128)S(1)}, s32[1,32]{1,0:T(1,128)S(1)}, u32[]{:S(2)}, u32[]{:S(2)}) collective-permute-start(s32[1,32]{1,0:T(1,128)S(1)} %dynamic_update_slice.5), channel_id=1, source_target_pairs={{0,1},{1,0},{2,3},{3,2},{4,5},{5,4},{6,7},{7,6},{8,9},{9,8},{10,11... | collective-permute-start | bytes 392 | tf_op jit(solution)/shard_map/ppermute | solution.py:37
  6.5 3.6 %collective-permute-start.3 = (s32[1,32]{1,0:T(1,128)S(1)}, s32[1,32]{1,0:T(1,128)S(1)}, u32[]{:S(2)}, u32[]{:S(2)}) collective-permute-start(s32[1,32]{1,0:T(1,128)S(1)} %add.24), channel_id=1, source_target_pairs={{0,2},{1,3},{2,0},{3,1},{4,6},{5,7},{6,4},{7,5},{8,10},{9,11},{10,... | collective-permute-start | bytes 392 | tf_op jit(solution)/shard_map/ppermute | solution.py:37
  10.1 6.4 %collective-permute-start.4 = (s32[1,32]{1,0:T(1,128)S(1)}, s32[1,32]{1,0:T(1,128)S(1)}, u32[]{:S(2)}, u32[]{:S(2)}) collective-permute-start(s32[1,32]{1,0:T(1,128)S(1)} %add.25), channel_id=1, source_target_pairs={{0,4},{4,0},{8,12},{12,8},{16,20},{20,16},{24,28},{28,24},{1,5},{5... | collective-permute-start | bytes 392 | tf_op jit(solution)/shard_map/ppermute | solution.py:37
  16.5 3.5 %collective-permute-start.5 = (s32[1,32]{1,0:T(1,128)S(1)}, s32[1,32]{1,0:T(1,128)S(1)}, u32[]{:S(2)}, u32[]{:S(2)}) collective-permute-start(s32[1,32]{1,0:T(1,128)S(1)} %add.26), channel_id=1, source_target_pairs={{0,8},{4,12},{8,0},{12,4},{16,24},{20,28},{24,16},{28,20},{1,9},{5... | collective-permute-start | bytes 392 | tf_op jit(solution)/shard_map/ppermute | solution.py:37
  20.0 4.4 %collective-permute-start.6 = (s32[1,32]{1,0:T(1,128)S(1)}, s32[1,32]{1,0:T(1,128)S(1)}, u32[]{:S(2)}, u32[]{:S(2)}) collective-permute-start(s32[1,32]{1,0:T(1,128)S(1)} %add.27), channel_id=1, source_target_pairs={{0,16},{4,20},{8,24},{12,28},{16,0},{20,4},{24,8},{28,12},{1,17},{... | collective-permute-start | bytes 392 | tf_op jit(solution)/shard_map/ppermute | solution.py:37
  24.5 1.2 %copy-start = (bf16[512,1024]{1,0:T(8,128)(2,1)S(1)}, bf16[512,1024]{1,0:T(8,128)(2,1)}, u32[]{:S(2)}) copy-start(bf16[512,1024]{1,0:T(8,128)(2,1)} %refs_0_.3) | copy-start | bytes 3145732
  25.7 1.2 %copy-start.2 = (bf16[512,1024]{1,0:T(8,128)(2,1)S(1)}, bf16[512,1024]{1,0:T(8,128)(2,1)}, u32[]{:S(2)}) copy-start(bf16[512,1024]{1,0:T(8,128)(2,1)} %refs_1_.3) | copy-start | bytes 3145732
  26.9 0.9 %copy-start.4 = (bf16[512,256]{1,0:T(8,128)(2,1)S(1)}, bf16[512,256]{1,0:T(8,128)(2,1)}, u32[]{:S(2)}) copy-start(bf16[512,256]{1,0:T(8,128)(2,1)} %refs_2_.3) | copy-start | bytes 786436
  27.9 0.9 %copy-start.6 = (bf16[512,256]{1,0:T(8,128)(2,1)S(1)}, bf16[512,256]{1,0:T(8,128)(2,1)}, u32[]{:S(2)}) copy-start(bf16[512,256]{1,0:T(8,128)(2,1)} %refs_3_.3) | copy-start | bytes 786436
  32.6 11.4 %copy-start.1 = (bf16[512,1024]{1,0:T(8,128)(2,1)S(1)}, bf16[512,1024]{1,0:T(8,128)(2,1)}, u32[]{:S(2)}) copy-start(bf16[512,1024]{1,0:T(8,128)(2,1)} %refs_0_.3) | copy-start | bytes 3145732
  32.6 11.4 %copy-start.3 = (bf16[512,1024]{1,0:T(8,128)(2,1)S(1)}, bf16[512,1024]{1,0:T(8,128)(2,1)}, u32[]{:S(2)}) copy-start(bf16[512,1024]{1,0:T(8,128)(2,1)} %refs_1_.3) | copy-start | bytes 3145732
  32.7 11.4 %copy-start.5 = (bf16[512,256]{1,0:T(8,128)(2,1)S(1)}, bf16[512,256]{1,0:T(8,128)(2,1)}, u32[]{:S(2)}) copy-start(bf16[512,256]{1,0:T(8,128)(2,1)} %refs_2_.3) | copy-start | bytes 786436
  32.7 11.4 %copy-start.7 = (bf16[512,256]{1,0:T(8,128)(2,1)S(1)}, bf16[512,256]{1,0:T(8,128)(2,1)}, u32[]{:S(2)}) copy-start(bf16[512,256]{1,0:T(8,128)(2,1)} %refs_3_.3) | copy-start | bytes 786436
  32.7 19.0 %collective-permute-start.7 = (bf16[512,256]{1,0:T(8,128)(2,1)S(1)}, bf16[512,256]{1,0:T(8,128)(2,1)S(1)}, u32[]{:S(2)}, u32[]{:S(2)}) collective-permute-start(bf16[512,256]{1,0:T(8,128)(2,1)S(1)} %get-tuple-element.23), channel_id=1, source_target_pairs={{4,0},{8,4},{12,8},{16,12},{20,16},{24,20},{28,24},{5,1},{9,5},{13... | collective-permute-start | bytes 786440 | tf_op jit(solution)/shard_map/ppermute | solution.py:26
  39.0 12.7 %collective-permute-start.8 = (bf16[512,256]{1,0:T(8,128)(2,1)S(1)}, bf16[512,256]{1,0:T(8,128)(2,1)S(1)}, u32[]{:S(2)}, u32[]{:S(2)}) collective-permute-start(bf16[512,256]{1,0:T(8,128)(2,1)S(1)} %get-tuple-element.24), channel_id=1, source_target_pairs={{4,0},{8,4},{12,8},{16,12},{20,16},{24,20},{28,24},{5,1},{9,5},{13... | collective-permute-start | bytes 786440 | tf_op jit(solution)/shard_map/ppermute | solution.py:26

commit v2 on v1

v2 whole, which is shorter than its diff:
```python
import functools

import jax
import jax.numpy as jnp
from jax import lax
from jax.experimental import pallas as pl
from jax.experimental.pallas import tpu as pltpu
from jax.sharding import PartitionSpec as P

HEAD_WIDTH = 128
BLOCK = 128
SCALE = HEAD_WIDTH ** (-0.5)
LOG2E = 1.4426950408889634
NT = (((1,), (1,)), ((), ()))
NN = (((1,), (0,)), ((), ()))
TN = (((0,), (0,)), ((), ()))


def dot(a, b, dims):
    return lax.dot_general(a, b, dims, preferred_element_type=jnp.float32)


def rotated(value, axis, steps):
    count = lax.axis_size(axis)
    return lax.ppermute(value, axis, [(s, (s + steps) % count) for s in range(count)])


def summed_everywhere(value, axis, lone):
    count = lax.axis_size(axis)
    if count & (count - 1):
        return lax.psum(value, axis)
    step = 1
    while step < count:
        bits = 1 if lone or 2 * step == count else 2
        lone = False
        masks = [m * step for m in range(1, 1 << bits)]
        others = [lax.ppermute(value, axis, [(s, s ^ m) for s in range(count)]) for m in masks]
        value = functools.reduce(jnp.add, others, value)
        step <<= bits
    return value


def gathered_lengths(doc_lengths):
    own = doc_lengths.shape[0]
    shards = lax.axis_size("seq") * lax.axis_size("head")
    place = lax.axis_index("seq") * lax.axis_size("head") + lax.axis_index("head")
    spot = lax.broadcasted_iota(jnp.int32, (1, shards, own), 1) == place
    row = jnp.where(spot, doc_lengths[None, None, :], 0).reshape(1, shards * own)
    return summed_everywhere(summed_everywhere(row, "seq", True), "head", False)


def start_row(lengths, first, rows):
    docs = lengths.shape[1]
    before = lax.broadcasted_iota(jnp.int32, (docs, docs), 1) < lax.broadcasted_iota(
        jnp.int32, (docs, docs), 0
    )
    starts = jnp.sum(
        jnp.where(before, jnp.broadcast_to(lengths, (docs, docs)), 0), axis=1, keepdims=True
    )
    starts = jnp.broadcast_to(starts - first, (docs, rows))
    own = lax.broadcasted_iota(jnp.int32, (docs, rows), 1)
    return jnp.max(jnp.where(starts <= own, starts, -first), axis=0, keepdims=True)


def stacked(ref, i, g, heads):
    return jnp.concatenate(
        [
            ref[pl.ds(i * BLOCK, BLOCK), pl.ds((g * heads + h) * HEAD_WIDTH, HEAD_WIDTH)]
            for h in range(heads)
        ],
        axis=0,
    )


def masked(scores, start, query, first_key, diagonal):
    key = first_key + lax.broadcasted_iota(jnp.int32, (scores.shape[0], BLOCK), 0)
    allowed = key >= start
    if diagonal:
        allowed = allowed & (key <= query)
    return jnp.concatenate(
        [
            jnp.where(allowed, scores[:, c : c + BLOCK], -jnp.inf)
            for c in range(0, scores.shape[1], BLOCK)
        ],
        axis=1,
    )


def own_span(i):
    return slice(i * (i + 1) // 2 * BLOCK, (i + 1) * (i + 2) // 2 * BLOCK)


def prev_span(i, blocks):
    first = i * blocks - i * (i - 1) // 2
    return slice(first * BLOCK, (first + blocks - i) * BLOCK)


def query_row(i):
    return i * BLOCK + lax.broadcasted_iota(jnp.int32, (1, BLOCK), 1)


def column(g):
    return slice(g * HEAD_WIDTH, (g + 1) * HEAD_WIDTH)


def raw_kernel(q_ref, g_ref, k_ref, v_ref, *outs):
    rows, width = q_ref.shape
    kv_heads = k_ref.shape[1] // HEAD_WIDTH
    heads = width // k_ref.shape[1]
    for g in range(kv_heads):
        s_ref, d_ref = outs[2 * g : 2 * g + 2]
        for i in range(rows // BLOCK):
            seen = slice(0, (i + 1) * BLOCK)
            s_ref[own_span(i), :] = dot(k_ref[seen, column(g)], stacked(q_ref, i, g, heads), NT)
            d_ref[own_span(i), :] = dot(v_ref[seen, column(g)], stacked(g_ref, i, g, heads), NT)


def prev_kernel(
    g, first_ref, len_ref, q_ref, g_ref, pk_ref, pv_ref, s_ref, d_ref,
    send_ref, stat_ref, start_ref, ds_ref, dk_ref, dv_ref,
):
    rows, width = q_ref.shape
    heads = width // pk_ref.shape[1]
    blocks = rows // BLOCK
    start_ref[...] = start_row(len_ref[...], first_ref[0], rows)
    for i in range(blocks):
        start = start_ref[:, i * BLOCK : (i + 1) * BLOCK]
        query_rows = stacked(q_ref, i, g, heads)
        grad_rows = stacked(g_ref, i, g, heads)
        seen = slice(i * BLOCK, rows)
        prev = dot(pk_ref[seen, column(g)], query_rows, NT)
        prev = masked(prev, start, query_row(i), i * BLOCK - rows, False)
        own = masked(s_ref[own_span(i), :], start, query_row(i), 0, True)
        top = jnp.maximum(
            jnp.max(prev, axis=0, keepdims=True), jnp.max(own, axis=0, keepdims=True)
        )
        prev = jnp.exp2((prev - top) * (SCALE * LOG2E))
        own = jnp.exp2((own - top) * (SCALE * LOG2E))
        total = jnp.sum(prev, axis=0, keepdims=True) + jnp.sum(own, axis=0, keepdims=True)
        inverse = 1.0 / total
        dprev = dot(pv_ref[seen, column(g)], grad_rows, NT)
        delta = inverse * (
            jnp.sum(prev * dprev, axis=0, keepdims=True)
            + jnp.sum(own * d_ref[own_span(i), :], axis=0, keepdims=True)
        )
        prob = prev * inverse
        dscore = (prob * (dprev - delta)).astype(jnp.bfloat16)
        ds_ref[prev_span(i, blocks), :] = dscore
        dv = dot(prob.astype(jnp.bfloat16), grad_rows, NN)
        dk = dot(dscore, query_rows, NN)
        if i == 0:
            dv_ref[...] = dv
            dk_ref[...] = dk
        else:
            dv_ref[seen, :] += dv
            dk_ref[seen, :] += dk
        stat_ref[i, 0:1, :] = top
        stat_ref[i, 1:2, :] = inverse
        stat_ref[i, 2:3, :] = delta
    send_ref[:, :HEAD_WIDTH] = (dk_ref[...] * SCALE).astype(jnp.bfloat16)
    send_ref[:, HEAD_WIDTH:] = dv_ref[...].astype(jnp.bfloat16)


def own_kernel(kv_heads, *refs):
    q_ref, g_ref, k_ref, pk_ref, start_ref = refs[:5]
    per_head = [refs[5 + 4 * g : 9 + 4 * g] for g in range(kv_heads)]
    refs = refs[5 + 4 * kv_heads :]
    dq_hbm, keeps, (dq_ref, dk_ref, dv_ref, sems) = refs[0], refs[1 : 1 + kv_heads], refs[1 + kv_heads :]
    rows, width = q_ref.shape
    heads = width // k_ref.shape[1]
    blocks = rows // BLOCK
    copies = []
    for g in range(kv_heads):
        s_ref, d_ref, stat_ref, ds_ref = per_head[g]
        for i in reversed(range(blocks)):
            start = start_ref[:, i * BLOCK : (i + 1) * BLOCK]
            query_rows = stacked(q_ref, i, g, heads)
            grad_rows = stacked(g_ref, i, g, heads)
            seen = slice(0, (i + 1) * BLOCK)
            top, inverse, delta = (stat_ref[i, n : n + 1, :] for n in range(3))
            own = masked(s_ref[own_span(i), :], start, query_row(i), 0, True)
            own = jnp.exp2((own - top) * (SCALE * LOG2E)) * inverse
            down = (own * (d_ref[own_span(i), :] - delta)).astype(jnp.bfloat16)
            dv = dot(own.astype(jnp.bfloat16), grad_rows, NN)
            dk = dot(down, query_rows, NN)
            if i == blocks - 1:
                dv_ref[...] = dv
                dk_ref[...] = dk
            else:
                dv_ref[seen, :] += dv
                dk_ref[seen, :] += dk
            dq = dot(pk_ref[i * BLOCK : rows, column(g)], ds_ref[prev_span(i, blocks), :], TN)
            dq = (dq + dot(k_ref[seen, column(g)], down, TN)) * SCALE
            place = (
                pl.ds(i * BLOCK, BLOCK),
                pl.ds(g * heads * HEAD_WIDTH, heads * HEAD_WIDTH),
            )
            for h in range(heads):
                dq_ref[place[0], pl.ds((g * heads + h) * HEAD_WIDTH, HEAD_WIDTH)] = jnp.transpose(
                    dq[:, h * BLOCK : (h + 1) * BLOCK]
                ).astype(jnp.bfloat16)
            copy = pltpu.make_async_copy(
                dq_ref.at[place], dq_hbm.at[place], sems.at[g * blocks + i]
            )
            copy.start()
            copies.append(copy)
        keeps[g][:, :HEAD_WIDTH] = dk_ref[...] * SCALE
        keeps[g][:, HEAD_WIDTH:] = dv_ref[...]
    for copy in copies:
        copy.wait()


def sum_kernel(kv_heads, *refs):
    keep, back = refs[:kv_heads], refs[kv_heads : 2 * kv_heads]
    dk_ref, dv_ref = refs[2 * kv_heads :]
    for g in range(kv_heads):
        total = keep[g][...] + back[g][...].astype(jnp.float32)
        dk_ref[:, column(g)] = total[:, :HEAD_WIDTH].astype(jnp.bfloat16)
        dv_ref[:, column(g)] = total[:, HEAD_WIDTH:].astype(jnp.bfloat16)


def body(queries, keys, values, output_gradient, doc_lengths):
    rows = queries.shape[0]
    kv_heads = keys.shape[1] // HEAD_WIDTH
    heads = queries.shape[1] // keys.shape[1]
    blocks = rows // BLOCK
    pairs = blocks * (blocks + 1) // 2 * BLOCK
    lanes = heads * BLOCK
    prev_keys = rotated(keys, "seq", 1)
    prev_values = rotated(values, "seq", 1)
    lengths = gathered_lengths(doc_lengths)
    first = (lax.axis_index("seq") * rows).astype(jnp.int32).reshape(1)
    params = pltpu.CompilerParams(vmem_limit_bytes=24 * 1024 * 1024)
    shape = jax.ShapeDtypeStruct
    vmem = pl.BlockSpec(memory_space=pltpu.VMEM)
    pair = shape((rows, 2 * HEAD_WIDTH), jnp.bfloat16)
    scratch = [pltpu.VMEM((rows, HEAD_WIDTH), jnp.float32)] * 2

    raw = pl.pallas_call(
        raw_kernel,
        out_shape=[shape((pairs, lanes), jnp.float32)] * (2 * kv_heads),
        compiler_params=params,
        name="own_products",
    )(queries, output_gradient, keys, values)
    sends, per_head = [], []
    for g in range(kv_heads):
        send, stat, start, ds = pl.pallas_call(
            functools.partial(prev_kernel, g),
            out_shape=(
                pair,
                shape((blocks, 8, lanes), jnp.float32),
                shape((1, rows), jnp.int32),
                shape((pairs, lanes), jnp.bfloat16),
            ),
            in_specs=[pl.BlockSpec(memory_space=pltpu.SMEM)] + [vmem] * 7,
            scratch_shapes=scratch,
            compiler_params=params,
            name="prev_grads",
        )(
            first, lengths, queries, output_gradient, prev_keys, prev_values,
            raw[2 * g], raw[2 * g + 1],
        )
        sends.append(send)
        per_head += [raw[2 * g], raw[2 * g + 1], stat, ds]
    backs = [rotated(send, "seq", -1) for send in sends]
    grad_queries, *keeps = pl.pallas_call(
        functools.partial(own_kernel, kv_heads),
        out_shape=[shape(queries.shape, jnp.bfloat16)]
        + [shape(pair.shape, jnp.float32)] * kv_heads,
        in_specs=[vmem] * (5 + 4 * kv_heads),
        out_specs=[pl.BlockSpec(memory_space=pl.ANY)] + [vmem] * kv_heads,
        scratch_shapes=[pltpu.VMEM(queries.shape, jnp.bfloat16)]
        + scratch
        + [pltpu.SemaphoreType.DMA((kv_heads * blocks,))],
        compiler_params=params,
        name="own_grads",
    )(queries, output_gradient, keys, prev_keys, start, *per_head)
    key_gradient, value_gradient = pl.pallas_call(
        functools.partial(sum_kernel, kv_heads),
        out_shape=[shape(keys.shape, jnp.bfloat16)] * 2,
        compiler_params=params,
        name="sums",
    )(*keeps, *backs)
    return (grad_queries, key_gradient, value_gradient)


def solution(mesh):
    in_specs = (
        P("seq", "head"),
        P("seq", "head"),
        P("seq", "head"),
        P("seq", "head"),
        P(("seq", "head")),
    )
    out_specs = (P("seq", "head"), P("seq", "head"), P("seq", "head"))
    return jax.shard_map(body, mesh=mesh, in_specs=in_specs, out_specs=out_specs, check_vma=False)
```

time: 53 us -> 43.2 us (0.82)
  the two profiles are of different devices: /device:TPU:26 before, /device:TPU:0 now
where the time goes in v2:
time: 43.2 us; the launch traced here: 42.9 us
  starting transfers between devices  16.2 us (38%)
  Pallas kernels  14 us (32%)
  waiting for transfers between devices  7.04 us (16%)
  local copies, waits for them, and re-layouts  4.35 us (10%)
  between operations  1.37 us (3%)
    ppermute x7, starting transfers between devices, summed_everywhere(): lax.ppermute(value, axis, [(s, s ^ m) for s in range(count)])  9.38 us
    pallas_call x2, Pallas kernels, body(): pl.pallas_call(functools.partial(prev_kernel, g), out_shape=(pair, shape(...  7.58 us
    ppermute x4, starting transfers between devices, rotated(): lax.ppermute(value, axis, [(s, (s + steps) % count) for s in range(count)])  6.84 us
    unnamed x8, local copies, waits for them, and re-layouts  4.35 us
    ppermute x7, waiting for transfers between devices, summed_everywhere(): lax.ppermute(value, axis, [(s, s ^ m) for s in range(count)])  4.07 us
    pallas_call x1, Pallas kernels, body(): pl.pallas_call(functools.partial(own_kernel, kv_heads), out_shape=[shape(...  3.96 us
    ppermute x4, waiting for transfers between devices, rotated(): lax.ppermute(value, axis, [(s, (s + steps) % count) for s in range(count)])  2.97 us
    pallas_call x1, Pallas kernels, body(): pl.pallas_call(raw_kernel, out_shape=[shape((pairs, lanes), jnp.float32)]...  1.52 us
  transfers between devices with their start and end apart: 11, of which 5 were waited for; matrix products, arithmetic and copies ran while one was open for 0% of the time, Pallas kernels for 22%

profile of v2, /device:TPU:0, one launch (start us, length us, event | category | flops | bytes accessed | tf_op | source)
XLA Modules:
  0.0 42.9 jit_solution(17613156678892967107)
XLA Ops:
  1.3 3.0 %collective-permute-start.1 = (s32[1,32]{1,0:T(1,128)S(1)}, s32[1,32]{1,0:T(1,128)S(1)}, u32[]{:S(2)}, u32[]{:S(2)}) collective-permute-start(s32[1,32]{1,0:T(1,128)S(1)} %compare_select_fusion), channel_id=1, source_target_pairs={{0,4},{4,0},{8,12},{12,8},{16,20},{20,16},{24,28},{28,24},{1,5},{5... | collective-permute-start | bytes 392 | tf_op jit(solution)/shard_map/ppermute | solution.py:37
  4.4 3.0 %collective-permute-start = (bf16[512,256]{1,0:T(8,128)(2,1)}, bf16[512,256]{1,0:T(8,128)(2,1)S(1)}, u32[]{:S(2)}, u32[]{:S(2)}) collective-permute-start(bf16[512,256]{1,0:T(8,128)(2,1)} %refs_2_.1), channel_id=1, source_target_pairs={{0,4},{4,8},{8,12},{12,16},{16,20},{20,24},{24,28},{28,0},{1,5},{5... | collective-permute-start | bytes 786440 | tf_op jit(solution)/shard_map/ppermute | solution.py:25
  7.3 1.2 %copy-done = bf16[512,1024]{1,0:T(8,128)(2,1)S(1)} copy-done((bf16[512,1024]{1,0:T(8,128)(2,1)S(1)}, bf16[512,1024]{1,0:T(8,128)(2,1)}, u32[]{:S(2)}) %copy-start) | copy-done | bytes 1048600
  8.6 1.2 %copy-done.1 = bf16[512,1024]{1,0:T(8,128)(2,1)S(1)} copy-done((bf16[512,1024]{1,0:T(8,128)(2,1)S(1)}, bf16[512,1024]{1,0:T(8,128)(2,1)}, u32[]{:S(2)}) %copy-start.1) | copy-done | bytes 1048600
  9.8 0.9 %copy-done.2 = bf16[512,256]{1,0:T(8,128)(2,1)S(1)} copy-done((bf16[512,256]{1,0:T(8,128)(2,1)S(1)}, bf16[512,256]{1,0:T(8,128)(2,1)}, u32[]{:S(2)}) %copy-start.2) | copy-done | bytes 262168
  10.7 0.9 %copy-done.3 = bf16[512,256]{1,0:T(8,128)(2,1)S(1)} copy-done((bf16[512,256]{1,0:T(8,128)(2,1)S(1)}, bf16[512,256]{1,0:T(8,128)(2,1)}, u32[]{:S(2)}) %copy-start.3) | copy-done | bytes 262168
  11.7 1.5 %own_products.1 = (f32[1280,512]{1,0:T(8,128)S(1)}, f32[1280,512]{1,0:T(8,128)S(1)}, f32[1280,512]{1,0:T(8,128)S(1)}, f32[1280,512]{1,0:T(8,128)S(1)}) custom-call(bf16[512,1024]{1,0:T(8,128)(2,1)S(1)} %copy-done, bf16[512,1024]{1,0:T(8,128)(2,1)S(1)} %copy-done.1, bf16[512,256]{1,0:T(8,128)(2,1)S(1)} %copy-done.2, bf16[512,256]{1,0:T(8,128)(2,1)S(1)} %copy-done.3), custom_call_target="tpu_custom_call" | custom-call | tf_op jit(solution)/shard_map/own_products/pallas_call | solution.py:239
  13.2 2.3 %collective-permute-start.4 = (s32[1,32]{1,0:T(1,128)S(1)}, s32[1,32]{1,0:T(1,128)S(1)}, u32[]{:S(2)}, u32[]{:S(2)}) collective-permute-start(s32[1,32]{1,0:T(1,128)S(1)} %fusion), channel_id=1, source_target_pairs={{0,24},{4,28},{8,16},{12,20},{16,8},{20,12},{24,0},{28,4},{1,25},{... | collective-permute-start | bytes 392 | tf_op jit(solution)/shard_map/ppermute | solution.py:37
  15.6 0.8 %collective-permute-start.3 = (s32[1,32]{1,0:T(1,128)S(1)}, s32[1,32]{1,0:T(1,128)S(1)}, u32[]{:S(2)}, u32[]{:S(2)}) collective-permute-start(s32[1,32]{1,0:T(1,128)S(1)} %fusion), channel_id=1, source_target_pairs={{0,16},{4,20},{8,24},{12,28},{16,0},{20,4},{24,8},{28,12},{1,17},{... | collective-permute-start | bytes 392 | tf_op jit(solution)/shard_map/ppermute | solution.py:37
  16.3 1.3 %collective-permute-start.2 = (s32[1,32]{1,0:T(1,128)S(1)}, s32[1,32]{1,0:T(1,128)S(1)}, u32[]{:S(2)}, u32[]{:S(2)}) collective-permute-start(s32[1,32]{1,0:T(1,128)S(1)} %fusion), channel_id=1, source_target_pairs={{0,8},{4,12},{8,0},{12,4},{16,24},{20,28},{24,16},{28,20},{1,9},{5... | collective-permute-start | bytes 392 | tf_op jit(solution)/shard_map/ppermute | solution.py:37
  17.7 0.9 %collective-permute-done.4 = s32[1,32]{1,0:T(1,128)S(1)} collective-permute-done((s32[1,32]{1,0:T(1,128)S(1)}, s32[1,32]{1,0:T(1,128)S(1)}, u32[]{:S(2)}, u32[]{:S(2)}) %collective-permute-start.4) | collective-permute-done | bytes 160 | tf_op jit(solution)/shard_map/ppermute | solution.py:37
  18.6 1.4 %collective-permute-done.3 = s32[1,32]{1,0:T(1,128)S(1)} collective-permute-done((s32[1,32]{1,0:T(1,128)S(1)}, s32[1,32]{1,0:T(1,128)S(1)}, u32[]{:S(2)}, u32[]{:S(2)}) %collective-permute-start.3) | collective-permute-done | bytes 160 | tf_op jit(solution)/shard_map/ppermute | solution.py:37
  20.0 0.1 collective-permute-start.7
  20.1 1.6 %collective-permute-start.6 = (s32[1,32]{1,0:T(1,128)S(1)}, s32[1,32]{1,0:T(1,128)S(1)}, u32[]{:S(2)}, u32[]{:S(2)}) collective-permute-start(s32[1,32]{1,0:T(1,128)S(1)} %add_add_fusion.1), channel_id=1, source_target_pairs={{0,2},{1,3},{2,0},{3,1},{4,6},{5,7},{6,4},{7,5},{8,10},{9,11},{10,... | collective-permute-start | bytes 392 | tf_op jit(solution)/shard_map/ppermute | solution.py:37
  21.7 0.3 collective-permute-start.5
  21.9 1.1 %collective-permute-done.7 = s32[1,32]{1,0:T(1,128)S(1)} collective-permute-done((s32[1,32]{1,0:T(1,128)S(1)}, s32[1,32]{1,0:T(1,128)S(1)}, u32[]{:S(2)}, u32[]{:S(2)}) %collective-permute-start.7) | collective-permute-done | bytes 160 | tf_op jit(solution)/shard_map/ppermute | solution.py:37
  23.0 0.7 %collective-permute-done.6 = s32[1,32]{1,0:T(1,128)S(1)} collective-permute-done((s32[1,32]{1,0:T(1,128)S(1)}, s32[1,32]{1,0:T(1,128)S(1)}, u32[]{:S(2)}, u32[]{:S(2)}) %collective-permute-start.6) | collective-permute-done | bytes 160 | tf_op jit(solution)/shard_map/ppermute | solution.py:37
  23.7 3.5 %prev_grads.2 = (bf16[512,256]{1,0:T(8,128)(2,1)S(1)}, f32[4,8,512]{2,1,0:T(8,128)S(1)}, s32[1,512]{1,0:T(1,128)S(1)}, bf16[1280,512]{1,0:T(8,128)(2,1)S(1)}) custom-call(s32[1]{0:T(128)} %bitcast.first_ref, s32[1,32]{1,0:T(1,128)S(1)} %add_add_fusion.len_ref, bf16[512,1024]{1,0:T(8,128)(2,1)S(1)} %copy-done, bf16[512,1024]{1,0:T(8,128)(2,1)S(1)} %copy-done.1, ...), custom_call_target="tpu_custom_call" | custom-call | tf_op jit(solution)/shard_map/prev_grads/pallas_call | solution.py:247
  27.2 2.4 %collective-permute-start.10 = (bf16[512,256]{1,0:T(8,128)(2,1)S(1)}, bf16[512,256]{1,0:T(8,128)(2,1)S(1)}, u32[]{:S(2)}, u32[]{:S(2)}) collective-permute-start(bf16[512,256]{1,0:T(8,128)(2,1)S(1)} %get-tuple-element.32), channel_id=1, source_target_pairs={{0,28},{4,0},{8,4},{12,8},{16,12},{20,16},{24,20},{28,24},{1,29},{... | collective-permute-start | bytes 786440 | tf_op jit(solution)/shard_map/ppermute | solution.py:25
  29.6 4.1 %prev_grads.3 = (bf16[512,256]{1,0:T(8,128)(2,1)S(1)}, f32[4,8,512]{2,1,0:T(8,128)S(1)}, s32[1,512]{1,0:T(1,128)}, bf16[1280,512]{1,0:T(8,128)(2,1)S(1)}) custom-call(s32[1]{0:T(128)} %bitcast.first_ref, s32[1,32]{1,0:T(1,128)S(1)} %add_add_fusion.len_ref, bf16[512,1024]{1,0:T(8,128)(2,1)S(1)} %copy-done, bf16[512,1024]{1,0:T(8,128)(2,1)S(1)} %copy-done.1, ...), custom_call_target="tpu_custom_call" | custom-call | tf_op jit(solution)/shard_map/prev_grads/pallas_call | solution.py:247
  33.7 1.4 %collective-permute-start.9 = (bf16[512,256]{1,0:T(8,128)(2,1)S(1)}, bf16[512,256]{1,0:T(8,128)(2,1)S(1)}, u32[]{:S(2)}, u32[]{:S(2)}) collective-permute-start(bf16[512,256]{1,0:T(8,128)(2,1)S(1)} %get-tuple-element.31), channel_id=1, source_target_pairs={{0,28},{4,0},{8,4},{12,8},{16,12},{20,16},{24,20},{28,24},{1,29},{... | collective-permute-start | bytes 786440 | tf_op jit(solution)/shard_map/ppermute | solution.py:25
  35.1 4.0 %own_grads.1 = (bf16[512,1024]{1,0:T(8,128)(2,1)}, f32[512,256]{1,0:T(8,128)S(1)}, f32[512,256]{1,0:T(8,128)S(1)}) custom-call(bf16[512,1024]{1,0:T(8,128)(2,1)S(1)} %copy-done, bf16[512,1024]{1,0:T(8,128)(2,1)S(1)} %copy-done.1, bf16[512,256]{1,0:T(8,128)(2,1)S(1)} %copy-done.2, bf16[512,256]{1,0:T(8,128)(2,1)S(1)} %collective-permute-done.pk_ref.refs_3_, ...), custom_call_target="tpu_custom_call" | custom-call | tf_op jit(solution)/shard_map/own_grads/pallas_call | solution.py:266
  39.1 3.0 %collective-permute-done.9.refs_2_ = bf16[512,256]{1,0:T(8,128)(2,1)S(1)} collective-permute-done((bf16[512,256]{1,0:T(8,128)(2,1)S(1)}, bf16[512,256]{1,0:T(8,128)(2,1)S(1)}, u32[]{:S(2)}, u32[]{:S(2)}) %collective-permute-start.9) | collective-permute-done | bytes 262176 | tf_op jit(solution)/shard_map/ppermute | solution.py:25
  42.0 0.9 %sums.1 = (bf16[512,256]{1,0:T(8,128)(2,1)}, bf16[512,256]{1,0:T(8,128)(2,1)}) custom-call(f32[512,256]{1,0:T(8,128)S(1)} %get-tuple-element.29.refs_0_, f32[512,256]{1,0:T(8,128)S(1)} %get-tuple-element.30.refs_1_, bf16[512,256]{1,0:T(8,128)(2,1)S(1)} %collective-permute-done.9.refs_2_, bf16[512,256]{1,0:T(8,128)(2,1)S(1)} %collective-permute-done.10.refs_3_), custom_call_target="tpu_custom_call" | custom-call | tf_op jit(solution)/shard_map/sums/pallas_call | solution.py:278
  (15 shorter events, 0.1 us)
Async XLA Ops:
  1.3 11.9 %collective-permute-start.1 = (s32[1,32]{1,0:T(1,128)S(1)}, s32[1,32]{1,0:T(1,128)S(1)}, u32[]{:S(2)}, u32[]{:S(2)}) collective-permute-start(s32[1,32]{1,0:T(1,128)S(1)} %compare_select_fusion), channel_id=1, source_target_pairs={{0,4},{4,0},{8,12},{12,8},{16,20},{20,16},{24,28},{28,24},{1,5},{5... | collective-permute-start | bytes 392 | tf_op jit(solution)/shard_map/ppermute | solution.py:37
  4.3 19.4 %collective-permute-start.8 = (bf16[512,256]{1,0:T(8,128)(2,1)}, bf16[512,256]{1,0:T(8,128)(2,1)S(1)}, u32[]{:S(2)}, u32[]{:S(2)}) collective-permute-start(bf16[512,256]{1,0:T(8,128)(2,1)} %v_ref.1), channel_id=1, source_target_pairs={{0,4},{4,8},{8,12},{12,16},{16,20},{20,24},{24,28},{28,0},{1,5},{5... | collective-permute-start | bytes 786440 | tf_op jit(solution)/shard_map/ppermute | solution.py:25
  4.4 19.4 %collective-permute-start = (bf16[512,256]{1,0:T(8,128)(2,1)}, bf16[512,256]{1,0:T(8,128)(2,1)S(1)}, u32[]{:S(2)}, u32[]{:S(2)}) collective-permute-start(bf16[512,256]{1,0:T(8,128)(2,1)} %refs_2_.1), channel_id=1, source_target_pairs={{0,4},{4,8},{8,12},{12,16},{16,20},{20,24},{24,28},{28,0},{1,5},{5... | collective-permute-start | bytes 786440 | tf_op jit(solution)/shard_map/ppermute | solution.py:25
  7.3 1.2 %copy-start = (bf16[512,1024]{1,0:T(8,128)(2,1)S(1)}, bf16[512,1024]{1,0:T(8,128)(2,1)}, u32[]{:S(2)}) copy-start(bf16[512,1024]{1,0:T(8,128)(2,1)} %refs_0_.1) | copy-start | bytes 3145732
  8.6 1.2 %copy-start.1 = (bf16[512,1024]{1,0:T(8,128)(2,1)S(1)}, bf16[512,1024]{1,0:T(8,128)(2,1)}, u32[]{:S(2)}) copy-start(bf16[512,1024]{1,0:T(8,128)(2,1)} %refs_1_.1) | copy-start | bytes 3145732
  9.8 0.9 %copy-start.2 = (bf16[512,256]{1,0:T(8,128)(2,1)S(1)}, bf16[512,256]{1,0:T(8,128)(2,1)}, u32[]{:S(2)}) copy-start(bf16[512,256]{1,0:T(8,128)(2,1)} %refs_2_.1) | copy-start | bytes 786436
  10.7 0.9 %copy-start.3 = (bf16[512,256]{1,0:T(8,128)(2,1)S(1)}, bf16[512,256]{1,0:T(8,128)(2,1)}, u32[]{:S(2)}) copy-start(bf16[512,256]{1,0:T(8,128)(2,1)} %v_ref.1) | copy-start | bytes 786436
  13.2 5.4 %collective-permute-start.4 = (s32[1,32]{1,0:T(1,128)S(1)}, s32[1,32]{1,0:T(1,128)S(1)}, u32[]{:S(2)}, u32[]{:S(2)}) collective-permute-start(s32[1,32]{1,0:T(1,128)S(1)} %fusion), channel_id=1, source_target_pairs={{0,24},{4,28},{8,16},{12,20},{16,8},{20,12},{24,0},{28,4},{1,25},{... | collective-permute-start | bytes 392 | tf_op jit(solution)/shard_map/ppermute | solution.py:37
  15.6 4.4 %collective-permute-start.3 = (s32[1,32]{1,0:T(1,128)S(1)}, s32[1,32]{1,0:T(1,128)S(1)}, u32[]{:S(2)}, u32[]{:S(2)}) collective-permute-start(s32[1,32]{1,0:T(1,128)S(1)} %fusion), channel_id=1, source_target_pairs={{0,16},{4,20},{8,24},{12,28},{16,0},{20,4},{24,8},{28,12},{1,17},{... | collective-permute-start | bytes 392 | tf_op jit(solution)/shard_map/ppermute | solution.py:37
  16.3 3.7 %collective-permute-start.2 = (s32[1,32]{1,0:T(1,128)S(1)}, s32[1,32]{1,0:T(1,128)S(1)}, u32[]{:S(2)}, u32[]{:S(2)}) collective-permute-start(s32[1,32]{1,0:T(1,128)S(1)} %fusion), channel_id=1, source_target_pairs={{0,8},{4,12},{8,0},{12,4},{16,24},{20,28},{24,16},{28,20},{1,9},{5... | collective-permute-start | bytes 392 | tf_op jit(solution)/shard_map/ppermute | solution.py:37
  20.0 3.0 %collective-permute-start.7 = (s32[1,32]{1,0:T(1,128)S(1)}, s32[1,32]{1,0:T(1,128)S(1)}, u32[]{:S(2)}, u32[]{:S(2)}) collective-permute-start(s32[1,32]{1,0:T(1,128)S(1)} %add_add_fusion.1), channel_id=1, source_target_pairs={{0,3},{1,2},{2,1},{3,0},{4,7},{5,6},{6,5},{7,4},{8,11},{9,10},{10,... | collective-permute-start | bytes 392 | tf_op jit(solution)/shard_map/ppermute | solution.py:37
  20.1 3.6 %collective-permute-start.6 = (s32[1,32]{1,0:T(1,128)S(1)}, s32[1,32]{1,0:T(1,128)S(1)}, u32[]{:S(2)}, u32[]{:S(2)}) collective-permute-start(s32[1,32]{1,0:T(1,128)S(1)} %add_add_fusion.1), channel_id=1, source_target_pairs={{0,2},{1,3},{2,0},{3,1},{4,6},{5,7},{6,4},{7,5},{8,10},{9,11},{10,... | collective-permute-start | bytes 392 | tf_op jit(solution)/shard_map/ppermute | solution.py:37
  21.7 2.0 %collective-permute-start.5 = (s32[1,32]{1,0:T(1,128)S(1)}, s32[1,32]{1,0:T(1,128)S(1)}, u32[]{:S(2)}, u32[]{:S(2)}) collective-permute-start(s32[1,32]{1,0:T(1,128)S(1)} %add_add_fusion.1), channel_id=1, source_target_pairs={{0,1},{1,0},{2,3},{3,2},{4,5},{5,4},{6,7},{7,6},{8,9},{9,8},{10,11... | collective-permute-start | bytes 392 | tf_op jit(solution)/shard_map/ppermute | solution.py:37
  27.2 11.8 %collective-permute-start.10 = (bf16[512,256]{1,0:T(8,128)(2,1)S(1)}, bf16[512,256]{1,0:T(8,128)(2,1)S(1)}, u32[]{:S(2)}, u32[]{:S(2)}) collective-permute-start(bf16[512,256]{1,0:T(8,128)(2,1)S(1)} %get-tuple-element.32), channel_id=1, source_target_pairs={{0,28},{4,0},{8,4},{12,8},{16,12},{20,16},{24,20},{28,24},{1,29},{... | collective-permute-start | bytes 786440 | tf_op jit(solution)/shard_map/ppermute | solution.py:25
  33.7 8.4 %collective-permute-start.9 = (bf16[512,256]{1,0:T(8,128)(2,1)S(1)}, bf16[512,256]{1,0:T(8,128)(2,1)S(1)}, u32[]{:S(2)}, u32[]{:S(2)}) collective-permute-start(bf16[512,256]{1,0:T(8,128)(2,1)S(1)} %get-tuple-element.31), channel_id=1, source_target_pairs={{0,28},{4,0},{8,4},{12,8},{16,12},{20,16},{24,20},{28,24},{1,29},{... | collective-permute-start | bytes 786440 | tf_op jit(solution)/shard_map/ppermute | solution.py:25

commit v3 on v2

v3 whole, which is shorter than its diff:
```python
import functools

import jax
import jax.numpy as jnp
from jax import lax
from jax.experimental import pallas as pl
from jax.experimental.pallas import tpu as pltpu
from jax.sharding import PartitionSpec as P

HEAD_WIDTH = 128
BLOCK = 128
SCALE = HEAD_WIDTH ** (-0.5)
LOG2E = 1.4426950408889634
NT = (((1,), (1,)), ((), ()))
NN = (((1,), (0,)), ((), ()))
TN = (((0,), (0,)), ((), ()))


def dot(a, b, dims):
    return lax.dot_general(a, b, dims, preferred_element_type=jnp.float32)


def rotated(value, axis, steps):
    count = lax.axis_size(axis)
    return lax.ppermute(value, axis, [(s, (s + steps) % count) for s in range(count)])


def round_groups(axes):
    count = lax.axis_size(axes)
    bits = [1 << b for b in range(1, count.bit_length() - 1)]
    return [bits[n : n + 2] for n in range(0, len(bits), 2)] + [[1]]


def summed_round(value, axes, group):
    count = lax.axis_size(axes)
    masks = group + [sum(group)] * (len(group) - 1)
    others = [lax.ppermute(value, axes, [(s, s ^ m) for s in range(count)]) for m in masks]
    return functools.reduce(jnp.add, others, value)


def lengths_row(doc_lengths, axes):
    own = doc_lengths.shape[0]
    shards = lax.axis_size(axes)
    spot = lax.broadcasted_iota(jnp.int32, (1, shards, own), 1) == lax.axis_index(axes)
    return jnp.where(spot, doc_lengths[None, None, :], 0).reshape(1, shards * own)


def start_row(lengths, first, rows):
    docs = lengths.shape[1]
    before = lax.broadcasted_iota(jnp.int32, (docs, docs), 1) < lax.broadcasted_iota(
        jnp.int32, (docs, docs), 0
    )
    starts = jnp.sum(
        jnp.where(before, jnp.broadcast_to(lengths, (docs, docs)), 0), axis=1, keepdims=True
    )
    starts = jnp.broadcast_to(starts - first, (docs, rows))
    own = lax.broadcasted_iota(jnp.int32, (docs, rows), 1)
    return jnp.max(jnp.where(starts <= own, starts, -first), axis=0, keepdims=True)


def stacked(ref, i, g, heads):
    return jnp.concatenate(
        [
            ref[pl.ds(i * BLOCK, BLOCK), pl.ds((g * heads + h) * HEAD_WIDTH, HEAD_WIDTH)]
            for h in range(heads)
        ],
        axis=0,
    )


def masked(scores, start, first_key, query=None):
    key = first_key + lax.broadcasted_iota(jnp.int32, (scores.shape[0], BLOCK), 0)
    allowed = key >= start
    if query is not None:
        allowed = allowed & (key <= query)
    return jnp.concatenate(
        [
            jnp.where(allowed, scores[:, c : c + BLOCK], -jnp.inf)
            for c in range(0, scores.shape[1], BLOCK)
        ],
        axis=1,
    )


def own_span(i):
    return slice(i * (i + 1) // 2 * BLOCK, (i + 1) * (i + 2) // 2 * BLOCK)


def own_scores(s_ref, start_ref, i):
    at = slice(i * BLOCK, (i + 1) * BLOCK)
    query = i * BLOCK + lax.broadcasted_iota(jnp.int32, (1, BLOCK), 1)
    return masked(s_ref[own_span(i), :], start_ref[:, at], 0, query)


def column(g):
    return slice(g * HEAD_WIDTH, (g + 1) * HEAD_WIDTH)


def raw_kernel(after_ref, q_hbm, g_hbm, k_hbm, v_hbm, zero_ref, q_ref, g_ref, k_ref, v_ref, *outs):
    outs, sems = outs[:-1], outs[-1]
    rows, width = q_ref.shape
    kv_heads = k_ref.shape[1] // HEAD_WIDTH
    heads = width // k_ref.shape[1]
    blocks = rows // BLOCK

    def fetch(n, source, target, at):
        copy = pltpu.make_async_copy(source.at[at], target.at[at], sems.at[n])
        copy.start()
        return copy

    zero_ref[...] = jnp.zeros(zero_ref.shape, jnp.int32)
    whole = pl.ds(0, rows)
    first = [fetch(0, k_hbm, k_ref, whole), fetch(1, v_hbm, v_ref, whole)]
    parts = [
        [
            fetch(2 + 2 * i, q_hbm, q_ref, pl.ds(i * BLOCK, BLOCK)),
            fetch(3 + 2 * i, g_hbm, g_ref, pl.ds(i * BLOCK, BLOCK)),
        ]
        for i in range(blocks)
    ]
    for copy in first:
        copy.wait()
    for i in range(blocks):
        for copy in parts[i]:
            copy.wait()
        seen = slice(0, (i + 1) * BLOCK)
        for g in range(kv_heads):
            s_ref, d_ref = outs[2 * g : 2 * g + 2]
            scores = dot(k_ref[seen, column(g)], stacked(q_ref, i, g, heads), NT)
            s_ref[own_span(i), :] = scores * (SCALE * LOG2E)
            d_ref[own_span(i), :] = dot(v_ref[seen, column(g)], stacked(g_ref, i, g, heads), NT)


def prev_kernel(
    g, first_ref, len_ref, q_ref, g_ref, pk_ref, pv_ref, s_ref, d_ref,
    send_ref, stat_ref, start_ref, dq_ref, reach_ref,
):
    rows, width = q_ref.shape
    heads = width // pk_ref.shape[1]
    blocks = rows // BLOCK
    start = start_row(len_ref[...], first_ref[0], rows)
    start_ref[...] = start
    before = pl.cdiv(jnp.maximum(-jnp.min(start), 0), BLOCK)
    after = pl.cdiv(jnp.sum((start < 0).astype(jnp.int32)), BLOCK)
    reach_ref[0] = after
    for i in range(blocks):
        own = own_scores(s_ref, start_ref, i)
        top = jnp.max(own, axis=0, keepdims=True)
        own = jnp.exp2(own - top)
        stat_ref[i, 0:1, :] = top
        stat_ref[i, 1:2, :] = jnp.sum(own, axis=0, keepdims=True)
        stat_ref[i, 2:3, :] = jnp.sum(own * d_ref[own_span(i), :], axis=0, keepdims=True)

    def crossing(keys, queries):
        seen = slice((blocks - keys) * BLOCK, rows)
        key_rows, value_rows = pk_ref[seen, column(g)], pv_ref[seen, column(g)]
        probs, dscores, query_rows, grad_rows = [], [], [], []
        for i in range(queries):
            query_rows.append(stacked(q_ref, i, g, heads))
            grad_rows.append(stacked(g_ref, i, g, heads))
            prev = dot(key_rows, query_rows[i], NT) * (SCALE * LOG2E)
            prev = masked(prev, start_ref[:, i * BLOCK : (i + 1) * BLOCK], -keys * BLOCK)
            own_top, own_total, own_sum = (stat_ref[i, n : n + 1, :] for n in range(3))
            top = jnp.maximum(own_top, jnp.max(prev, axis=0, keepdims=True))
            prev = jnp.exp2(prev - top)
            kept = jnp.exp2(own_top - top)
            dprev = dot(value_rows, grad_rows[i], NT)
            total = own_total * kept + jnp.sum(prev, axis=0, keepdims=True)
            dsum = own_sum * kept + jnp.sum(prev * dprev, axis=0, keepdims=True)
            stat_ref[i, 0:1, :] = top
            stat_ref[i, 1:2, :] = total
            stat_ref[i, 2:3, :] = dsum
            inverse = 1.0 / total
            prob = prev * inverse
            dscore = (prob * (dprev - dsum * inverse)).astype(jnp.bfloat16)
            probs.append(prob.astype(jnp.bfloat16))
            dscores.append(dscore)
        probs, dscores = (jnp.concatenate(x, axis=1) for x in (probs, dscores))
        query_rows, grad_rows = (jnp.concatenate(x, axis=0) for x in (query_rows, grad_rows))
        send_ref[seen, HEAD_WIDTH:] = dot(probs, grad_rows, NN).astype(jnp.bfloat16)
        send_ref[seen, :HEAD_WIDTH] = (dot(dscores, query_rows, NN) * SCALE).astype(jnp.bfloat16)
        dq = dot(key_rows, dscores, TN)
        for i in range(queries):
            dq_ref[i] = dq[:, i * heads * BLOCK : (i + 1) * heads * BLOCK]
        if keys < blocks:
            rest = slice(0, (blocks - keys) * BLOCK)
            send_ref[rest, :] = jnp.zeros(send_ref[rest, :].shape, jnp.bfloat16)

    for keys in range(1, blocks + 1):
        for queries in range(1, blocks + 2 - keys):
            pl.when((before == keys) & (after == queries))(
                functools.partial(crossing, keys, queries)
            )

    @pl.when(after == 0)
    def _():
        send_ref[...] = jnp.zeros(send_ref.shape, jnp.bfloat16)


def own_kernel(kv_heads, *refs):
    reach_ref, q_ref, g_ref, k_ref, start_ref = refs[:5]
    per_head = [refs[5 + 4 * g : 9 + 4 * g] for g in range(kv_heads)]
    refs = refs[5 + 4 * kv_heads :]
    dq_hbm, keeps, (dq_ref, dk_ref, dv_ref, sems) = refs[0], refs[1 : 1 + kv_heads], refs[1 + kv_heads :]
    rows, width = q_ref.shape
    heads = width // k_ref.shape[1]
    blocks = rows // BLOCK
    reach = reach_ref[0]
    copies = []
    for g in range(kv_heads):
        s_ref, d_ref, stat_ref, dqp_ref = per_head[g]
        for i in reversed(range(blocks)):
            query_rows = stacked(q_ref, i, g, heads)
            grad_rows = stacked(g_ref, i, g, heads)
            seen = slice(0, (i + 1) * BLOCK)
            top, total, dsum = (stat_ref[i, n : n + 1, :] for n in range(3))
            inverse = 1.0 / total
            own = jnp.exp2(own_scores(s_ref, start_ref, i) - top) * inverse
            down = (own * (d_ref[own_span(i), :] - dsum * inverse)).astype(jnp.bfloat16)
            dv = dot(own.astype(jnp.bfloat16), grad_rows, NN)
            dk = dot(down, query_rows, NN)
            if i == blocks - 1:
                dv_ref[...] = dv
                dk_ref[...] = dk
            else:
                dv_ref[seen, :] += dv
                dk_ref[seen, :] += dk
            dq = dot(k_ref[seen, column(g)], down, TN)
            dq = (dq + jnp.where(i < reach, dqp_ref[i], 0.0)) * SCALE
            place = (
                pl.ds(i * BLOCK, BLOCK),
                pl.ds(g * heads * HEAD_WIDTH, heads * HEAD_WIDTH),
            )
            for h in range(heads):
                dq_ref[place[0], pl.ds((g * heads + h) * HEAD_WIDTH, HEAD_WIDTH)] = jnp.transpose(
                    dq[:, h * BLOCK : (h + 1) * BLOCK]
                ).astype(jnp.bfloat16)
            copy = pltpu.make_async_copy(
                dq_ref.at[place], dq_hbm.at[place], sems.at[g * blocks + i]
            )
            copy.start()
            copies.append(copy)
        keeps[g][:, :HEAD_WIDTH] = dk_ref[...] * SCALE
        keeps[g][:, HEAD_WIDTH:] = dv_ref[...]
    for copy in copies:
        copy.wait()


def sum_kernel(kv_heads, *refs):
    keep, back = refs[:kv_heads], refs[kv_heads : 2 * kv_heads]
    dk_ref, dv_ref = refs[2 * kv_heads :]
    for g in range(kv_heads):
        total = keep[g][...] + back[g][...].astype(jnp.float32)
        dk_ref[:, column(g)] = total[:, :HEAD_WIDTH].astype(jnp.bfloat16)
        dv_ref[:, column(g)] = total[:, HEAD_WIDTH:].astype(jnp.bfloat16)


def body(queries, keys, values, output_gradient, doc_lengths):
    rows = queries.shape[0]
    kv_heads = keys.shape[1] // HEAD_WIDTH
    heads = queries.shape[1] // keys.shape[1]
    blocks = rows // BLOCK
    pairs = blocks * (blocks + 1) // 2 * BLOCK
    lanes = heads * BLOCK
    prev_keys = rotated(keys, "seq", 1)
    prev_values = rotated(values, "seq", 1)
    axes = ("seq", "head")
    groups = round_groups(axes)
    row = summed_round(lengths_row(doc_lengths, axes), axes, groups[0])
    first = (lax.axis_index("seq") * rows).astype(jnp.int32).reshape(1)
    params = pltpu.CompilerParams(vmem_limit_bytes=24 * 1024 * 1024)
    shape = jax.ShapeDtypeStruct
    vmem = pl.BlockSpec(memory_space=pltpu.VMEM)
    smem = pl.BlockSpec(memory_space=pltpu.SMEM)
    hbm = pl.BlockSpec(memory_space=pltpu.HBM)
    pair = shape((rows, 2 * HEAD_WIDTH), jnp.bfloat16)
    scratch = [pltpu.VMEM((rows, HEAD_WIDTH), jnp.float32)] * 2

    arrays = (queries, output_gradient, keys, values)
    zero, q, g_out, k, v, *raw = pl.pallas_call(
        raw_kernel,
        out_shape=[shape(row.shape, jnp.int32)]
        + [pltpu.VMEM(a.shape, a.dtype) for a in arrays]
        + [pltpu.VMEM((pairs, lanes), jnp.float32)] * (2 * kv_heads),
        in_specs=[hbm] * 5,
        out_specs=[vmem] * (5 + 2 * kv_heads),
        scratch_shapes=[pltpu.SemaphoreType.DMA((2 + 2 * blocks,))],
        compiler_params=params,
        name="own_products",
    )(row, *(pltpu.with_memory_space_constraint(a, pltpu.HBM) for a in arrays))
    for n, group in enumerate(groups[1:]):
        if n == len(groups) - 2:
            row = row + zero
        row = summed_round(row, axes, group)
    sends, per_head = [], []
    for g in range(kv_heads):
        send, stat, start, dq, reach = pl.pallas_call(
            functools.partial(prev_kernel, g),
            out_shape=(
                pair,
                shape((blocks, 8, lanes), jnp.float32),
                shape((1, rows), jnp.int32),
                shape((blocks, HEAD_WIDTH, lanes), jnp.float32),
                shape((1,), jnp.int32),
            ),
            in_specs=[smem] + [vmem] * 7,
            out_specs=[vmem] * 4 + [smem],
            compiler_params=params,
            name="prev_grads",
        )(first, row, q, g_out, prev_keys, prev_values, raw[2 * g], raw[2 * g + 1])
        sends.append(send)
        per_head += [raw[2 * g], raw[2 * g + 1], stat, dq]
    backs = [rotated(send, "seq", -1) for send in sends]
    grad_queries, *keeps = pl.pallas_call(
        functools.partial(own_kernel, kv_heads),
        out_shape=[shape(queries.shape, jnp.bfloat16)]
        + [shape(pair.shape, jnp.float32)] * kv_heads,
        in_specs=[smem] + [vmem] * (4 + 4 * kv_heads),
        out_specs=[hbm] + [vmem] * kv_heads,
        scratch_shapes=[pltpu.VMEM(queries.shape, jnp.bfloat16)]
        + scratch
        + [pltpu.SemaphoreType.DMA((kv_heads * blocks,))],
        compiler_params=params,
        name="own_grads",
    )(reach, q, g_out, k, start, *per_head)
    key_gradient, value_gradient = pl.pallas_call(
        functools.partial(sum_kernel, kv_heads),
        out_shape=[shape(keys.shape, jnp.bfloat16)] * 2,
        compiler_params=params,
        name="sums",
    )(*keeps, *backs)
    return (grad_queries, key_gradient, value_gradient)


def solution(mesh):
    in_specs = (
        P("seq", "head"),
        P("seq", "head"),
        P("seq", "head"),
        P("seq", "head"),
        P(("seq", "head")),
    )
    out_specs = (P("seq", "head"), P("seq", "head"), P("seq", "head"))
    return jax.shard_map(body, mesh=mesh, in_specs=in_specs, out_specs=out_specs, check_vma=False)
```

time: 43.2 us -> 51.1 us (1.18)
  local copies, waits for them, and re-layouts: 4.35 us -> 12.5 us
  starting transfers between devices: 16.2 us -> 18.7 us
  Pallas kernels: 14 us -> 12.2 us
  waiting for transfers between devices: 7.04 us -> 5.68 us
    unnamed x8 -> x24, local copies, waits for them, and re-layouts: 4.35 us -> 12.5 us
    pallas_call x2, Pallas kernels: 7.58 us -> 3.76 us  [body(): pl.pallas_call(functools.partial(prev_kernel, g), out_shape=(pair, shape(...]
    ppermute x7, waiting for transfers between devices: 4.07 us -> 1.12 us  [summed_round(): lax.ppermute(value, axes, [(s, s ^ m) for s in range(count)])]
    ppermute x4, starting transfers between devices: 6.84 us -> 9.6 us  [rotated(): lax.ppermute(value, axis, [(s, (s + steps) % count) for s in range(count)])]
    pallas_call x1, Pallas kernels: 1.52 us -> 3.65 us  [body(): pl.pallas_call(raw_kernel, out_shape=[shape(row.shape, jnp.int32)] + [plt...]
    ppermute x4, waiting for transfers between devices: 2.97 us -> 4.57 us  [rotated(): lax.ppermute(value, axis, [(s, (s + steps) % count) for s in range(count)])]
  transfers between devices with their start and end apart: 11 -> 11, of which waited for: 5 -> 2; matrix products, arithmetic and copies ran while one was open for 0% -> 0% of each run, Pallas kernels for 22% -> 19%
where the time goes in v3:
time: 51.1 us; the launch traced here: 50.5 us
  starting transfers between devices  18.7 us (37%)
  local copies, waits for them, and re-layouts  12.5 us (24%)
  Pallas kernels  12.2 us (24%)
  waiting for transfers between devices  5.68 us (11%)
  between operations  1.4 us (3%)
    unnamed x24, local copies, waits for them, and re-layouts  12.5 us
    ppermute x4, starting transfers between devices, rotated(): lax.ppermute(value, axis, [(s, (s + steps) % count) for s in range(count)])  9.6 us
    ppermute x7, starting transfers between devices, summed_round(): lax.ppermute(value, axes, [(s, s ^ m) for s in range(count)])  9.07 us
    ppermute x4, waiting for transfers between devices, rotated(): lax.ppermute(value, axis, [(s, (s + steps) % count) for s in range(count)])  4.57 us
    pallas_call x1, Pallas kernels, body(): pl.pallas_call(functools.partial(own_kernel, kv_heads), out_shape=[shape(...  3.87 us
    pallas_call x2, Pallas kernels, body(): pl.pallas_call(functools.partial(prev_kernel, g), out_shape=(pair, shape(...  3.76 us
    pallas_call x1, Pallas kernels, body(): pl.pallas_call(raw_kernel, out_shape=[shape(row.shape, jnp.int32)] + [plt...  3.65 us
    ppermute x7, waiting for transfers between devices, summed_round(): lax.ppermute(value, axes, [(s, s ^ m) for s in range(count)])  1.12 us
  transfers between devices with their start and end apart: 11, of which 2 were waited for; matrix products, arithmetic and copies ran while one was open for 0% of the time, Pallas kernels for 19%

profile of v3, /device:TPU:0, one launch (start us, length us, event | category | flops | bytes accessed | tf_op | source)
XLA Modules:
  0.0 50.5 jit_solution(14095882264048195813)
XLA Ops:
  1.3 3.0 %collective-permute-start.1 = (s32[1,32]{1,0:T(1,128)S(1)}, s32[1,32]{1,0:T(1,128)S(1)}, u32[]{:S(2)}, u32[]{:S(2)}) collective-permute-start(s32[1,32]{1,0:T(1,128)S(1)} %compare_select_fusion), channel_id=1, source_target_pairs={{0,4},{1,5},{2,6},{3,7},{4,0},{5,1},{6,2},{7,3},{8,12},{9,13},{10,... | collective-permute-start | bytes 392 | tf_op jit(solution)/shard_map/ppermute | solution.py:37
  4.3 1.5 %collective-permute-start.2 = (s32[1,32]{1,0:T(1,128)S(1)}, s32[1,32]{1,0:T(1,128)S(1)}, u32[]{:S(2)}, u32[]{:S(2)}) collective-permute-start(s32[1,32]{1,0:T(1,128)S(1)} %compare_select_fusion), channel_id=1, source_target_pairs={{0,6},{1,7},{2,4},{3,5},{4,2},{5,3},{6,0},{7,1},{8,14},{9,15},{10,... | collective-permute-start | bytes 392 | tf_op jit(solution)/shard_map/ppermute | solution.py:37
  5.8 1.9 %collective-permute-start.7 = (bf16[512,256]{1,0:T(8,128)(2,1)}, bf16[512,256]{1,0:T(8,128)(2,1)S(1)}, u32[]{:S(2)}, u32[]{:S(2)}) collective-permute-start(bf16[512,256]{1,0:T(8,128)(2,1)} %k_hbm.1), channel_id=1, source_target_pairs={{0,4},{4,8},{8,12},{12,16},{16,20},{20,24},{24,28},{28,0},{1,5},{5... | collective-permute-start | bytes 786440 | tf_op jit(solution)/shard_map/ppermute | solution.py:25
  7.8 1.5 %collective-permute-start.8 = (bf16[512,256]{1,0:T(8,128)(2,1)}, bf16[512,256]{1,0:T(8,128)(2,1)S(1)}, u32[]{:S(2)}, u32[]{:S(2)}) collective-permute-start(bf16[512,256]{1,0:T(8,128)(2,1)} %v_hbm.1), channel_id=1, source_target_pairs={{0,4},{4,8},{8,12},{12,16},{16,20},{20,24},{24,28},{28,0},{1,5},{5... | collective-permute-start | bytes 786440 | tf_op jit(solution)/shard_map/ppermute | solution.py:25
  9.4 3.6 %collective-permute-start.5 = (s32[1,32]{1,0:T(1,128)S(1)}, s32[1,32]{1,0:T(1,128)S(1)}, u32[]{:S(2)}, u32[]{:S(2)}) collective-permute-start(s32[1,32]{1,0:T(1,128)S(1)} %add_add_fusion.1.after_ref), channel_id=1, source_target_pairs={{0,24},{1,25},{2,26},{3,27},{4,28},{5,29},{6,30},{7,31},{8,16},{9,... | collective-permute-start | bytes 392 | tf_op jit(solution)/shard_map/ppermute | solution.py:37
  12.9 0.9 %collective-permute-start.3 = (s32[1,32]{1,0:T(1,128)S(1)}, s32[1,32]{1,0:T(1,128)S(1)}, u32[]{:S(2)}, u32[]{:S(2)}) collective-permute-start(s32[1,32]{1,0:T(1,128)S(1)} %add_add_fusion.1.after_ref), channel_id=1, source_target_pairs={{0,8},{1,9},{2,10},{3,11},{4,12},{5,13},{6,14},{7,15},{8,0},{9,1},... | collective-permute-start | bytes 392 | tf_op jit(solution)/shard_map/ppermute | solution.py:37
  13.8 3.7 %own_products.1 = (s32[1,32]{1,0:T(1,128)S(1)}, bf16[512,1024]{1,0:T(8,128)(2,1)S(1)}, bf16[512,1024]{1,0:T(8,128)(2,1)S(1)}, bf16[512,256]{1,0:T(8,128)(2,1)S(1...) custom-call(s32[1,32]{1,0:T(1,128)S(1)} %add_add_fusion.1.after_ref,, ...), custom_call_target="tpu_custom_call" | custom-call | tf_op jit(solution)/shard_map/own_products/pallas_call | solution.py:280
  17.5 1.5 %copy-done = f32[1280,512]{1,0:T(8,128)} copy-done((f32[1280,512]{1,0:T(8,128)}, f32[1280,512]{1,0:T(8,128)S(1)}, u32[]{:S(2)}) %copy-start) | copy-done | bytes 2621464
  19.0 1.5 %copy-done.2 = f32[1280,512]{1,0:T(8,128)} copy-done((f32[1280,512]{1,0:T(8,128)}, f32[1280,512]{1,0:T(8,128)S(1)}, u32[]{:S(2)}) %copy-start.2) | copy-done | bytes 2621464
  20.5 1.6 %copy-done.5 = f32[1280,512]{1,0:T(8,128)} copy-done((f32[1280,512]{1,0:T(8,128)}, f32[1280,512]{1,0:T(8,128)S(1)}, u32[]{:S(2)}) %copy-start.5) | copy-done | bytes 2621464
  22.1 1.0 %copy-done.8 = bf16[512,1024]{1,0:T(8,128)(2,1)} copy-done((bf16[512,1024]{1,0:T(8,128)(2,1)}, bf16[512,1024]{1,0:T(8,128)(2,1)S(1)}, u32[]{:S(2)}) %copy-start.8) | copy-done | bytes 1048600
  23.0 1.1 %copy-done.10 = bf16[512,1024]{1,0:T(8,128)(2,1)} copy-done((bf16[512,1024]{1,0:T(8,128)(2,1)}, bf16[512,1024]{1,0:T(8,128)(2,1)S(1)}, u32[]{:S(2)}) %copy-start.10) | copy-done | bytes 1048600
  24.2 1.1 %collective-permute-done.6 = s32[1,32]{1,0:T(1,128)S(1)} collective-permute-done((s32[1,32]{1,0:T(1,128)S(1)}, s32[1,32]{1,0:T(1,128)S(1)}, u32[]{:S(2)}, u32[]{:S(2)}) %collective-permute-start.6) | collective-permute-done | bytes 160 | tf_op jit(solution)/shard_map/ppermute | solution.py:37
  25.3 1.7 %copy-done.3 = f32[1280,512]{1,0:T(8,128)S(1)} copy-done((f32[1280,512]{1,0:T(8,128)S(1)}, f32[1280,512]{1,0:T(8,128)}, u32[]{:S(2)}) %copy-start.3) | copy-done | bytes 2621464
  27.0 1.7 %copy-done.6 = f32[1280,512]{1,0:T(8,128)S(1)} copy-done((f32[1280,512]{1,0:T(8,128)S(1)}, f32[1280,512]{1,0:T(8,128)}, u32[]{:S(2)}) %copy-start.6) | copy-done | bytes 2621464
  28.8 1.2 %copy-done.9 = bf16[512,1024]{1,0:T(8,128)(2,1)S(1)} copy-done((bf16[512,1024]{1,0:T(8,128)(2,1)S(1)}, bf16[512,1024]{1,0:T(8,128)(2,1)}, u32[]{:S(2)}) %copy-start.9) | copy-done | bytes 1048600
  30.0 1.2 %copy-done.11 = bf16[512,1024]{1,0:T(8,128)(2,1)S(1)} copy-done((bf16[512,1024]{1,0:T(8,128)(2,1)S(1)}, bf16[512,1024]{1,0:T(8,128)(2,1)}, u32[]{:S(2)}) %copy-start.11) | copy-done | bytes 1048600
  31.2 1.8 %prev_grads.2 = (bf16[512,256]{1,0:T(8,128)(2,1)S(1)}, f32[4,8,512]{2,1,0:T(8,128)S(1)}, s32[1,512]{1,0:T(1,128)S(1)}, f32[4,128,512]{2,1,0:T(8,128)S(1)}, s32[1]{0:T(128)}) custom-call(s32[1]{0:T(128)} %bitcast.first_ref, s32[1,32]{1,0:T(1,128)S(1)} %add.35.len_ref, bf16[512,1024]{1,0:T(8,128)(2,1)S(1)} %copy-done.9, bf16[512,1024]{1,0:T(8,128)(2,1)S(1)} %copy-done.11, ...), custom_call_target="tpu_custom_call" | custom-call | tf_op jit(solution)/shard_map/prev_grads/pallas_call | solution.py:297
  33.0 5.0 %collective-permute-start.10 = (bf16[512,256]{1,0:T(8,128)(2,1)S(1)}, bf16[512,256]{1,0:T(8,128)(2,1)S(1)}, u32[]{:S(2)}, u32[]{:S(2)}) collective-permute-start(bf16[512,256]{1,0:T(8,128)(2,1)S(1)} %get-tuple-element.42), channel_id=1, source_target_pairs={{0,28},{4,0},{8,4},{12,8},{16,12},{20,16},{24,20},{28,24},{1,29},{... | collective-permute-start | bytes 786440 | tf_op jit(solution)/shard_map/ppermute | solution.py:25
  38.0 2.0 %prev_grads.3 = (bf16[512,256]{1,0:T(8,128)(2,1)S(1)}, f32[4,8,512]{2,1,0:T(8,128)S(1)}, s32[1,512]{1,0:T(1,128)}, f32[4,128,512]{2,1,0:T(8,128)S(1)}, s32[1]{0:T(128)}) custom-call(s32[1]{0:T(128)} %bitcast.first_ref, s32[1,32]{1,0:T(1,128)S(1)} %add.35.len_ref, bf16[512,1024]{1,0:T(8,128)(2,1)S(1)} %copy-done.9, bf16[512,1024]{1,0:T(8,128)(2,1)S(1)} %copy-done.11, ...), custom_call_target="tpu_custom_call" | custom-call | tf_op jit(solution)/shard_map/prev_grads/pallas_call | solution.py:297
  40.0 1.1 %collective-permute-start.9 = (bf16[512,256]{1,0:T(8,128)(2,1)S(1)}, bf16[512,256]{1,0:T(8,128)(2,1)S(1)}, u32[]{:S(2)}, u32[]{:S(2)}) collective-permute-start(bf16[512,256]{1,0:T(8,128)(2,1)S(1)} %get-tuple-element.41), channel_id=1, source_target_pairs={{0,28},{4,0},{8,4},{12,8},{16,12},{20,16},{24,20},{28,24},{1,29},{... | collective-permute-start | bytes 786440 | tf_op jit(solution)/shard_map/ppermute | solution.py:25
  41.1 3.9 %own_grads.1 = (bf16[512,1024]{1,0:T(8,128)(2,1)}, f32[512,256]{1,0:T(8,128)S(1)}, f32[512,256]{1,0:T(8,128)S(1)}) custom-call(s32[1]{0:T(128)} %get-tuple-element.29.refs_0_, bf16[512,1024]{1,0:T(8,128)(2,1)S(1)} %copy-done.9, bf16[512,1024]{1,0:T(8,128)(2,1)S(1)} %copy-done.11, bf16[512,256]{1,0:T(8,128)(2,1)S(1)} %get-tuple-element.30.refs_3_, ...), custom_call_target="tpu_custom_call" | custom-call | tf_op jit(solution)/shard_map/own_grads/pallas_call | solution.py:314
  45.0 4.6 %collective-permute-done.9.refs_2_ = bf16[512,256]{1,0:T(8,128)(2,1)S(1)} collective-permute-done((bf16[512,256]{1,0:T(8,128)(2,1)S(1)}, bf16[512,256]{1,0:T(8,128)(2,1)S(1)}, u32[]{:S(2)}, u32[]{:S(2)}) %collective-permute-start.9) | collective-permute-done | bytes 262176 | tf_op jit(solution)/shard_map/ppermute | solution.py:25
  49.6 0.9 %sums.1 = (bf16[512,256]{1,0:T(8,128)(2,1)}, bf16[512,256]{1,0:T(8,128)(2,1)}) custom-call(f32[512,256]{1,0:T(8,128)S(1)} %get-tuple-element.39.refs_0_, f32[512,256]{1,0:T(8,128)S(1)} %get-tuple-element.40.refs_1_, bf16[512,256]{1,0:T(8,128)(2,1)S(1)} %collective-permute-done.9.refs_2_, bf16[512,256]{1,0:T(8,128)(2,1)S(1)} %collective-permute-done.10.refs_3_), custom_call_target="tpu_custom_call" | custom-call | tf_op jit(solution)/shard_map/sums/pallas_call | solution.py:326
  (31 shorter events, 0.2 us)
Async XLA Ops:
  1.3 8.0 %collective-permute-start.1 = (s32[1,32]{1,0:T(1,128)S(1)}, s32[1,32]{1,0:T(1,128)S(1)}, u32[]{:S(2)}, u32[]{:S(2)}) collective-permute-start(s32[1,32]{1,0:T(1,128)S(1)} %compare_select_fusion), channel_id=1, source_target_pairs={{0,4},{1,5},{2,6},{3,7},{4,0},{5,1},{6,2},{7,3},{8,12},{9,13},{10,... | collective-permute-start | bytes 392 | tf_op jit(solution)/shard_map/ppermute | solution.py:37
  4.3 5.0 %collective-permute-start.2 = (s32[1,32]{1,0:T(1,128)S(1)}, s32[1,32]{1,0:T(1,128)S(1)}, u32[]{:S(2)}, u32[]{:S(2)}) collective-permute-start(s32[1,32]{1,0:T(1,128)S(1)} %compare_select_fusion), channel_id=1, source_target_pairs={{0,6},{1,7},{2,4},{3,5},{4,2},{5,3},{6,0},{7,1},{8,14},{9,15},{10,... | collective-permute-start | bytes 392 | tf_op jit(solution)/shard_map/ppermute | solution.py:37
  5.8 3.6 %collective-permute-start = (s32[1,32]{1,0:T(1,128)S(1)}, s32[1,32]{1,0:T(1,128)S(1)}, u32[]{:S(2)}, u32[]{:S(2)}) collective-permute-start(s32[1,32]{1,0:T(1,128)S(1)} %compare_select_fusion), channel_id=1, source_target_pairs={{0,2},{1,3},{2,0},{3,1},{4,6},{5,7},{6,4},{7,5},{8,10},{9,11},{10,... | collective-permute-start | bytes 392 | tf_op jit(solution)/shard_map/ppermute | solution.py:37
  5.8 19.5 %collective-permute-start.7 = (bf16[512,256]{1,0:T(8,128)(2,1)}, bf16[512,256]{1,0:T(8,128)(2,1)S(1)}, u32[]{:S(2)}, u32[]{:S(2)}) collective-permute-start(bf16[512,256]{1,0:T(8,128)(2,1)} %k_hbm.1), channel_id=1, source_target_pairs={{0,4},{4,8},{8,12},{12,16},{16,20},{20,24},{24,28},{28,0},{1,5},{5... | collective-permute-start | bytes 786440 | tf_op jit(solution)/shard_map/ppermute | solution.py:25
  7.8 17.5 %collective-permute-start.8 = (bf16[512,256]{1,0:T(8,128)(2,1)}, bf16[512,256]{1,0:T(8,128)(2,1)S(1)}, u32[]{:S(2)}, u32[]{:S(2)}) collective-permute-start(bf16[512,256]{1,0:T(8,128)(2,1)} %v_hbm.1), channel_id=1, source_target_pairs={{0,4},{4,8},{8,12},{12,16},{16,20},{20,24},{24,28},{28,0},{1,5},{5... | collective-permute-start | bytes 786440 | tf_op jit(solution)/shard_map/ppermute | solution.py:25
  9.4 14.7 %collective-permute-start.5 = (s32[1,32]{1,0:T(1,128)S(1)}, s32[1,32]{1,0:T(1,128)S(1)}, u32[]{:S(2)}, u32[]{:S(2)}) collective-permute-start(s32[1,32]{1,0:T(1,128)S(1)} %add_add_fusion.1.after_ref), channel_id=1, source_target_pairs={{0,24},{1,25},{2,26},{3,27},{4,28},{5,29},{6,30},{7,31},{8,16},{9,... | collective-permute-start | bytes 392 | tf_op jit(solution)/shard_map/ppermute | solution.py:37
  12.9 11.1 %collective-permute-start.4 = (s32[1,32]{1,0:T(1,128)S(1)}, s32[1,32]{1,0:T(1,128)S(1)}, u32[]{:S(2)}, u32[]{:S(2)}) collective-permute-start(s32[1,32]{1,0:T(1,128)S(1)} %add_add_fusion.1.after_ref), channel_id=1, source_target_pairs={{0,16},{1,17},{2,18},{3,19},{4,20},{5,21},{6,22},{7,23},{8,24},{9,... | collective-permute-start | bytes 392 | tf_op jit(solution)/shard_map/ppermute | solution.py:37
  12.9 11.1 %collective-permute-start.3 = (s32[1,32]{1,0:T(1,128)S(1)}, s32[1,32]{1,0:T(1,128)S(1)}, u32[]{:S(2)}, u32[]{:S(2)}) collective-permute-start(s32[1,32]{1,0:T(1,128)S(1)} %add_add_fusion.1.after_ref), channel_id=1, source_target_pairs={{0,8},{1,9},{2,10},{3,11},{4,12},{5,13},{6,14},{7,15},{8,0},{9,1},... | collective-permute-start | bytes 392 | tf_op jit(solution)/shard_map/ppermute | solution.py:37
  17.5 1.5 %copy-start = (f32[1280,512]{1,0:T(8,128)}, f32[1280,512]{1,0:T(8,128)S(1)}, u32[]{:S(2)}) copy-start(f32[1280,512]{1,0:T(8,128)S(1)} %get-tuple-element.33.d_ref.refs_6_) | copy-start | bytes 7864324
  19.0 1.5 %copy-start.2 = (f32[1280,512]{1,0:T(8,128)}, f32[1280,512]{1,0:T(8,128)S(1)}, u32[]{:S(2)}) copy-start(f32[1280,512]{1,0:T(8,128)S(1)} %get-tuple-element.27.s_ref.refs_9_) | copy-start | bytes 7864324
  20.5 1.6 %copy-start.5 = (f32[1280,512]{1,0:T(8,128)}, f32[1280,512]{1,0:T(8,128)S(1)}, u32[]{:S(2)}) copy-start(f32[1280,512]{1,0:T(8,128)S(1)} %get-tuple-element.28.d_ref.refs_10_) | copy-start | bytes 7864324
  22.0 1.0 %copy-start.8 = (bf16[512,1024]{1,0:T(8,128)(2,1)}, bf16[512,1024]{1,0:T(8,128)(2,1)S(1)}, u32[]{:S(2)}) copy-start(bf16[512,1024]{1,0:T(8,128)(2,1)S(1)} %get-tuple-element.25.q_ref.refs_1_) | copy-start | bytes 3145732
  23.0 1.1 %copy-start.10 = (bf16[512,1024]{1,0:T(8,128)(2,1)}, bf16[512,1024]{1,0:T(8,128)(2,1)S(1)}, u32[]{:S(2)}) copy-start(bf16[512,1024]{1,0:T(8,128)(2,1)S(1)} %get-tuple-element.26.g_ref.refs_2_) | copy-start | bytes 3145732
  24.1 1.2 %collective-permute-start.6 = (s32[1,32]{1,0:T(1,128)S(1)}, s32[1,32]{1,0:T(1,128)S(1)}, u32[]{:S(2)}, u32[]{:S(2)}) collective-permute-start(s32[1,32]{1,0:T(1,128)S(1)} %add_add_fusion), channel_id=1, source_target_pairs={{0,1},{1,0},{2,3},{3,2},{4,5},{5,4},{6,7},{7,6},{8,9},{9,8},{10,11... | collective-permute-start | bytes 392 | tf_op jit(solution)/shard_map/ppermute | solution.py:37
  25.3 1.7 %copy-start.3 = (f32[1280,512]{1,0:T(8,128)S(1)}, f32[1280,512]{1,0:T(8,128)}, u32[]{:S(2)}) copy-start(f32[1280,512]{1,0:T(8,128)} %copy-done.2) | copy-start | bytes 7864324
  27.0 1.7 %copy-start.6 = (f32[1280,512]{1,0:T(8,128)S(1)}, f32[1280,512]{1,0:T(8,128)}, u32[]{:S(2)}) copy-start(f32[1280,512]{1,0:T(8,128)} %copy-done.5) | copy-start | bytes 7864324
  28.8 1.2 %copy-start.9 = (bf16[512,1024]{1,0:T(8,128)(2,1)S(1)}, bf16[512,1024]{1,0:T(8,128)(2,1)}, u32[]{:S(2)}) copy-start(bf16[512,1024]{1,0:T(8,128)(2,1)} %copy-done.8) | copy-start | bytes 3145732
  30.0 1.2 %copy-start.11 = (bf16[512,1024]{1,0:T(8,128)(2,1)S(1)}, bf16[512,1024]{1,0:T(8,128)(2,1)}, u32[]{:S(2)}) copy-start(bf16[512,1024]{1,0:T(8,128)(2,1)} %copy-done.10) | copy-start | bytes 3145732
  31.2 6.8 %copy-start.1 = (f32[1280,512]{1,0:T(8,128)S(1)}, f32[1280,512]{1,0:T(8,128)}, u32[]{:S(2)}) copy-start(f32[1280,512]{1,0:T(8,128)} %copy-done) | copy-start | bytes 7864324
  33.0 12.0 %collective-permute-start.10 = (bf16[512,256]{1,0:T(8,128)(2,1)S(1)}, bf16[512,256]{1,0:T(8,128)(2,1)S(1)}, u32[]{:S(2)}, u32[]{:S(2)}) collective-permute-start(bf16[512,256]{1,0:T(8,128)(2,1)S(1)} %get-tuple-element.42), channel_id=1, source_target_pairs={{0,28},{4,0},{8,4},{12,8},{16,12},{20,16},{24,20},{28,24},{1,29},{... | collective-permute-start | bytes 786440 | tf_op jit(solution)/shard_map/ppermute | solution.py:25
  38.0 3.1 %copy-start.4 = (f32[1280,512]{1,0:T(8,128)S(1)}, f32[1280,512]{1,0:T(8,128)}, u32[]{:S(2)}) copy-start(f32[1280,512]{1,0:T(8,128)} %copy-done.2) | copy-start | bytes 7864324
  38.0 3.1 %copy-start.7 = (f32[1280,512]{1,0:T(8,128)S(1)}, f32[1280,512]{1,0:T(8,128)}, u32[]{:S(2)}) copy-start(f32[1280,512]{1,0:T(8,128)} %copy-done.5) | copy-start | bytes 7864324
  40.0 9.6 %collective-permute-start.9 = (bf16[512,256]{1,0:T(8,128)(2,1)S(1)}, bf16[512,256]{1,0:T(8,128)(2,1)S(1)}, u32[]{:S(2)}, u32[]{:S(2)}) collective-permute-start(bf16[512,256]{1,0:T(8,128)(2,1)S(1)} %get-tuple-element.41), channel_id=1, source_target_pairs={{0,28},{4,0},{8,4},{12,8},{16,12},{20,16},{24,20},{28,24},{1,29},{... | collective-permute-start | bytes 786440 | tf_op jit(solution)/shard_map/ppermute | solution.py:25

commit v4 on v3

--- a/solution.py
+++ b/solution.py
@@ -96,8 +96,8 @@
     return slice(g * HEAD_WIDTH, (g + 1) * HEAD_WIDTH)
 
 
-def raw_kernel(after_ref, q_hbm, g_hbm, k_hbm, v_hbm, zero_ref, q_ref, g_ref, k_ref, v_ref, *outs):
-    outs, sems = outs[:-1], outs[-1]
+def raw_kernel(after_ref, q_hbm, g_hbm, k_hbm, v_hbm, zero_ref, q_ref, g_ref, k_ref, *outs):
+    outs, v_ref, sems = outs[:-2], outs[-2], outs[-1]
     rows, width = q_ref.shape
     kv_heads = k_ref.shape[1] // HEAD_WIDTH
     heads = width // k_ref.shape[1]
@@ -277,14 +277,17 @@
     scratch = [pltpu.VMEM((rows, HEAD_WIDTH), jnp.float32)] * 2
 
     arrays = (queries, output_gradient, keys, values)
-    zero, q, g_out, k, v, *raw = pl.pallas_call(
+    zero, q, g_out, k, *raw = pl.pallas_call(
         raw_kernel,
         out_shape=[shape(row.shape, jnp.int32)]
-        + [pltpu.VMEM(a.shape, a.dtype) for a in arrays]
-        + [pltpu.VMEM((pairs, lanes), jnp.float32)] * (2 * kv_heads),
+        + [shape(a.shape, a.dtype) for a in arrays[:3]]
+        + [shape((pairs, lanes), jnp.float32)] * (2 * kv_heads),
         in_specs=[hbm] * 5,
-        out_specs=[vmem] * (5 + 2 * kv_heads),
-        scratch_shapes=[pltpu.SemaphoreType.DMA((2 + 2 * blocks,))],
+        out_specs=[vmem] * (4 + 2 * kv_heads),
+        scratch_shapes=[
+            pltpu.VMEM(values.shape, values.dtype),
+            pltpu.SemaphoreType.DMA((2 + 2 * blocks,)),
+        ],
         compiler_params=params,
         name="own_products",
     )(row, *(pltpu.with_memory_space_constraint(a, pltpu.HBM) for a in arrays))

time: 51.1 us -> 50.5 us (0.988)
  transfers between devices with their start and end apart: 11 -> 11, of which waited for: 2 -> 2; matrix products, arithmetic and copies ran while one was open for 0% -> 0% of each run, Pallas kernels for 19% -> 18%
where the time goes in v4:
time: 50.5 us; the launch traced here: 50.1 us
  starting transfers between devices  18.9 us (37%)
  local copies, waits for them, and re-layouts  12.5 us (25%)
  Pallas kernels  11.8 us (23%)
  waiting for transfers between devices  5.45 us (11%)
  between operations  1.4 us (3%)
    unnamed x24, local copies, waits for them, and re-layouts  12.5 us
    ppermute x4, starting transfers between devices, rotated(): lax.ppermute(value, axis, [(s, (s + steps) % count) for s in range(count)])  9.83 us
    ppermute x7, starting transfers between devices, summed_round(): lax.ppermute(value, axes, [(s, s ^ m) for s in range(count)])  9.07 us
    ppermute x4, waiting for transfers between devices, rotated(): lax.ppermute(value, axis, [(s, (s + steps) % count) for s in range(count)])  4.33 us
    pallas_call x1, Pallas kernels, body(): pl.pallas_call(functools.partial(own_kernel, kv_heads), out_shape=[shape(...  3.87 us
    pallas_call x2, Pallas kernels, body(): pl.pallas_call(functools.partial(prev_kernel, g), out_shape=(pair, shape(...  3.76 us
    pallas_call x1, Pallas kernels, body(): pl.pallas_call(raw_kernel, out_shape=[shape(row.shape, jnp.int32)] + [sha...  3.3 us
    ppermute x7, waiting for transfers between devices, summed_round(): lax.ppermute(value, axes, [(s, s ^ m) for s in range(count)])  1.12 us
  transfers between devices with their start and end apart: 11, of which 2 were waited for; matrix products, arithmetic and copies ran while one was open for 0% of the time, Pallas kernels for 18%

profile of v4, /device:TPU:0, one launch (start us, length us, event | category | flops | bytes accessed | tf_op | source)
XLA Modules:
  0.0 50.1 jit_solution(5671930355925552862)
XLA Ops:
  1.3 3.0 %collective-permute-start.1 = (s32[1,32]{1,0:T(1,128)S(1)}, s32[1,32]{1,0:T(1,128)S(1)}, u32[]{:S(2)}, u32[]{:S(2)}) collective-permute-start(s32[1,32]{1,0:T(1,128)S(1)} %compare_select_fusion), channel_id=1, source_target_pairs={{0,4},{1,5},{2,6},{3,7},{4,0},{5,1},{6,2},{7,3},{8,12},{9,13},{10,... | collective-permute-start | bytes 392 | tf_op jit(solution)/shard_map/ppermute | solution.py:37
  4.3 1.5 %collective-permute-start.2 = (s32[1,32]{1,0:T(1,128)S(1)}, s32[1,32]{1,0:T(1,128)S(1)}, u32[]{:S(2)}, u32[]{:S(2)}) collective-permute-start(s32[1,32]{1,0:T(1,128)S(1)} %compare_select_fusion), channel_id=1, source_target_pairs={{0,6},{1,7},{2,4},{3,5},{4,2},{5,3},{6,0},{7,1},{8,14},{9,15},{10,... | collective-permute-start | bytes 392 | tf_op jit(solution)/shard_map/ppermute | solution.py:37
  5.8 1.9 %collective-permute-start.7 = (bf16[512,256]{1,0:T(8,128)(2,1)}, bf16[512,256]{1,0:T(8,128)(2,1)S(1)}, u32[]{:S(2)}, u32[]{:S(2)}) collective-permute-start(bf16[512,256]{1,0:T(8,128)(2,1)} %k_hbm.1), channel_id=1, source_target_pairs={{0,4},{4,8},{8,12},{12,16},{16,20},{20,24},{24,28},{28,0},{1,5},{5... | collective-permute-start | bytes 786440 | tf_op jit(solution)/shard_map/ppermute | solution.py:25
  7.8 1.5 %collective-permute-start.8 = (bf16[512,256]{1,0:T(8,128)(2,1)}, bf16[512,256]{1,0:T(8,128)(2,1)S(1)}, u32[]{:S(2)}, u32[]{:S(2)}) collective-permute-start(bf16[512,256]{1,0:T(8,128)(2,1)} %v_hbm.1), channel_id=1, source_target_pairs={{0,4},{4,8},{8,12},{12,16},{16,20},{20,24},{24,28},{28,0},{1,5},{5... | collective-permute-start | bytes 786440 | tf_op jit(solution)/shard_map/ppermute | solution.py:25
  9.4 3.6 %collective-permute-start.5 = (s32[1,32]{1,0:T(1,128)S(1)}, s32[1,32]{1,0:T(1,128)S(1)}, u32[]{:S(2)}, u32[]{:S(2)}) collective-permute-start(s32[1,32]{1,0:T(1,128)S(1)} %add_add_fusion.1.after_ref), channel_id=1, source_target_pairs={{0,24},{1,25},{2,26},{3,27},{4,28},{5,29},{6,30},{7,31},{8,16},{9,... | collective-permute-start | bytes 392 | tf_op jit(solution)/shard_map/ppermute | solution.py:37
  12.9 0.9 %collective-permute-start.3 = (s32[1,32]{1,0:T(1,128)S(1)}, s32[1,32]{1,0:T(1,128)S(1)}, u32[]{:S(2)}, u32[]{:S(2)}) collective-permute-start(s32[1,32]{1,0:T(1,128)S(1)} %add_add_fusion.1.after_ref), channel_id=1, source_target_pairs={{0,8},{1,9},{2,10},{3,11},{4,12},{5,13},{6,14},{7,15},{8,0},{9,1},... | collective-permute-start | bytes 392 | tf_op jit(solution)/shard_map/ppermute | solution.py:37
  13.8 3.3 %own_products.1 = (s32[1,32]{1,0:T(1,128)S(1)}, bf16[512,1024]{1,0:T(8,128)(2,1)S(1)}, bf16[512,1024]{1,0:T(8,128)(2,1)S(1)}, bf16[512,256]{1,0:T(8,128)(2,1)S(1...) custom-call(s32[1,32]{1,0:T(1,128)S(1)} %add_add_fusion.1.after_ref, ...), custom_call_target="tpu_custom_call" | custom-call | tf_op jit(solution)/shard_map/own_products/pallas_call | solution.py:280
  17.1 1.5 %copy-done = f32[1280,512]{1,0:T(8,128)} copy-done((f32[1280,512]{1,0:T(8,128)}, f32[1280,512]{1,0:T(8,128)S(1)}, u32[]{:S(2)}) %copy-start) | copy-done | bytes 2621464
  18.6 1.5 %copy-done.2 = f32[1280,512]{1,0:T(8,128)} copy-done((f32[1280,512]{1,0:T(8,128)}, f32[1280,512]{1,0:T(8,128)S(1)}, u32[]{:S(2)}) %copy-start.2) | copy-done | bytes 2621464
  20.1 1.6 %copy-done.5 = f32[1280,512]{1,0:T(8,128)} copy-done((f32[1280,512]{1,0:T(8,128)}, f32[1280,512]{1,0:T(8,128)S(1)}, u32[]{:S(2)}) %copy-start.5) | copy-done | bytes 2621464
  21.7 1.0 %copy-done.8 = bf16[512,1024]{1,0:T(8,128)(2,1)} copy-done((bf16[512,1024]{1,0:T(8,128)(2,1)}, bf16[512,1024]{1,0:T(8,128)(2,1)S(1)}, u32[]{:S(2)}) %copy-start.8) | copy-done | bytes 1048600
  22.7 1.1 %copy-done.10 = bf16[512,1024]{1,0:T(8,128)(2,1)} copy-done((bf16[512,1024]{1,0:T(8,128)(2,1)}, bf16[512,1024]{1,0:T(8,128)(2,1)S(1)}, u32[]{:S(2)}) %copy-start.10) | copy-done | bytes 1048600
  23.8 1.1 %collective-permute-done.6 = s32[1,32]{1,0:T(1,128)S(1)} collective-permute-done((s32[1,32]{1,0:T(1,128)S(1)}, s32[1,32]{1,0:T(1,128)S(1)}, u32[]{:S(2)}, u32[]{:S(2)}) %collective-permute-start.6) | collective-permute-done | bytes 160 | tf_op jit(solution)/shard_map/ppermute | solution.py:37
  25.0 1.7 %copy-done.3 = f32[1280,512]{1,0:T(8,128)S(1)} copy-done((f32[1280,512]{1,0:T(8,128)S(1)}, f32[1280,512]{1,0:T(8,128)}, u32[]{:S(2)}) %copy-start.3) | copy-done | bytes 2621464
  26.7 1.7 %copy-done.6 = f32[1280,512]{1,0:T(8,128)S(1)} copy-done((f32[1280,512]{1,0:T(8,128)S(1)}, f32[1280,512]{1,0:T(8,128)}, u32[]{:S(2)}) %copy-start.6) | copy-done | bytes 2621464
  28.4 1.2 %copy-done.9 = bf16[512,1024]{1,0:T(8,128)(2,1)S(1)} copy-done((bf16[512,1024]{1,0:T(8,128)(2,1)S(1)}, bf16[512,1024]{1,0:T(8,128)(2,1)}, u32[]{:S(2)}) %copy-start.9) | copy-done | bytes 1048600
  29.7 1.2 %copy-done.11 = bf16[512,1024]{1,0:T(8,128)(2,1)S(1)} copy-done((bf16[512,1024]{1,0:T(8,128)(2,1)S(1)}, bf16[512,1024]{1,0:T(8,128)(2,1)}, u32[]{:S(2)}) %copy-start.11) | copy-done | bytes 1048600
  30.9 1.8 %prev_grads.2 = (bf16[512,256]{1,0:T(8,128)(2,1)S(1)}, f32[4,8,512]{2,1,0:T(8,128)S(1)}, s32[1,512]{1,0:T(1,128)S(1)}, f32[4,128,512]{2,1,0:T(8,128)S(1)}, s32[1]{0:T(128)}) custom-call(s32[1]{0:T(128)} %bitcast.first_ref, s32[1,32]{1,0:T(1,128)S(1)} %add.35.len_ref, bf16[512,1024]{1,0:T(8,128)(2,1)S(1)} %copy-done.9, bf16[512,1024]{1,0:T(8,128)(2,1)S(1)} %copy-done.11, ...), custom_call_target="tpu_custom_call" | custom-call | tf_op jit(solution)/shard_map/prev_grads/pallas_call | solution.py:300
  32.7 5.0 %collective-permute-start.10 = (bf16[512,256]{1,0:T(8,128)(2,1)S(1)}, bf16[512,256]{1,0:T(8,128)(2,1)S(1)}, u32[]{:S(2)}, u32[]{:S(2)}) collective-permute-start(bf16[512,256]{1,0:T(8,128)(2,1)S(1)} %get-tuple-element.42), channel_id=1, source_target_pairs={{0,28},{4,0},{8,4},{12,8},{16,12},{20,16},{24,20},{28,24},{1,29},{... | collective-permute-start | bytes 786440 | tf_op jit(solution)/shard_map/ppermute | solution.py:25
  37.7 2.0 %prev_grads.3 = (bf16[512,256]{1,0:T(8,128)(2,1)S(1)}, f32[4,8,512]{2,1,0:T(8,128)S(1)}, s32[1,512]{1,0:T(1,128)}, f32[4,128,512]{2,1,0:T(8,128)S(1)}, s32[1]{0:T(128)}) custom-call(s32[1]{0:T(128)} %bitcast.first_ref, s32[1,32]{1,0:T(1,128)S(1)} %add.35.len_ref, bf16[512,1024]{1,0:T(8,128)(2,1)S(1)} %copy-done.9, bf16[512,1024]{1,0:T(8,128)(2,1)S(1)} %copy-done.11, ...), custom_call_target="tpu_custom_call" | custom-call | tf_op jit(solution)/shard_map/prev_grads/pallas_call | solution.py:300
  39.7 1.3 %collective-permute-start.9 = (bf16[512,256]{1,0:T(8,128)(2,1)S(1)}, bf16[512,256]{1,0:T(8,128)(2,1)S(1)}, u32[]{:S(2)}, u32[]{:S(2)}) collective-permute-start(bf16[512,256]{1,0:T(8,128)(2,1)S(1)} %get-tuple-element.41), channel_id=1, source_target_pairs={{0,28},{4,0},{8,4},{12,8},{16,12},{20,16},{24,20},{28,24},{1,29},{... | collective-permute-start | bytes 786440 | tf_op jit(solution)/shard_map/ppermute | solution.py:25
  41.0 3.9 %own_grads.1 = (bf16[512,1024]{1,0:T(8,128)(2,1)}, f32[512,256]{1,0:T(8,128)S(1)}, f32[512,256]{1,0:T(8,128)S(1)}) custom-call(s32[1]{0:T(128)} %get-tuple-element.29.refs_0_, bf16[512,1024]{1,0:T(8,128)(2,1)S(1)} %copy-done.9, bf16[512,1024]{1,0:T(8,128)(2,1)S(1)} %copy-done.11, bf16[512,256]{1,0:T(8,128)(2,1)S(1)} %get-tuple-element.30.refs_3_, ...), custom_call_target="tpu_custom_call" | custom-call | tf_op jit(solution)/shard_map/own_grads/pallas_call | solution.py:317
  44.9 4.3 %collective-permute-done.9.refs_2_ = bf16[512,256]{1,0:T(8,128)(2,1)S(1)} collective-permute-done((bf16[512,256]{1,0:T(8,128)(2,1)S(1)}, bf16[512,256]{1,0:T(8,128)(2,1)S(1)}, u32[]{:S(2)}, u32[]{:S(2)}) %collective-permute-start.9) | collective-permute-done | bytes 262176 | tf_op jit(solution)/shard_map/ppermute | solution.py:25
  49.2 0.9 %sums.1 = (bf16[512,256]{1,0:T(8,128)(2,1)}, bf16[512,256]{1,0:T(8,128)(2,1)}) custom-call(f32[512,256]{1,0:T(8,128)S(1)} %get-tuple-element.39.refs_0_, f32[512,256]{1,0:T(8,128)S(1)} %get-tuple-element.40.refs_1_, bf16[512,256]{1,0:T(8,128)(2,1)S(1)} %collective-permute-done.9.refs_2_, bf16[512,256]{1,0:T(8,128)(2,1)S(1)} %collective-permute-done.10.refs_3_), custom_call_target="tpu_custom_call" | custom-call | tf_op jit(solution)/shard_map/sums/pallas_call | solution.py:329
  (31 shorter events, 0.2 us)
Async XLA Ops:
  1.3 8.0 %collective-permute-start.1 = (s32[1,32]{1,0:T(1,128)S(1)}, s32[1,32]{1,0:T(1,128)S(1)}, u32[]{:S(2)}, u32[]{:S(2)}) collective-permute-start(s32[1,32]{1,0:T(1,128)S(1)} %compare_select_fusion), channel_id=1, source_target_pairs={{0,4},{1,5},{2,6},{3,7},{4,0},{5,1},{6,2},{7,3},{8,12},{9,13},{10,... | collective-permute-start | bytes 392 | tf_op jit(solution)/shard_map/ppermute | solution.py:37
  4.3 5.0 %collective-permute-start.2 = (s32[1,32]{1,0:T(1,128)S(1)}, s32[1,32]{1,0:T(1,128)S(1)}, u32[]{:S(2)}, u32[]{:S(2)}) collective-permute-start(s32[1,32]{1,0:T(1,128)S(1)} %compare_select_fusion), channel_id=1, source_target_pairs={{0,6},{1,7},{2,4},{3,5},{4,2},{5,3},{6,0},{7,1},{8,14},{9,15},{10,... | collective-permute-start | bytes 392 | tf_op jit(solution)/shard_map/ppermute | solution.py:37
  5.8 3.6 %collective-permute-start = (s32[1,32]{1,0:T(1,128)S(1)}, s32[1,32]{1,0:T(1,128)S(1)}, u32[]{:S(2)}, u32[]{:S(2)}) collective-permute-start(s32[1,32]{1,0:T(1,128)S(1)} %compare_select_fusion), channel_id=1, source_target_pairs={{0,2},{1,3},{2,0},{3,1},{4,6},{5,7},{6,4},{7,5},{8,10},{9,11},{10,... | collective-permute-start | bytes 392 | tf_op jit(solution)/shard_map/ppermute | solution.py:37
  5.8 19.1 %collective-permute-start.7 = (bf16[512,256]{1,0:T(8,128)(2,1)}, bf16[512,256]{1,0:T(8,128)(2,1)S(1)}, u32[]{:S(2)}, u32[]{:S(2)}) collective-permute-start(bf16[512,256]{1,0:T(8,128)(2,1)} %k_hbm.1), channel_id=1, source_target_pairs={{0,4},{4,8},{8,12},{12,16},{16,20},{20,24},{24,28},{28,0},{1,5},{5... | collective-permute-start | bytes 786440 | tf_op jit(solution)/shard_map/ppermute | solution.py:25
  7.8 17.2 %collective-permute-start.8 = (bf16[512,256]{1,0:T(8,128)(2,1)}, bf16[512,256]{1,0:T(8,128)(2,1)S(1)}, u32[]{:S(2)}, u32[]{:S(2)}) collective-permute-start(bf16[512,256]{1,0:T(8,128)(2,1)} %v_hbm.1), channel_id=1, source_target_pairs={{0,4},{4,8},{8,12},{12,16},{16,20},{20,24},{24,28},{28,0},{1,5},{5... | collective-permute-start | bytes 786440 | tf_op jit(solution)/shard_map/ppermute | solution.py:25
  9.4 14.4 %collective-permute-start.5 = (s32[1,32]{1,0:T(1,128)S(1)}, s32[1,32]{1,0:T(1,128)S(1)}, u32[]{:S(2)}, u32[]{:S(2)}) collective-permute-start(s32[1,32]{1,0:T(1,128)S(1)} %add_add_fusion.1.after_ref), channel_id=1, source_target_pairs={{0,24},{1,25},{2,26},{3,27},{4,28},{5,29},{6,30},{7,31},{8,16},{9,... | collective-permute-start | bytes 392 | tf_op jit(solution)/shard_map/ppermute | solution.py:37
  12.9 10.8 %collective-permute-start.4 = (s32[1,32]{1,0:T(1,128)S(1)}, s32[1,32]{1,0:T(1,128)S(1)}, u32[]{:S(2)}, u32[]{:S(2)}) collective-permute-start(s32[1,32]{1,0:T(1,128)S(1)} %add_add_fusion.1.after_ref), channel_id=1, source_target_pairs={{0,16},{1,17},{2,18},{3,19},{4,20},{5,21},{6,22},{7,23},{8,24},{9,... | collective-permute-start | bytes 392 | tf_op jit(solution)/shard_map/ppermute | solution.py:37
  12.9 10.8 %collective-permute-start.3 = (s32[1,32]{1,0:T(1,128)S(1)}, s32[1,32]{1,0:T(1,128)S(1)}, u32[]{:S(2)}, u32[]{:S(2)}) collective-permute-start(s32[1,32]{1,0:T(1,128)S(1)} %add_add_fusion.1.after_ref), channel_id=1, source_target_pairs={{0,8},{1,9},{2,10},{3,11},{4,12},{5,13},{6,14},{7,15},{8,0},{9,1},... | collective-permute-start | bytes 392 | tf_op jit(solution)/shard_map/ppermute | solution.py:37
  17.1 1.5 %copy-start = (f32[1280,512]{1,0:T(8,128)}, f32[1280,512]{1,0:T(8,128)S(1)}, u32[]{:S(2)}) copy-start(f32[1280,512]{1,0:T(8,128)S(1)} %get-tuple-element.33.d_ref.refs_6_) | copy-start | bytes 7864324
  18.6 1.5 %copy-start.2 = (f32[1280,512]{1,0:T(8,128)}, f32[1280,512]{1,0:T(8,128)S(1)}, u32[]{:S(2)}) copy-start(f32[1280,512]{1,0:T(8,128)S(1)} %get-tuple-element.27.s_ref.refs_9_) | copy-start | bytes 7864324
  20.1 1.6 %copy-start.5 = (f32[1280,512]{1,0:T(8,128)}, f32[1280,512]{1,0:T(8,128)S(1)}, u32[]{:S(2)}) copy-start(f32[1280,512]{1,0:T(8,128)S(1)} %get-tuple-element.28.d_ref.refs_10_) | copy-start | bytes 7864324
  21.7 1.0 %copy-start.8 = (bf16[512,1024]{1,0:T(8,128)(2,1)}, bf16[512,1024]{1,0:T(8,128)(2,1)S(1)}, u32[]{:S(2)}) copy-start(bf16[512,1024]{1,0:T(8,128)(2,1)S(1)} %get-tuple-element.25.q_ref.refs_1_) | copy-start | bytes 3145732
  22.7 1.1 %copy-start.10 = (bf16[512,1024]{1,0:T(8,128)(2,1)}, bf16[512,1024]{1,0:T(8,128)(2,1)S(1)}, u32[]{:S(2)}) copy-start(bf16[512,1024]{1,0:T(8,128)(2,1)S(1)} %get-tuple-element.26.g_ref.refs_2_) | copy-start | bytes 3145732
  23.8 1.2 %collective-permute-start.6 = (s32[1,32]{1,0:T(1,128)S(1)}, s32[1,32]{1,0:T(1,128)S(1)}, u32[]{:S(2)}, u32[]{:S(2)}) collective-permute-start(s32[1,32]{1,0:T(1,128)S(1)} %add_add_fusion), channel_id=1, source_target_pairs={{0,1},{1,0},{2,3},{3,2},{4,5},{5,4},{6,7},{7,6},{8,9},{9,8},{10,11... | collective-permute-start | bytes 392 | tf_op jit(solution)/shard_map/ppermute | solution.py:37
  25.0 1.7 %copy-start.3 = (f32[1280,512]{1,0:T(8,128)S(1)}, f32[1280,512]{1,0:T(8,128)}, u32[]{:S(2)}) copy-start(f32[1280,512]{1,0:T(8,128)} %copy-done.2) | copy-start | bytes 7864324
  26.7 1.7 %copy-start.6 = (f32[1280,512]{1,0:T(8,128)S(1)}, f32[1280,512]{1,0:T(8,128)}, u32[]{:S(2)}) copy-start(f32[1280,512]{1,0:T(8,128)} %copy-done.5) | copy-start | bytes 7864324
  28.4 1.2 %copy-start.9 = (bf16[512,1024]{1,0:T(8,128)(2,1)S(1)}, bf16[512,1024]{1,0:T(8,128)(2,1)}, u32[]{:S(2)}) copy-start(bf16[512,1024]{1,0:T(8,128)(2,1)} %copy-done.8) | copy-start | bytes 3145732
  29.7 1.2 %copy-start.11 = (bf16[512,1024]{1,0:T(8,128)(2,1)S(1)}, bf16[512,1024]{1,0:T(8,128)(2,1)}, u32[]{:S(2)}) copy-start(bf16[512,1024]{1,0:T(8,128)(2,1)} %copy-done.10) | copy-start | bytes 3145732
  30.9 6.8 %copy-start.1 = (f32[1280,512]{1,0:T(8,128)S(1)}, f32[1280,512]{1,0:T(8,128)}, u32[]{:S(2)}) copy-start(f32[1280,512]{1,0:T(8,128)} %copy-done) | copy-start | bytes 7864324
  32.7 12.2 %collective-permute-start.10 = (bf16[512,256]{1,0:T(8,128)(2,1)S(1)}, bf16[512,256]{1,0:T(8,128)(2,1)S(1)}, u32[]{:S(2)}, u32[]{:S(2)}) collective-permute-start(bf16[512,256]{1,0:T(8,128)(2,1)S(1)} %get-tuple-element.42), channel_id=1, source_target_pairs={{0,28},{4,0},{8,4},{12,8},{16,12},{20,16},{24,20},{28,24},{1,29},{... | collective-permute-start | bytes 786440 | tf_op jit(solution)/shard_map/ppermute | solution.py:25
  37.7 3.3 %copy-start.4 = (f32[1280,512]{1,0:T(8,128)S(1)}, f32[1280,512]{1,0:T(8,128)}, u32[]{:S(2)}) copy-start(f32[1280,512]{1,0:T(8,128)} %copy-done.2) | copy-start | bytes 7864324
  37.7 3.3 %copy-start.7 = (f32[1280,512]{1,0:T(8,128)S(1)}, f32[1280,512]{1,0:T(8,128)}, u32[]{:S(2)}) copy-start(f32[1280,512]{1,0:T(8,128)} %copy-done.5) | copy-start | bytes 7864324
  39.7 9.6 %collective-permute-start.9 = (bf16[512,256]{1,0:T(8,128)(2,1)S(1)}, bf16[512,256]{1,0:T(8,128)(2,1)S(1)}, u32[]{:S(2)}, u32[]{:S(2)}) collective-permute-start(bf16[512,256]{1,0:T(8,128)(2,1)S(1)} %get-tuple-element.41), channel_id=1, source_target_pairs={{0,28},{4,0},{8,4},{12,8},{16,12},{20,16},{24,20},{28,24},{1,29},{... | collective-permute-start | bytes 786440 | tf_op jit(solution)/shard_map/ppermute | solution.py:25

commit v5 on v3

--- a/solution.py
+++ b/solution.py
@@ -25,10 +25,12 @@
     return lax.ppermute(value, axis, [(s, (s + steps) % count) for s in range(count)])
 
 
-def round_groups(axes):
-    count = lax.axis_size(axes)
-    bits = [1 << b for b in range(1, count.bit_length() - 1)]
-    return [bits[n : n + 2] for n in range(0, len(bits), 2)] + [[1]]
+def round_groups():
+    low = lax.axis_size("head")
+    count = low * lax.axis_size("seq")
+    bits = [1 << b for b in range(count.bit_length() - 1)]
+    head, seq = [b for b in bits if b < low], [b for b in bits if b > low]
+    return [[low]] + [part[n : n + 2] for part in (head, seq) for n in range(0, len(part), 2)]
 
 
 def summed_round(value, axes, group):
@@ -82,74 +84,56 @@
     )
 
 
-def own_span(i):
-    return slice(i * (i + 1) // 2 * BLOCK, (i + 1) * (i + 2) // 2 * BLOCK)
-
-
-def own_scores(s_ref, start_ref, i):
-    at = slice(i * BLOCK, (i + 1) * BLOCK)
-    query = i * BLOCK + lax.broadcasted_iota(jnp.int32, (1, BLOCK), 1)
-    return masked(s_ref[own_span(i), :], start_ref[:, at], 0, query)
-
-
 def column(g):
     return slice(g * HEAD_WIDTH, (g + 1) * HEAD_WIDTH)
 
 
-def raw_kernel(after_ref, q_hbm, g_hbm, k_hbm, v_hbm, zero_ref, q_ref, g_ref, k_ref, v_ref, *outs):
-    outs, sems = outs[:-1], outs[-1]
+def own_block(i, g, heads, q_ref, g_ref, k_ref, v_ref, start_ref):
+    at, seen = slice(i * BLOCK, (i + 1) * BLOCK), slice(0, (i + 1) * BLOCK)
+    query_rows, grad_rows = stacked(q_ref, i, g, heads), stacked(g_ref, i, g, heads)
+    query = i * BLOCK + lax.broadcasted_iota(jnp.int32, (1, BLOCK), 1)
+    scores = dot(k_ref[seen, column(g)], query_rows, NT) * (SCALE * LOG2E)
+    scores = masked(scores, start_ref[:, at], 0, query)
+    return query_rows, grad_rows, scores, dot(v_ref[seen, column(g)], grad_rows, NT)
+
+
+def fetch_kernel(count, *refs):
+    sources, targets, sems = refs[:count], refs[count : 2 * count], refs[2 * count]
+    half = sources[0].shape[0] // 2
+    copies = []
+    for source, target in zip(sources, targets):
+        for at in (pl.ds(0, half), pl.ds(half, half)):
+            copies.append(
+                pltpu.make_async_copy(source.at[at], target.at[at], sems.at[len(copies)])
+            )
+            copies[-1].start()
+    for copy in copies:
+        copy.wait()
+
+
+def prev_kernel(g, first_ref, len_ref, pk_ref, pv_ref, *refs):
+    q_ref, g_ref, k_ref, v_ref = refs[:4]
+    if g == 0:
+        send_ref, stat_ref, dq_ref, reach_ref, start_ref = refs[4:]
+    else:
+        start_ref, send_ref, stat_ref, dq_ref = refs[4:]
     rows, width = q_ref.shape
-    kv_heads = k_ref.shape[1] // HEAD_WIDTH
     heads = width // k_ref.shape[1]
     blocks = rows // BLOCK
-
-    def fetch(n, source, target, at):
-        copy = pltpu.make_async_copy(source.at[at], target.at[at], sems.at[n])
-        copy.start()
-        return copy
-
-    zero_ref[...] = jnp.zeros(zero_ref.shape, jnp.int32)
-    whole = pl.ds(0, rows)
-    first = [fetch(0, k_hbm, k_ref, whole), fetch(1, v_hbm, v_ref, whole)]
-    parts = [
-        [
-            fetch(2 + 2 * i, q_hbm, q_ref, pl.ds(i * BLOCK, BLOCK)),
-            fetch(3 + 2 * i, g_hbm, g_ref, pl.ds(i * BLOCK, BLOCK)),
-        ]
-        for i in range(blocks)
-    ]
-    for copy in first:
-        copy.wait()
-    for i in range(blocks):
-        for copy in parts[i]:
-            copy.wait()
-        seen = slice(0, (i + 1) * BLOCK)
-        for g in range(kv_heads):
-            s_ref, d_ref = outs[2 * g : 2 * g + 2]
-            scores = dot(k_ref[seen, column(g)], stacked(q_ref, i, g, heads), NT)
-            s_ref[own_span(i), :] = scores * (SCALE * LOG2E)
-            d_ref[own_span(i), :] = dot(v_ref[seen, column(g)], stacked(g_ref, i, g, heads), NT)
-
-
-def prev_kernel(
-    g, first_ref, len_ref, q_ref, g_ref, pk_ref, pv_ref, s_ref, d_ref,
-    send_ref, stat_ref, start_ref, dq_ref, reach_ref,
-):
-    rows, width = q_ref.shape
-    heads = width // pk_ref.shape[1]
-    blocks = rows // BLOCK
-    start = start_row(len_ref[...], first_ref[0], rows)
-    start_ref[...] = start
+    if g == 0:
+        start_ref[...] = start_row(len_ref[...], first_ref[0], rows)
+    start = start_ref[...]
     before = pl.cdiv(jnp.maximum(-jnp.min(start), 0), BLOCK)
     after = pl.cdiv(jnp.sum((start < 0).astype(jnp.int32)), BLOCK)
-    reach_ref[0] = after
+    if g == 0:
+        reach_ref[0] = after
     for i in range(blocks):
-        own = own_scores(s_ref, start_ref, i)
+        _, _, own, down = own_block(i, g, heads, q_ref, g_ref, k_ref, v_ref, start_ref)
         top = jnp.max(own, axis=0, keepdims=True)
         own = jnp.exp2(own - top)
         stat_ref[i, 0:1, :] = top
         stat_ref[i, 1:2, :] = jnp.sum(own, axis=0, keepdims=True)
-        stat_ref[i, 2:3, :] = jnp.sum(own * d_ref[own_span(i), :], axis=0, keepdims=True)
+        stat_ref[i, 2:3, :] = jnp.sum(own * down, axis=0, keepdims=True)
 
     def crossing(keys, queries):
         seen = slice((blocks - keys) * BLOCK, rows)
@@ -198,9 +182,9 @@
 
 
 def own_kernel(kv_heads, *refs):
-    reach_ref, q_ref, g_ref, k_ref, start_ref = refs[:5]
-    per_head = [refs[5 + 4 * g : 9 + 4 * g] for g in range(kv_heads)]
-    refs = refs[5 + 4 * kv_heads :]
+    reach_ref, q_ref, g_ref, k_ref, v_ref, start_ref = refs[:6]
+    per_head = [refs[6 + 2 * g : 8 + 2 * g] for g in range(kv_heads)]
+    refs = refs[6 + 2 * kv_heads :]
     dq_hbm, keeps, (dq_ref, dk_ref, dv_ref, sems) = refs[0], refs[1 : 1 + kv_heads], refs[1 + kv_heads :]
     rows, width = q_ref.shape
     heads = width // k_ref.shape[1]
@@ -208,15 +192,16 @@
     reach = reach_ref[0]
     copies = []
     for g in range(kv_heads):
-        s_ref, d_ref, stat_ref, dqp_ref = per_head[g]
+        stat_ref, dqp_ref = per_head[g]
         for i in reversed(range(blocks)):
-            query_rows = stacked(q_ref, i, g, heads)
-            grad_rows = stacked(g_ref, i, g, heads)
             seen = slice(0, (i + 1) * BLOCK)
+            query_rows, grad_rows, own, down = own_block(
+                i, g, heads, q_ref, g_ref, k_ref, v_ref, start_ref
+            )
             top, total, dsum = (stat_ref[i, n : n + 1, :] for n in range(3))
             inverse = 1.0 / total
-            own = jnp.exp2(own_scores(s_ref, start_ref, i) - top) * inverse
-            down = (own * (d_ref[own_span(i), :] - dsum * inverse)).astype(jnp.bfloat16)
+            own = jnp.exp2(own - top) * inverse
+            down = (own * (down - dsum * inverse)).astype(jnp.bfloat16)
             dv = dot(own.astype(jnp.bfloat16), grad_rows, NN)
             dk = dot(down, query_rows, NN)
             if i == blocks - 1:
@@ -260,13 +245,13 @@
     kv_heads = keys.shape[1] // HEAD_WIDTH
     heads = queries.shape[1] // keys.shape[1]
     blocks = rows // BLOCK
-    pairs = blocks * (blocks + 1) // 2 * BLOCK
     lanes = heads * BLOCK
+    axes = ("seq", "head")
     prev_keys = rotated(keys, "seq", 1)
     prev_values = rotated(values, "seq", 1)
-    axes = ("seq", "head")
-    groups = round_groups(axes)
-    row = summed_round(lengths_row(doc_lengths, axes), axes, groups[0])
+    row = lengths_row(doc_lengths, axes)
+    for group in round_groups():
+        row = summed_round(row, axes, group)
     first = (lax.axis_index("seq") * rows).astype(jnp.int32).reshape(1)
     params = pltpu.CompilerParams(vmem_limit_bytes=24 * 1024 * 1024)
     shape = jax.ShapeDtypeStruct
@@ -274,55 +259,55 @@
     smem = pl.BlockSpec(memory_space=pltpu.SMEM)
     hbm = pl.BlockSpec(memory_space=pltpu.HBM)
     pair = shape((rows, 2 * HEAD_WIDTH), jnp.bfloat16)
-    scratch = [pltpu.VMEM((rows, HEAD_WIDTH), jnp.float32)] * 2
-
+    per_head = [
+        pair,
+        shape((blocks, 8, lanes), jnp.float32),
+        shape((blocks, HEAD_WIDTH, lanes), jnp.float32),
+    ]
     arrays = (queries, output_gradient, keys, values)
-    zero, q, g_out, k, v, *raw = pl.pallas_call(
-        raw_kernel,
-        out_shape=[shape(row.shape, jnp.int32)]
-        + [pltpu.VMEM(a.shape, a.dtype) for a in arrays]
-        + [pltpu.VMEM((pairs, lanes), jnp.float32)] * (2 * kv_heads),
-        in_specs=[hbm] * 5,
-        out_specs=[vmem] * (5 + 2 * kv_heads),
-        scratch_shapes=[pltpu.SemaphoreType.DMA((2 + 2 * blocks,))],
+    fetched = pl.pallas_call(
+        functools.partial(fetch_kernel, len(arrays)),
+        out_shape=[shape(a.shape, a.dtype) for a in arrays],
+        in_specs=[hbm] * len(arrays),
+        out_specs=[vmem] * len(arrays),
+        scratch_shapes=[pltpu.SemaphoreType.DMA((2 * len(arrays),))],
         compiler_params=params,
-        name="own_products",
-    )(row, *(pltpu.with_memory_space_constraint(a, pltpu.HBM) for a in arrays))
-    for n, group in enumerate(groups[1:]):
-        if n == len(groups) - 2:
-            row = row + zero
-        row = summed_round(row, axes, group)
-    sends, per_head = [], []
-    for g in range(kv_heads):
-        send, stat, start, dq, reach = pl.pallas_call(
+        name="fetch",
+    )(*(pltpu.with_memory_space_constraint(a, pltpu.HBM) for a in arrays))
+    send, stat, dq, reach, start = pl.pallas_call(
+        functools.partial(prev_kernel, 0),
+        out_shape=per_head
+        + [shape((1,), jnp.int32), shape((1, rows), jnp.int32)],
+        in_specs=[smem] + [vmem] * 7,
+        out_specs=[vmem] * 3 + [smem, vmem],
+        compiler_params=params,
+        name="prev_grads",
+    )(first, row, prev_keys, prev_values, *fetched)
+    sends, stats = [send], [stat, dq]
+    for g in range(1, kv_heads):
+        send, stat, dq = pl.pallas_call(
             functools.partial(prev_kernel, g),
-            out_shape=(
-                pair,
-                shape((blocks, 8, lanes), jnp.float32),
-                shape((1, rows), jnp.int32),
-                shape((blocks, HEAD_WIDTH, lanes), jnp.float32),
-                shape((1,), jnp.int32),
-            ),
-            in_specs=[smem] + [vmem] * 7,
-            out_specs=[vmem] * 4 + [smem],
+            out_shape=per_head,
+            in_specs=[smem] + [vmem] * 8,
+            out_specs=[vmem] * 3,
             compiler_params=params,
             name="prev_grads",
-        )(first, row, q, g_out, prev_keys, prev_values, raw[2 * g], raw[2 * g + 1])
+        )(first, row, prev_keys, prev_values, *fetched, start)
         sends.append(send)
-        per_head += [raw[2 * g], raw[2 * g + 1], stat, dq]
+        stats += [stat, dq]
     backs = [rotated(send, "seq", -1) for send in sends]
     grad_queries, *keeps = pl.pallas_call(
         functools.partial(own_kernel, kv_heads),
         out_shape=[shape(queries.shape, jnp.bfloat16)]
         + [shape(pair.shape, jnp.float32)] * kv_heads,
-        in_specs=[smem] + [vmem] * (4 + 4 * kv_heads),
+        in_specs=[smem] + [vmem] * (5 + 2 * kv_heads),
         out_specs=[hbm] + [vmem] * kv_heads,
         scratch_shapes=[pltpu.VMEM(queries.shape, jnp.bfloat16)]
-        + scratch
+        + [pltpu.VMEM((rows, HEAD_WIDTH), jnp.float32)] * 2
         + [pltpu.SemaphoreType.DMA((kv_heads * blocks,))],
         compiler_params=params,
         name="own_grads",
-    )(reach, q, g_out, k, start, *per_head)
+    )(reach, *fetched, start, *stats)
     key_gradient, value_gradient = pl.pallas_call(
         functools.partial(sum_kernel, kv_heads),
         out_shape=[shape(keys.shape, jnp.bfloat16)] * 2,

time: 51.1 us -> 36.4 us (0.71)
  local copies, waits for them, and re-layouts: 12.5 us -> 0 us
  starting transfers between devices: 18.7 us -> 17.2 us
  Pallas kernels: 12.2 us -> 10.9 us
  waiting for transfers between devices: 5.68 us -> 6.49 us
    unnamed x24 -> x0, local copies, waits for them, and re-layouts: 12.5 us -> none
    ppermute x7, waiting for transfers between devices: 1.12 us -> 4.11 us  [summed_round(): lax.ppermute(value, axes, [(s, s ^ m) for s in range(count)])]
    pallas_call x3, Pallas kernels: 7.41 us -> 4.67 us  [the longest x1 1.72 us: body(): pl.pallas_call(functools.partial(prev_kernel, 0), out_shape=per_head + [s...]
    ppermute x4, waiting for transfers between devices: 4.57 us -> 2.38 us  [rotated(): lax.ppermute(value, axis, [(s, (s + steps) % count) for s in range(count)])]
    ppermute x4, starting transfers between devices: 9.6 us -> 7.79 us  [rotated(): lax.ppermute(value, axis, [(s, (s + steps) % count) for s in range(count)])]
    pallas_call x1, Pallas kernels: 3.87 us -> 5.28 us  [body(): pl.pallas_call(functools.partial(own_kernel, kv_heads), out_shape=[shape(...]
  transfers between devices with their start and end apart: 11 -> 11, of which waited for: 2 -> 6; matrix products, arithmetic and copies ran while one was open for 0% -> 0% of each run, Pallas kernels for 19% -> 23%
where the time goes in v5:
time: 36.4 us; the launch traced here: 35.9 us
  starting transfers between devices  17.2 us (47%)
  Pallas kernels  10.9 us (30%)
  waiting for transfers between devices  6.49 us (18%)
  between operations  1.37 us (4%)
    ppermute x7, starting transfers between devices, summed_round(): lax.ppermute(value, axes, [(s, s ^ m) for s in range(count)])  9.4 us
    ppermute x4, starting transfers between devices, rotated(): lax.ppermute(value, axis, [(s, (s + steps) % count) for s in range(count)])  7.79 us
    pallas_call x1, Pallas kernels, body(): pl.pallas_call(functools.partial(own_kernel, kv_heads), out_shape=[shape(...  5.28 us
    ppermute x7, waiting for transfers between devices, summed_round(): lax.ppermute(value, axes, [(s, s ^ m) for s in range(count)])  4.11 us
    ppermute x4, waiting for transfers between devices, rotated(): lax.ppermute(value, axis, [(s, (s + steps) % count) for s in range(count)])  2.38 us
    pallas_call x1, Pallas kernels, body(): pl.pallas_call(functools.partial(prev_kernel, 0), out_shape=per_head + [s...  1.72 us
    pallas_call x1, Pallas kernels, body(): pl.pallas_call(functools.partial(fetch_kernel, len(arrays)), out_shape=[s...  1.72 us
    pallas_call x1, Pallas kernels, body(): pl.pallas_call(functools.partial(prev_kernel, g), out_shape=per_head, in_...  1.23 us
  transfers between devices with their start and end apart: 11, of which 6 were waited for; matrix products, arithmetic and copies ran while one was open for 0% of the time, Pallas kernels for 23%

profile of v5, /device:TPU:0, one launch (start us, length us, event | category | flops | bytes accessed | tf_op | source)
XLA Modules:
  0.0 35.9 jit_solution(12738346613530457143)
XLA Ops:
  1.3 3.0 %collective-permute-start = (s32[1,32]{1,0:T(1,128)S(1)}, s32[1,32]{1,0:T(1,128)S(1)}, u32[]{:S(2)}, u32[]{:S(2)}) collective-permute-start(s32[1,32]{1,0:T(1,128)S(1)} %compare_select_fusion), channel_id=1, source_target_pairs={{0,4},{1,5},{2,6},{3,7},{4,0},{5,1},{6,2},{7,3},{8,12},{9,13},{10,... | collective-permute-start | bytes 392 | tf_op jit(solution)/shard_map/ppermute | solution.py:39
  4.3 0.1 collective-permute-start.7
  4.4 3.0 %collective-permute-start.8 = (bf16[512,256]{1,0:T(8,128)(2,1)}, bf16[512,256]{1,0:T(8,128)(2,1)S(1)}, u32[]{:S(2)}, u32[]{:S(2)}) collective-permute-start(bf16[512,256]{1,0:T(8,128)(2,1)} %refs_3_.1), channel_id=1, source_target_pairs={{0,4},{4,8},{8,12},{12,16},{16,20},{20,24},{24,28},{28,0},{1,5},{5... | collective-permute-start | bytes 786440 | tf_op jit(solution)/shard_map/ppermute | solution.py:25
  7.3 1.7 %fetch.1 = (bf16[512,1024]{1,0:T(8,128)(2,1)S(1)}, bf16[512,1024]{1,0:T(8,128)(2,1)S(1)}, bf16[512,256]{1,0:T(8,128)(2,1)S(1)}, bf16[512,256]{1,0:T(8,128)(2,1)S(1)}) custom-call(bf16[512,1024]{1,0:T(8,128)(2,1)} %refs_0_.1, bf16[512,1024]{1,0:T(8,128)(2,1)} %refs_1_.1, bf16[512,256]{1,0:T(8,128)(2,1)} %refs_2_.1, bf16[512,256]{1,0:T(8,128)(2,1)} %refs_3_.1), custom_call_target="tpu_custom_call" | custom-call | tf_op jit(solution)/shard_map/fetch/pallas_call | solution.py:268
  9.1 0.0 collective-permute-done
  9.1 0.2 collective-permute-start.3
  9.3 1.5 %collective-permute-start.2 = (s32[1,32]{1,0:T(1,128)S(1)}, s32[1,32]{1,0:T(1,128)S(1)}, u32[]{:S(2)}, u32[]{:S(2)}) collective-permute-start(s32[1,32]{1,0:T(1,128)S(1)} %fusion), channel_id=1, source_target_pairs={{0,2},{1,3},{2,0},{3,1},{4,6},{5,7},{6,4},{7,5},{8,10},{9,11},{10,... | collective-permute-start | bytes 392 | tf_op jit(solution)/shard_map/ppermute | solution.py:39
  10.8 0.3 collective-permute-start.1
  11.0 1.1 %collective-permute-done.3 = s32[1,32]{1,0:T(1,128)S(1)} collective-permute-done((s32[1,32]{1,0:T(1,128)S(1)}, s32[1,32]{1,0:T(1,128)S(1)}, u32[]{:S(2)}, u32[]{:S(2)}) %collective-permute-start.3) | collective-permute-done | bytes 160 | tf_op jit(solution)/shard_map/ppermute | solution.py:39
  12.1 0.7 %collective-permute-done.2 = s32[1,32]{1,0:T(1,128)S(1)} collective-permute-done((s32[1,32]{1,0:T(1,128)S(1)}, s32[1,32]{1,0:T(1,128)S(1)}, u32[]{:S(2)}, u32[]{:S(2)}) %collective-permute-start.2) | collective-permute-done | bytes 160 | tf_op jit(solution)/shard_map/ppermute | solution.py:39
  12.8 2.3 %collective-permute-start.6 = (s32[1,32]{1,0:T(1,128)S(1)}, s32[1,32]{1,0:T(1,128)S(1)}, u32[]{:S(2)}, u32[]{:S(2)}) collective-permute-start(s32[1,32]{1,0:T(1,128)S(1)} %add_add_fusion.1), channel_id=1, source_target_pairs={{0,24},{1,25},{2,26},{3,27},{4,28},{5,29},{6,30},{7,31},{8,16},{9,... | collective-permute-start | bytes 392 | tf_op jit(solution)/shard_map/ppermute | solution.py:39
  15.2 0.8 %collective-permute-start.5 = (s32[1,32]{1,0:T(1,128)S(1)}, s32[1,32]{1,0:T(1,128)S(1)}, u32[]{:S(2)}, u32[]{:S(2)}) collective-permute-start(s32[1,32]{1,0:T(1,128)S(1)} %add_add_fusion.1), channel_id=1, source_target_pairs={{0,16},{1,17},{2,18},{3,19},{4,20},{5,21},{6,22},{7,23},{8,24},{9,... | collective-permute-start | bytes 392 | tf_op jit(solution)/shard_map/ppermute | solution.py:39
  16.0 1.3 %collective-permute-start.4 = (s32[1,32]{1,0:T(1,128)S(1)}, s32[1,32]{1,0:T(1,128)S(1)}, u32[]{:S(2)}, u32[]{:S(2)}) collective-permute-start(s32[1,32]{1,0:T(1,128)S(1)} %add_add_fusion.1), channel_id=1, source_target_pairs={{0,8},{1,9},{2,10},{3,11},{4,12},{5,13},{6,14},{7,15},{8,0},{9,1},... | collective-permute-start | bytes 392 | tf_op jit(solution)/shard_map/ppermute | solution.py:39
  17.3 0.9 %collective-permute-done.6 = s32[1,32]{1,0:T(1,128)S(1)} collective-permute-done((s32[1,32]{1,0:T(1,128)S(1)}, s32[1,32]{1,0:T(1,128)S(1)}, u32[]{:S(2)}, u32[]{:S(2)}) %collective-permute-start.6) | collective-permute-done | bytes 160 | tf_op jit(solution)/shard_map/ppermute | solution.py:39
  18.2 1.4 %collective-permute-done.5 = s32[1,32]{1,0:T(1,128)S(1)} collective-permute-done((s32[1,32]{1,0:T(1,128)S(1)}, s32[1,32]{1,0:T(1,128)S(1)}, u32[]{:S(2)}, u32[]{:S(2)}) %collective-permute-start.5) | collective-permute-done | bytes 160 | tf_op jit(solution)/shard_map/ppermute | solution.py:39
  19.6 0.0 collective-permute-done.4
  19.6 1.0 %collective-permute-done.8.pv_ref = bf16[512,256]{1,0:T(8,128)(2,1)S(1)} collective-permute-done((bf16[512,256]{1,0:T(8,128)(2,1)}, bf16[512,256]{1,0:T(8,128)(2,1)S(1)}, u32[]{:S(2)}, u32[]{:S(2)}) %collective-permute-start.8) | collective-permute-done | bytes 262176 | tf_op jit(solution)/shard_map/ppermute | solution.py:25
  20.6 1.7 %prev_grads.2 = (bf16[512,256]{1,0:T(8,128)(2,1)S(1)}, f32[4,8,512]{2,1,0:T(8,128)S(1)}, f32[4,128,512]{2,1,0:T(8,128)S(1)}, s32[1]{0:T(128)}, s32[1,512]{1,0:T(1,128)S(1)}) custom-call(s32[1]{0:T(128)} %bitcast.first_ref, s32[1,32]{1,0:T(1,128)S(1)} %add_add_fusion.len_ref, bf16[512,256]{1,0:T(8,128)(2,1)S(1)} %collective-permute-done.7.pk_ref, ...), custom_call_target="tpu_custom_call" | custom-call | tf_op jit(solution)/shard_map/prev_grads/pallas_call | solution.py:277
  22.4 2.0 %collective-permute-start.9 = (bf16[512,256]{1,0:T(8,128)(2,1)S(1)}, bf16[512,256]{1,0:T(8,128)(2,1)S(1)}, u32[]{:S(2)}, u32[]{:S(2)}) collective-permute-start(bf16[512,256]{1,0:T(8,128)(2,1)S(1)} %get-tuple-element.33), channel_id=1, source_target_pairs={{0,28},{4,0},{8,4},{12,8},{16,12},{20,16},{24,20},{28,24},{1,29},{... | collective-permute-start | bytes 786440 | tf_op jit(solution)/shard_map/ppermute | solution.py:25
  24.4 1.2 %prev_grads.3 = (bf16[512,256]{1,0:T(8,128)(2,1)S(1)}, f32[4,8,512]{2,1,0:T(8,128)S(1)}, f32[4,128,512]{2,1,0:T(8,128)S(1)}) custom-call(s32[1]{0:T(128)} %bitcast.first_ref, s32[1,32]{1,0:T(1,128)S(1)} %add_add_fusion.len_ref, bf16[512,256]{1,0:T(8,128)(2,1)S(1)} %collective-permute-done.7.pk_ref, bf16[512,256]{1,0:T(8,128)(2,1)S(1)} %collective-permute-done.8.pv_ref, ...), custom_call_target="tpu_custom_call" | custom-call | tf_op jit(solution)/shard_map/prev_grads/pallas_call | solution.py:288
  25.6 2.7 %collective-permute-start.10 = (bf16[512,256]{1,0:T(8,128)(2,1)S(1)}, bf16[512,256]{1,0:T(8,128)(2,1)S(1)}, u32[]{:S(2)}, u32[]{:S(2)}) collective-permute-start(bf16[512,256]{1,0:T(8,128)(2,1)S(1)} %get-tuple-element.34), channel_id=1, source_target_pairs={{0,28},{4,0},{8,4},{12,8},{16,12},{20,16},{24,20},{28,24},{1,29},{... | collective-permute-start | bytes 786440 | tf_op jit(solution)/shard_map/ppermute | solution.py:25
  28.3 5.3 %own_grads.1 = (bf16[512,1024]{1,0:T(8,128)(2,1)}, f32[512,256]{1,0:T(8,128)S(1)}, f32[512,256]{1,0:T(8,128)S(1)}) custom-call(s32[1]{0:T(128)} %get-tuple-element.24.refs_0_, bf16[512,1024]{1,0:T(8,128)(2,1)S(1)} %get-tuple-element.20.refs_0_.refs_1_, bf16[512,1024]{1,0:T(8,128)(2,1)S(1)} %get-tuple-element.21.refs_1_.refs_2_, ...), custom_call_target="tpu_custom_call" | custom-call | tf_op jit(solution)/shard_map/own_grads/pallas_call | solution.py:299
  33.6 1.4 %collective-permute-done.10.refs_3_ = bf16[512,256]{1,0:T(8,128)(2,1)S(1)} collective-permute-done((bf16[512,256]{1,0:T(8,128)(2,1)S(1)}, bf16[512,256]{1,0:T(8,128)(2,1)S(1)}, u32[]{:S(2)}, u32[]{:S(2)}) %collective-permute-start.10) | collective-permute-done | bytes 262176 | tf_op jit(solution)/shard_map/ppermute | solution.py:25
  35.0 0.9 %sums.1 = (bf16[512,256]{1,0:T(8,128)(2,1)}, bf16[512,256]{1,0:T(8,128)(2,1)}) custom-call(f32[512,256]{1,0:T(8,128)S(1)} %get-tuple-element.31.refs_0_, f32[512,256]{1,0:T(8,128)S(1)} %get-tuple-element.32.refs_1_, bf16[512,256]{1,0:T(8,128)(2,1)S(1)} %collective-permute-done.9.refs_2_, bf16[512,256]{1,0:T(8,128)(2,1)S(1)} %collective-permute-done.10.refs_3_), custom_call_target="tpu_custom_call" | custom-call | tf_op jit(solution)/shard_map/sums/pallas_call | solution.py:311
  (7 shorter events, 0.0 us)
Async XLA Ops:
  1.3 7.8 %collective-permute-start = (s32[1,32]{1,0:T(1,128)S(1)}, s32[1,32]{1,0:T(1,128)S(1)}, u32[]{:S(2)}, u32[]{:S(2)}) collective-permute-start(s32[1,32]{1,0:T(1,128)S(1)} %compare_select_fusion), channel_id=1, source_target_pairs={{0,4},{1,5},{2,6},{3,7},{4,0},{5,1},{6,2},{7,3},{8,12},{9,13},{10,... | collective-permute-start | bytes 392 | tf_op jit(solution)/shard_map/ppermute | solution.py:39
  4.3 15.3 %collective-permute-start.7 = (bf16[512,256]{1,0:T(8,128)(2,1)}, bf16[512,256]{1,0:T(8,128)(2,1)S(1)}, u32[]{:S(2)}, u32[]{:S(2)}) collective-permute-start(bf16[512,256]{1,0:T(8,128)(2,1)} %refs_2_.1), channel_id=1, source_target_pairs={{0,4},{4,8},{8,12},{12,16},{16,20},{20,24},{24,28},{28,0},{1,5},{5... | collective-permute-start | bytes 786440 | tf_op jit(solution)/shard_map/ppermute | solution.py:25
  4.4 16.3 %collective-permute-start.8 = (bf16[512,256]{1,0:T(8,128)(2,1)}, bf16[512,256]{1,0:T(8,128)(2,1)S(1)}, u32[]{:S(2)}, u32[]{:S(2)}) collective-permute-start(bf16[512,256]{1,0:T(8,128)(2,1)} %refs_3_.1), channel_id=1, source_target_pairs={{0,4},{4,8},{8,12},{12,16},{16,20},{20,24},{24,28},{28,0},{1,5},{5... | collective-permute-start | bytes 786440 | tf_op jit(solution)/shard_map/ppermute | solution.py:25
  9.1 3.0 %collective-permute-start.3 = (s32[1,32]{1,0:T(1,128)S(1)}, s32[1,32]{1,0:T(1,128)S(1)}, u32[]{:S(2)}, u32[]{:S(2)}) collective-permute-start(s32[1,32]{1,0:T(1,128)S(1)} %fusion), channel_id=1, source_target_pairs={{0,3},{1,2},{2,1},{3,0},{4,7},{5,6},{6,5},{7,4},{8,11},{9,10},{10,... | collective-permute-start | bytes 392 | tf_op jit(solution)/shard_map/ppermute | solution.py:39
  9.3 3.5 %collective-permute-start.2 = (s32[1,32]{1,0:T(1,128)S(1)}, s32[1,32]{1,0:T(1,128)S(1)}, u32[]{:S(2)}, u32[]{:S(2)}) collective-permute-start(s32[1,32]{1,0:T(1,128)S(1)} %fusion), channel_id=1, source_target_pairs={{0,2},{1,3},{2,0},{3,1},{4,6},{5,7},{6,4},{7,5},{8,10},{9,11},{10,... | collective-permute-start | bytes 392 | tf_op jit(solution)/shard_map/ppermute | solution.py:39
  10.8 2.1 %collective-permute-start.1 = (s32[1,32]{1,0:T(1,128)S(1)}, s32[1,32]{1,0:T(1,128)S(1)}, u32[]{:S(2)}, u32[]{:S(2)}) collective-permute-start(s32[1,32]{1,0:T(1,128)S(1)} %fusion), channel_id=1, source_target_pairs={{0,1},{1,0},{2,3},{3,2},{4,5},{5,4},{6,7},{7,6},{8,9},{9,8},{10,11... | collective-permute-start | bytes 392 | tf_op jit(solution)/shard_map/ppermute | solution.py:39
  12.8 5.4 %collective-permute-start.6 = (s32[1,32]{1,0:T(1,128)S(1)}, s32[1,32]{1,0:T(1,128)S(1)}, u32[]{:S(2)}, u32[]{:S(2)}) collective-permute-start(s32[1,32]{1,0:T(1,128)S(1)} %add_add_fusion.1), channel_id=1, source_target_pairs={{0,24},{1,25},{2,26},{3,27},{4,28},{5,29},{6,30},{7,31},{8,16},{9,... | collective-permute-start | bytes 392 | tf_op jit(solution)/shard_map/ppermute | solution.py:39
  15.2 4.5 %collective-permute-start.5 = (s32[1,32]{1,0:T(1,128)S(1)}, s32[1,32]{1,0:T(1,128)S(1)}, u32[]{:S(2)}, u32[]{:S(2)}) collective-permute-start(s32[1,32]{1,0:T(1,128)S(1)} %add_add_fusion.1), channel_id=1, source_target_pairs={{0,16},{1,17},{2,18},{3,19},{4,20},{5,21},{6,22},{7,23},{8,24},{9,... | collective-permute-start | bytes 392 | tf_op jit(solution)/shard_map/ppermute | solution.py:39
  16.0 3.7 %collective-permute-start.4 = (s32[1,32]{1,0:T(1,128)S(1)}, s32[1,32]{1,0:T(1,128)S(1)}, u32[]{:S(2)}, u32[]{:S(2)}) collective-permute-start(s32[1,32]{1,0:T(1,128)S(1)} %add_add_fusion.1), channel_id=1, source_target_pairs={{0,8},{1,9},{2,10},{3,11},{4,12},{5,13},{6,14},{7,15},{8,0},{9,1},... | collective-permute-start | bytes 392 | tf_op jit(solution)/shard_map/ppermute | solution.py:39
  22.4 11.3 %collective-permute-start.9 = (bf16[512,256]{1,0:T(8,128)(2,1)S(1)}, bf16[512,256]{1,0:T(8,128)(2,1)S(1)}, u32[]{:S(2)}, u32[]{:S(2)}) collective-permute-start(bf16[512,256]{1,0:T(8,128)(2,1)S(1)} %get-tuple-element.33), channel_id=1, source_target_pairs={{0,28},{4,0},{8,4},{12,8},{16,12},{20,16},{24,20},{28,24},{1,29},{... | collective-permute-start | bytes 786440 | tf_op jit(solution)/shard_map/ppermute | solution.py:25
  25.6 9.4 %collective-permute-start.10 = (bf16[512,256]{1,0:T(8,128)(2,1)S(1)}, bf16[512,256]{1,0:T(8,128)(2,1)S(1)}, u32[]{:S(2)}, u32[]{:S(2)}) collective-permute-start(bf16[512,256]{1,0:T(8,128)(2,1)S(1)} %get-tuple-element.34), channel_id=1, source_target_pairs={{0,28},{4,0},{8,4},{12,8},{16,12},{20,16},{24,20},{28,24},{1,29},{... | collective-permute-start | bytes 786440 | tf_op jit(solution)/shard_map/ppermute | solution.py:25

commit v6 on v5

--- a/solution.py
+++ b/solution.py
@@ -97,7 +97,16 @@
     return query_rows, grad_rows, scores, dot(v_ref[seen, column(g)], grad_rows, NT)
 
 
-def fetch_kernel(count, *refs):
+def own_sums(stat_ref, i, g, heads, q_ref, g_ref, k_ref, v_ref, start_ref):
+    _, _, own, down = own_block(i, g, heads, q_ref, g_ref, k_ref, v_ref, start_ref)
+    top = jnp.max(own, axis=0, keepdims=True)
+    own = jnp.exp2(own - top)
+    stat_ref[0:1, :] = top
+    stat_ref[1:2, :] = jnp.sum(own, axis=0, keepdims=True)
+    stat_ref[2:3, :] = jnp.sum(own * down, axis=0, keepdims=True)
+
+
+def fetch_kernel(count, after_ref, *refs):
     sources, targets, sems = refs[:count], refs[count : 2 * count], refs[2 * count]
     half = sources[0].shape[0] // 2
     copies = []
@@ -111,10 +120,24 @@
         copy.wait()
 
 
+def first_kernel(first_ref, len_ref, q_ref, g_ref, k_ref, v_ref, stat_ref, start_ref):
+    rows, width = q_ref.shape
+
+    @pl.when(first_ref[0] == 0)
+    def _():
+        start_ref[...] = start_row(len_ref[...], first_ref[0], rows)
+        for g in range(k_ref.shape[1] // HEAD_WIDTH):
+            for i in range(rows // BLOCK):
+                own_sums(
+                    stat_ref.at[g, i], i, g, width // k_ref.shape[1],
+                    q_ref, g_ref, k_ref, v_ref, start_ref,
+                )
+
+
 def prev_kernel(g, first_ref, len_ref, pk_ref, pv_ref, *refs):
     q_ref, g_ref, k_ref, v_ref = refs[:4]
     if g == 0:
-        send_ref, stat_ref, dq_ref, reach_ref, start_ref = refs[4:]
+        send_ref, stat_ref, dq_ref, reach_ref, start_ref = refs[5:]
     else:
         start_ref, send_ref, stat_ref, dq_ref = refs[4:]
     rows, width = q_ref.shape
@@ -123,34 +146,30 @@
     if g == 0:
         start_ref[...] = start_row(len_ref[...], first_ref[0], rows)
     start = start_ref[...]
-    before = pl.cdiv(jnp.maximum(-jnp.min(start), 0), BLOCK)
     after = pl.cdiv(jnp.sum((start < 0).astype(jnp.int32)), BLOCK)
     if g == 0:
         reach_ref[0] = after
-    for i in range(blocks):
-        _, _, own, down = own_block(i, g, heads, q_ref, g_ref, k_ref, v_ref, start_ref)
-        top = jnp.max(own, axis=0, keepdims=True)
-        own = jnp.exp2(own - top)
-        stat_ref[i, 0:1, :] = top
-        stat_ref[i, 1:2, :] = jnp.sum(own, axis=0, keepdims=True)
-        stat_ref[i, 2:3, :] = jnp.sum(own * down, axis=0, keepdims=True)
-
     def crossing(keys, queries):
         seen = slice((blocks - keys) * BLOCK, rows)
         key_rows, value_rows = pk_ref[seen, column(g)], pv_ref[seen, column(g)]
         probs, dscores, query_rows, grad_rows = [], [], [], []
         for i in range(queries):
-            query_rows.append(stacked(q_ref, i, g, heads))
-            grad_rows.append(stacked(g_ref, i, g, heads))
-            prev = dot(key_rows, query_rows[i], NT) * (SCALE * LOG2E)
+            rows_i, grads_i, own, down = own_block(
+                i, g, heads, q_ref, g_ref, k_ref, v_ref, start_ref
+            )
+            query_rows.append(rows_i)
+            grad_rows.append(grads_i)
+            prev = dot(key_rows, rows_i, NT) * (SCALE * LOG2E)
             prev = masked(prev, start_ref[:, i * BLOCK : (i + 1) * BLOCK], -keys * BLOCK)
-            own_top, own_total, own_sum = (stat_ref[i, n : n + 1, :] for n in range(3))
-            top = jnp.maximum(own_top, jnp.max(prev, axis=0, keepdims=True))
-            prev = jnp.exp2(prev - top)
-            kept = jnp.exp2(own_top - top)
-            dprev = dot(value_rows, grad_rows[i], NT)
-            total = own_total * kept + jnp.sum(prev, axis=0, keepdims=True)
-            dsum = own_sum * kept + jnp.sum(prev * dprev, axis=0, keepdims=True)
+            dprev = dot(value_rows, grads_i, NT)
+            top = jnp.maximum(
+                jnp.max(own, axis=0, keepdims=True), jnp.max(prev, axis=0, keepdims=True)
+            )
+            own, prev = jnp.exp2(own - top), jnp.exp2(prev - top)
+            total = jnp.sum(own, axis=0, keepdims=True) + jnp.sum(prev, axis=0, keepdims=True)
+            dsum = jnp.sum(own * down, axis=0, keepdims=True) + jnp.sum(
+                prev * dprev, axis=0, keepdims=True
+            )
             stat_ref[i, 0:1, :] = top
             stat_ref[i, 1:2, :] = total
             stat_ref[i, 2:3, :] = dsum
@@ -170,11 +189,8 @@
             rest = slice(0, (blocks - keys) * BLOCK)
             send_ref[rest, :] = jnp.zeros(send_ref[rest, :].shape, jnp.bfloat16)
 
-    for keys in range(1, blocks + 1):
-        for queries in range(1, blocks + 2 - keys):
-            pl.when((before == keys) & (after == queries))(
-                functools.partial(crossing, keys, queries)
-            )
+    for queries in range(1, blocks + 1):
+        pl.when(after == queries)(functools.partial(crossing, blocks + 1 - queries, queries))
 
     @pl.when(after == 0)
     def _():
@@ -182,23 +198,38 @@
 
 
 def own_kernel(kv_heads, *refs):
-    reach_ref, q_ref, g_ref, k_ref, v_ref, start_ref = refs[:6]
-    per_head = [refs[6 + 2 * g : 8 + 2 * g] for g in range(kv_heads)]
-    refs = refs[6 + 2 * kv_heads :]
-    dq_hbm, keeps, (dq_ref, dk_ref, dv_ref, sems) = refs[0], refs[1 : 1 + kv_heads], refs[1 + kv_heads :]
+    first_ref, reach_ref, q_ref, g_ref, k_ref, v_ref, start_ref, stat_ref = refs[:8]
+    per_head = [refs[8 + 2 * g : 10 + 2 * g] for g in range(kv_heads)]
+    refs = refs[8 + 2 * kv_heads :]
+    dq_hbm, keeps, (dq_ref, dk_ref, dv_ref, sums_ref, sems) = refs[0], refs[1 : 1 + kv_heads], refs[1 + kv_heads :]
     rows, width = q_ref.shape
     heads = width // k_ref.shape[1]
     blocks = rows // BLOCK
     reach = reach_ref[0]
+    @pl.when(first_ref[0] == 0)
+    def _():
+        sums_ref[...] = stat_ref[...]
+
+    for g in range(kv_heads):
+        for i in range(blocks):
+
+            @pl.when(i < reach)
+            def _():
+                sums_ref[g, i] = per_head[g][0][i]
+
+            @pl.when((first_ref[0] > 0) & (i >= reach))
+            def _():
+                own_sums(sums_ref.at[g, i], i, g, heads, q_ref, g_ref, k_ref, v_ref, start_ref)
+
     copies = []
     for g in range(kv_heads):
-        stat_ref, dqp_ref = per_head[g]
+        dqp_ref = per_head[g][1]
         for i in reversed(range(blocks)):
             seen = slice(0, (i + 1) * BLOCK)
             query_rows, grad_rows, own, down = own_block(
                 i, g, heads, q_ref, g_ref, k_ref, v_ref, start_ref
             )
-            top, total, dsum = (stat_ref[i, n : n + 1, :] for n in range(3))
+            top, total, dsum = (sums_ref[g, i, n : n + 1, :] for n in range(3))
             inverse = 1.0 / total
             own = jnp.exp2(own - top) * inverse
             down = (own * (down - dsum * inverse)).astype(jnp.bfloat16)
@@ -250,8 +281,10 @@
     prev_keys = rotated(keys, "seq", 1)
     prev_values = rotated(values, "seq", 1)
     row = lengths_row(doc_lengths, axes)
+    known = []
     for group in round_groups():
         row = summed_round(row, axes, group)
+        known.append(row)
     first = (lax.axis_index("seq") * rows).astype(jnp.int32).reshape(1)
     params = pltpu.CompilerParams(vmem_limit_bytes=24 * 1024 * 1024)
     shape = jax.ShapeDtypeStruct
@@ -268,21 +301,30 @@
     fetched = pl.pallas_call(
         functools.partial(fetch_kernel, len(arrays)),
         out_shape=[shape(a.shape, a.dtype) for a in arrays],
-        in_specs=[hbm] * len(arrays),
+        in_specs=[hbm] * (1 + len(arrays)),
         out_specs=[vmem] * len(arrays),
         scratch_shapes=[pltpu.SemaphoreType.DMA((2 * len(arrays),))],
         compiler_params=params,
         name="fetch",
-    )(*(pltpu.with_memory_space_constraint(a, pltpu.HBM) for a in arrays))
+    )(known[1], *(pltpu.with_memory_space_constraint(a, pltpu.HBM) for a in arrays))
+    first_stats = pl.pallas_call(
+        first_kernel,
+        out_shape=shape((kv_heads, blocks, 8, lanes), jnp.float32),
+        in_specs=[smem] + [vmem] * 5,
+        out_specs=vmem,
+        scratch_shapes=[pltpu.VMEM((1, rows), jnp.int32)],
+        compiler_params=params,
+        name="first_sums",
+    )(first, row, *fetched)
     send, stat, dq, reach, start = pl.pallas_call(
         functools.partial(prev_kernel, 0),
         out_shape=per_head
         + [shape((1,), jnp.int32), shape((1, rows), jnp.int32)],
-        in_specs=[smem] + [vmem] * 7,
+        in_specs=[smem] + [vmem] * 8,
         out_specs=[vmem] * 3 + [smem, vmem],
         compiler_params=params,
         name="prev_grads",
-    )(first, row, prev_keys, prev_values, *fetched)
+    )(first, row, prev_keys, prev_values, *fetched, first_stats)
     sends, stats = [send], [stat, dq]
     for g in range(1, kv_heads):
         send, stat, dq = pl.pallas_call(
@@ -300,14 +342,15 @@
         functools.partial(own_kernel, kv_heads),
         out_shape=[shape(queries.shape, jnp.bfloat16)]
         + [shape(pair.shape, jnp.float32)] * kv_heads,
-        in_specs=[smem] + [vmem] * (5 + 2 * kv_heads),
+        in_specs=[smem] * 2 + [vmem] * (6 + 2 * kv_heads),
         out_specs=[hbm] + [vmem] * kv_heads,
         scratch_shapes=[pltpu.VMEM(queries.shape, jnp.bfloat16)]
         + [pltpu.VMEM((rows, HEAD_WIDTH), jnp.float32)] * 2
+        + [pltpu.VMEM((kv_heads, blocks, 8, lanes), jnp.float32)]
         + [pltpu.SemaphoreType.DMA((kv_heads * blocks,))],
         compiler_params=params,
         name="own_grads",
-    )(reach, *fetched, start, *stats)
+    )(first, reach, *fetched, start, first_stats, *stats)
     key_gradient, value_gradient = pl.pallas_call(
         functools.partial(sum_kernel, kv_heads),
         out_shape=[shape(keys.shape, jnp.bfloat16)] * 2,

time: 36.4 us -> 35.7 us (0.981)
  waiting for transfers between devices: 6.49 us -> 4.07 us
  starting transfers between devices: 17.2 us -> 18.4 us
  Pallas kernels: 10.9 us -> 11.7 us
    pallas_call x0 -> x1, Pallas kernels: none -> 2.26 us  [body(): pl.pallas_call(first_kernel, out_shape=shape((kv_heads, blocks, 8, lanes)...]
    ppermute x7, waiting for transfers between devices: 4.11 us -> 2.6 us  [summed_round(): lax.ppermute(value, axes, [(s, s ^ m) for s in range(count)])]
    ppermute x4, starting transfers between devices: 7.79 us -> 9.01 us  [rotated(): lax.ppermute(value, axis, [(s, (s + steps) % count) for s in range(count)])]
    pallas_call x1, Pallas kernels: 1.72 us -> 0.79 us  [body(): pl.pallas_call(functools.partial(prev_kernel, 0), out_shape=per_head + [s...]
    ppermute x4, waiting for transfers between devices: 2.38 us -> 1.47 us  [rotated(): lax.ppermute(value, axis, [(s, (s + steps) % count) for s in range(count)])]
    pallas_call x1, Pallas kernels: 1.23 us -> 0.35 us  [body(): pl.pallas_call(functools.partial(prev_kernel, g), out_shape=per_head, in_...]
    pallas_call x1, Pallas kernels: 5.28 us -> 5.69 us  [body(): pl.pallas_call(functools.partial(own_kernel, kv_heads), out_shape=[shape(...]
  transfers between devices with their start and end apart: 11 -> 11, of which waited for: 6 -> 5; matrix products, arithmetic and copies ran while one was open for 0% -> 0% of each run, Pallas kernels for 23% -> 28%
where the time goes in v6:
time: 35.7 us; the launch traced here: 35.6 us
  starting transfers between devices  18.4 us (52%)
  Pallas kernels  11.7 us (33%)
  waiting for transfers between devices  4.07 us (11%)
  between operations  1.37 us (4%)
    ppermute x7, starting transfers between devices, summed_round(): lax.ppermute(value, axes, [(s, s ^ m) for s in range(count)])  9.4 us
    ppermute x4, starting transfers between devices, rotated(): lax.ppermute(value, axis, [(s, (s + steps) % count) for s in range(count)])  9.01 us
    pallas_call x1, Pallas kernels, body(): pl.pallas_call(functools.partial(own_kernel, kv_heads), out_shape=[shape(...  5.69 us
    ppermute x7, waiting for transfers between devices, summed_round(): lax.ppermute(value, axes, [(s, s ^ m) for s in range(count)])  2.6 us
    pallas_call x1, Pallas kernels, body(): pl.pallas_call(first_kernel, out_shape=shape((kv_heads, blocks, 8, lanes)...  2.26 us
    pallas_call x1, Pallas kernels, body(): pl.pallas_call(functools.partial(fetch_kernel, len(arrays)), out_shape=[s...  1.72 us
    ppermute x4, waiting for transfers between devices, rotated(): lax.ppermute(value, axis, [(s, (s + steps) % count) for s in range(count)])  1.47 us
    pallas_call x1, Pallas kernels, body(): pl.pallas_call(functools.partial(sum_kernel, kv_heads), out_shape=[shape(...  0.9 us
  transfers between devices with their start and end apart: 11, of which 5 were waited for; matrix products, arithmetic and copies ran while one was open for 0% of the time, Pallas kernels for 28%

profile of v6, /device:TPU:0, one launch (start us, length us, event | category | flops | bytes accessed | tf_op | source)
XLA Modules:
  0.0 35.6 jit_solution(12101994919433847021)
XLA Ops:
  1.3 3.0 %collective-permute-start = (s32[1,32]{1,0:T(1,128)S(1)}, s32[1,32]{1,0:T(1,128)S(1)}, u32[]{:S(2)}, u32[]{:S(2)}) collective-permute-start(s32[1,32]{1,0:T(1,128)S(1)} %compare_select_fusion), channel_id=1, source_target_pairs={{0,4},{1,5},{2,6},{3,7},{4,0},{5,1},{6,2},{7,3},{8,12},{9,13},{10,... | collective-permute-start | bytes 392 | tf_op jit(solution)/shard_map/ppermute | solution.py:39
  4.3 0.1 collective-permute-start.7
  4.4 3.0 %collective-permute-start.8 = (bf16[512,256]{1,0:T(8,128)(2,1)}, bf16[512,256]{1,0:T(8,128)(2,1)S(1)}, u32[]{:S(2)}, u32[]{:S(2)}) collective-permute-start(bf16[512,256]{1,0:T(8,128)(2,1)} %refs_3_.1), channel_id=1, source_target_pairs={{0,4},{4,8},{8,12},{12,16},{16,20},{20,24},{24,28},{28,0},{1,5},{5... | collective-permute-start | bytes 786440 | tf_op jit(solution)/shard_map/ppermute | solution.py:25
  7.3 0.2 collective-permute-start.3
  7.5 1.5 %collective-permute-start.2 = (s32[1,32]{1,0:T(1,128)S(1)}, s32[1,32]{1,0:T(1,128)S(1)}, u32[]{:S(2)}, u32[]{:S(2)}) collective-permute-start(s32[1,32]{1,0:T(1,128)S(1)} %fusion), channel_id=1, source_target_pairs={{0,2},{1,3},{2,0},{3,1},{4,6},{5,7},{6,4},{7,5},{8,10},{9,11},{10,... | collective-permute-start | bytes 392 | tf_op jit(solution)/shard_map/ppermute | solution.py:39
  9.0 0.3 collective-permute-start.1
  9.3 1.1 %collective-permute-done.3 = s32[1,32]{1,0:T(1,128)S(1)} collective-permute-done((s32[1,32]{1,0:T(1,128)S(1)}, s32[1,32]{1,0:T(1,128)S(1)}, u32[]{:S(2)}, u32[]{:S(2)}) %collective-permute-start.3) | collective-permute-done | bytes 160 | tf_op jit(solution)/shard_map/ppermute | solution.py:39
  10.4 0.7 %collective-permute-done.2 = s32[1,32]{1,0:T(1,128)S(1)} collective-permute-done((s32[1,32]{1,0:T(1,128)S(1)}, s32[1,32]{1,0:T(1,128)S(1)}, u32[]{:S(2)}, u32[]{:S(2)}) %collective-permute-start.2) | collective-permute-done | bytes 160 | tf_op jit(solution)/shard_map/ppermute | solution.py:39
  11.1 0.0 collective-permute-done.1
  11.1 2.6 %collective-permute-start.6 = (s32[1,32]{1,0:T(1,128)S(1)}, s32[1,32]{1,0:T(1,128)S(1)}, u32[]{:S(2)}, u32[]{:S(2)}) collective-permute-start(s32[1,32]{1,0:T(1,128)S(1)} %add_add_fusion.1.after_ref), channel_id=1, source_target_pairs={{0,24},{1,25},{2,26},{3,27},{4,28},{5,29},{6,30},{7,31},{8,16},{9,... | collective-permute-start | bytes 392 | tf_op jit(solution)/shard_map/ppermute | solution.py:39
  13.6 0.6 %collective-permute-start.5 = (s32[1,32]{1,0:T(1,128)S(1)}, s32[1,32]{1,0:T(1,128)S(1)}, u32[]{:S(2)}, u32[]{:S(2)}) collective-permute-start(s32[1,32]{1,0:T(1,128)S(1)} %add_add_fusion.1.after_ref), channel_id=1, source_target_pairs={{0,16},{1,17},{2,18},{3,19},{4,20},{5,21},{6,22},{7,23},{8,24},{9,... | collective-permute-start | bytes 392 | tf_op jit(solution)/shard_map/ppermute | solution.py:39
  14.2 1.3 %collective-permute-start.4 = (s32[1,32]{1,0:T(1,128)S(1)}, s32[1,32]{1,0:T(1,128)S(1)}, u32[]{:S(2)}, u32[]{:S(2)}) collective-permute-start(s32[1,32]{1,0:T(1,128)S(1)} %add_add_fusion.1.after_ref), channel_id=1, source_target_pairs={{0,8},{1,9},{2,10},{3,11},{4,12},{5,13},{6,14},{7,15},{8,0},{9,1},... | collective-permute-start | bytes 392 | tf_op jit(solution)/shard_map/ppermute | solution.py:39
  15.6 1.7 %fetch.1 = (bf16[512,1024]{1,0:T(8,128)(2,1)S(1)}, bf16[512,1024]{1,0:T(8,128)(2,1)S(1)}, bf16[512,256]{1,0:T(8,128)(2,1)S(1)}, bf16[512,256]{1,0:T(8,128)(2,1)S(1)}) custom-call(s32[1,32]{1,0:T(1,128)S(1)} %add_add_fusion.1.after_ref, bf16[512,1024]{1,0:T(8,128)(2,1)} %refs_0_.1, bf16[512,1024]{1,0:T(8,128)(2,1)} %refs_1_.1, bf16[512,256]{1,0:T(8,128)(2,1)} %refs_2_.1, ...), custom_call_target="tpu_custom_call" | custom-call | tf_op jit(solution)/shard_map/fetch/pallas_call | solution.py:301
  17.3 0.8 %collective-permute-done.5 = s32[1,32]{1,0:T(1,128)S(1)} collective-permute-done((s32[1,32]{1,0:T(1,128)S(1)}, s32[1,32]{1,0:T(1,128)S(1)}, u32[]{:S(2)}, u32[]{:S(2)}) %collective-permute-start.5) | collective-permute-done | bytes 160 | tf_op jit(solution)/shard_map/ppermute | solution.py:39
  18.1 0.0 collective-permute-done.4
  18.1 2.3 %first_sums.1.refs_4_.refs_7_ = f32[2,4,8,512]{3,2,1,0:T(8,128)S(1)} custom-call(s32[1]{0:T(128)} %bitcast.first_ref.refs_0_, s32[1,32]{1,0:T(1,128)S(1)} %add_add_fusion.len_ref, bf16[512,1024]{1,0:T(8,128)(2,1)S(1)} %get-tuple-element.20.q_ref.refs_0_.refs_2_, bf16[512,1024]{1,0:T(8,128)(2,1)S(1)} %get-tuple-element.21.g_ref.refs_1_.refs_3_, ...), custom_call_target="tpu_custom_call" | custom-call | tf_op jit(solution)/shard_map/first_sums/pallas_call | solution.py:310
  20.4 0.3 collective-permute-done.8.pv_ref
  20.6 0.8 %prev_grads.2 = (bf16[512,256]{1,0:T(8,128)(2,1)S(1)}, f32[4,8,512]{2,1,0:T(8,128)S(1)}, f32[4,128,512]{2,1,0:T(8,128)S(1)}, s32[1]{0:T(128)}, s32[1,512]{1,0:T(1,128)S(1)}) custom-call(s32[1]{0:T(128)} %bitcast.first_ref.refs_0_, s32[1,32]{1,0:T(1,128)S(1)} %add_add_fusion.len_ref, bf16[512,256]{1,0:T(8,128)(2,1)S(1)} %collective-permute-done.7.pk_ref, ...), custom_call_target="tpu_custom_call" | custom-call | tf_op jit(solution)/shard_map/prev_grads/pallas_call | solution.py:319
  21.4 3.2 %collective-permute-start.9 = (bf16[512,256]{1,0:T(8,128)(2,1)S(1)}, bf16[512,256]{1,0:T(8,128)(2,1)S(1)}, u32[]{:S(2)}, u32[]{:S(2)}) collective-permute-start(bf16[512,256]{1,0:T(8,128)(2,1)S(1)} %get-tuple-element.33), channel_id=1, source_target_pairs={{0,28},{4,0},{8,4},{12,8},{16,12},{20,16},{24,20},{28,24},{1,29},{... | collective-permute-start | bytes 786440 | tf_op jit(solution)/shard_map/ppermute | solution.py:25
  24.6 0.3 prev_grads.3
  24.9 2.8 %collective-permute-start.10 = (bf16[512,256]{1,0:T(8,128)(2,1)S(1)}, bf16[512,256]{1,0:T(8,128)(2,1)S(1)}, u32[]{:S(2)}, u32[]{:S(2)}) collective-permute-start(bf16[512,256]{1,0:T(8,128)(2,1)S(1)} %get-tuple-element.34), channel_id=1, source_target_pairs={{0,28},{4,0},{8,4},{12,8},{16,12},{20,16},{24,20},{28,24},{1,29},{... | collective-permute-start | bytes 786440 | tf_op jit(solution)/shard_map/ppermute | solution.py:25
  27.8 5.7 %own_grads.1 = (bf16[512,1024]{1,0:T(8,128)(2,1)}, f32[512,256]{1,0:T(8,128)S(1)}, f32[512,256]{1,0:T(8,128)S(1)}) custom-call(s32[1]{0:T(128)} %bitcast.first_ref.refs_0_, s32[1]{0:T(128)} %get-tuple-element.24.refs_1_, bf16[512,1024]{1,0:T(8,128)(2,1)S(1)} %get-tuple-element.20.q_ref.refs_0_.refs_2_, ...), custom_call_target="tpu_custom_call" | custom-call | tf_op jit(solution)/shard_map/own_grads/pallas_call | solution.py:341
  33.5 1.2 %collective-permute-done.10.refs_3_ = bf16[512,256]{1,0:T(8,128)(2,1)S(1)} collective-permute-done((bf16[512,256]{1,0:T(8,128)(2,1)S(1)}, bf16[512,256]{1,0:T(8,128)(2,1)S(1)}, u32[]{:S(2)}, u32[]{:S(2)}) %collective-permute-start.10) | collective-permute-done | bytes 262176 | tf_op jit(solution)/shard_map/ppermute | solution.py:25
  34.7 0.9 %sums.1 = (bf16[512,256]{1,0:T(8,128)(2,1)}, bf16[512,256]{1,0:T(8,128)(2,1)}) custom-call(f32[512,256]{1,0:T(8,128)S(1)} %get-tuple-element.31.refs_0_, f32[512,256]{1,0:T(8,128)S(1)} %get-tuple-element.32.refs_1_, bf16[512,256]{1,0:T(8,128)(2,1)S(1)} %collective-permute-done.9.refs_2_, bf16[512,256]{1,0:T(8,128)(2,1)S(1)} %collective-permute-done.10.refs_3_), custom_call_target="tpu_custom_call" | custom-call | tf_op jit(solution)/shard_map/sums/pallas_call | solution.py:354
  (8 shorter events, 0.0 us)
Async XLA Ops:
  1.3 6.0 %collective-permute-start = (s32[1,32]{1,0:T(1,128)S(1)}, s32[1,32]{1,0:T(1,128)S(1)}, u32[]{:S(2)}, u32[]{:S(2)}) collective-permute-start(s32[1,32]{1,0:T(1,128)S(1)} %compare_select_fusion), channel_id=1, source_target_pairs={{0,4},{1,5},{2,6},{3,7},{4,0},{5,1},{6,2},{7,3},{8,12},{9,13},{10,... | collective-permute-start | bytes 392 | tf_op jit(solution)/shard_map/ppermute | solution.py:39
  4.3 16.1 %collective-permute-start.7 = (bf16[512,256]{1,0:T(8,128)(2,1)}, bf16[512,256]{1,0:T(8,128)(2,1)S(1)}, u32[]{:S(2)}, u32[]{:S(2)}) collective-permute-start(bf16[512,256]{1,0:T(8,128)(2,1)} %refs_2_.1), channel_id=1, source_target_pairs={{0,4},{4,8},{8,12},{12,16},{16,20},{20,24},{24,28},{28,0},{1,5},{5... | collective-permute-start | bytes 786440 | tf_op jit(solution)/shard_map/ppermute | solution.py:25
  4.4 16.3 %collective-permute-start.8 = (bf16[512,256]{1,0:T(8,128)(2,1)}, bf16[512,256]{1,0:T(8,128)(2,1)S(1)}, u32[]{:S(2)}, u32[]{:S(2)}) collective-permute-start(bf16[512,256]{1,0:T(8,128)(2,1)} %refs_3_.1), channel_id=1, source_target_pairs={{0,4},{4,8},{8,12},{12,16},{16,20},{20,24},{24,28},{28,0},{1,5},{5... | collective-permute-start | bytes 786440 | tf_op jit(solution)/shard_map/ppermute | solution.py:25
  7.3 3.0 %collective-permute-start.3 = (s32[1,32]{1,0:T(1,128)S(1)}, s32[1,32]{1,0:T(1,128)S(1)}, u32[]{:S(2)}, u32[]{:S(2)}) collective-permute-start(s32[1,32]{1,0:T(1,128)S(1)} %fusion), channel_id=1, source_target_pairs={{0,3},{1,2},{2,1},{3,0},{4,7},{5,6},{6,5},{7,4},{8,11},{9,10},{10,... | collective-permute-start | bytes 392 | tf_op jit(solution)/shard_map/ppermute | solution.py:39
  7.5 3.5 %collective-permute-start.2 = (s32[1,32]{1,0:T(1,128)S(1)}, s32[1,32]{1,0:T(1,128)S(1)}, u32[]{:S(2)}, u32[]{:S(2)}) collective-permute-start(s32[1,32]{1,0:T(1,128)S(1)} %fusion), channel_id=1, source_target_pairs={{0,2},{1,3},{2,0},{3,1},{4,6},{5,7},{6,4},{7,5},{8,10},{9,11},{10,... | collective-permute-start | bytes 392 | tf_op jit(solution)/shard_map/ppermute | solution.py:39
  9.0 2.1 %collective-permute-start.1 = (s32[1,32]{1,0:T(1,128)S(1)}, s32[1,32]{1,0:T(1,128)S(1)}, u32[]{:S(2)}, u32[]{:S(2)}) collective-permute-start(s32[1,32]{1,0:T(1,128)S(1)} %fusion), channel_id=1, source_target_pairs={{0,1},{1,0},{2,3},{3,2},{4,5},{5,4},{6,7},{7,6},{8,9},{9,8},{10,11... | collective-permute-start | bytes 392 | tf_op jit(solution)/shard_map/ppermute | solution.py:39
  11.1 6.2 %collective-permute-start.6 = (s32[1,32]{1,0:T(1,128)S(1)}, s32[1,32]{1,0:T(1,128)S(1)}, u32[]{:S(2)}, u32[]{:S(2)}) collective-permute-start(s32[1,32]{1,0:T(1,128)S(1)} %add_add_fusion.1.after_ref), channel_id=1, source_target_pairs={{0,24},{1,25},{2,26},{3,27},{4,28},{5,29},{6,30},{7,31},{8,16},{9,... | collective-permute-start | bytes 392 | tf_op jit(solution)/shard_map/ppermute | solution.py:39
  13.6 4.4 %collective-permute-start.5 = (s32[1,32]{1,0:T(1,128)S(1)}, s32[1,32]{1,0:T(1,128)S(1)}, u32[]{:S(2)}, u32[]{:S(2)}) collective-permute-start(s32[1,32]{1,0:T(1,128)S(1)} %add_add_fusion.1.after_ref), channel_id=1, source_target_pairs={{0,16},{1,17},{2,18},{3,19},{4,20},{5,21},{6,22},{7,23},{8,24},{9,... | collective-permute-start | bytes 392 | tf_op jit(solution)/shard_map/ppermute | solution.py:39
  14.2 3.9 %collective-permute-start.4 = (s32[1,32]{1,0:T(1,128)S(1)}, s32[1,32]{1,0:T(1,128)S(1)}, u32[]{:S(2)}, u32[]{:S(2)}) collective-permute-start(s32[1,32]{1,0:T(1,128)S(1)} %add_add_fusion.1.after_ref), channel_id=1, source_target_pairs={{0,8},{1,9},{2,10},{3,11},{4,12},{5,13},{6,14},{7,15},{8,0},{9,1},... | collective-permute-start | bytes 392 | tf_op jit(solution)/shard_map/ppermute | solution.py:39
  21.4 12.0 %collective-permute-start.9 = (bf16[512,256]{1,0:T(8,128)(2,1)S(1)}, bf16[512,256]{1,0:T(8,128)(2,1)S(1)}, u32[]{:S(2)}, u32[]{:S(2)}) collective-permute-start(bf16[512,256]{1,0:T(8,128)(2,1)S(1)} %get-tuple-element.33), channel_id=1, source_target_pairs={{0,28},{4,0},{8,4},{12,8},{16,12},{20,16},{24,20},{28,24},{1,29},{... | collective-permute-start | bytes 786440 | tf_op jit(solution)/shard_map/ppermute | solution.py:25
  24.9 9.7 %collective-permute-start.10 = (bf16[512,256]{1,0:T(8,128)(2,1)S(1)}, bf16[512,256]{1,0:T(8,128)(2,1)S(1)}, u32[]{:S(2)}, u32[]{:S(2)}) collective-permute-start(bf16[512,256]{1,0:T(8,128)(2,1)S(1)} %get-tuple-element.34), channel_id=1, source_target_pairs={{0,28},{4,0},{8,4},{12,8},{16,12},{20,16},{24,20},{28,24},{1,29},{... | collective-permute-start | bytes 786440 | tf_op jit(solution)/shard_map/ppermute | solution.py:25

commit v7 on v6

--- a/solution.py
+++ b/solution.py
@@ -30,7 +30,7 @@
     count = low * lax.axis_size("seq")
     bits = [1 << b for b in range(count.bit_length() - 1)]
     head, seq = [b for b in bits if b < low], [b for b in bits if b > low]
-    return [[low]] + [part[n : n + 2] for part in (head, seq) for n in range(0, len(part), 2)]
+    return [part[n : n + 2] for part in (head, seq) for n in range(0, len(part), 2)]
 
 
 def summed_round(value, axes, group):
@@ -40,10 +40,9 @@
     return functools.reduce(jnp.add, others, value)
 
 
-def lengths_row(doc_lengths, axes):
+def lengths_row(doc_lengths, place, shards):
     own = doc_lengths.shape[0]
-    shards = lax.axis_size(axes)
-    spot = lax.broadcasted_iota(jnp.int32, (1, shards, own), 1) == lax.axis_index(axes)
+    spot = lax.broadcasted_iota(jnp.int32, (1, shards, own), 1) == place
     return jnp.where(spot, doc_lengths[None, None, :], 0).reshape(1, shards * own)
 
 
@@ -280,8 +279,11 @@
     axes = ("seq", "head")
     prev_keys = rotated(keys, "seq", 1)
     prev_values = rotated(values, "seq", 1)
-    row = lengths_row(doc_lengths, axes)
-    known = []
+    shards, place, low = lax.axis_size(axes), lax.axis_index(axes), lax.axis_size("head")
+    others = lax.ppermute(doc_lengths, axes, [(s, s ^ low) for s in range(shards)])
+    row = lengths_row(doc_lengths, place, shards) + lengths_row(others, place ^ low, shards)
+    row = lax.optimization_barrier(row)
+    known = [row]
     for group in round_groups():
         row = summed_round(row, axes, group)
         known.append(row)

time: 35.7 us -> 36.1 us (1.011)
  other arithmetic: 0.02 us -> 0.63 us
    ppermute x0 -> x1, starting transfers between devices: none -> 3 us  [body(): lax.ppermute(doc_lengths, axes, [(s, s ^ low) for s in range(shards)])]
    ppermute x7 -> x6, starting transfers between devices: 9.4 us -> 6.4 us  [summed_round(): lax.ppermute(value, axes, [(s, s ^ m) for s in range(count)])]
    add x0 -> x1, other arithmetic: none -> 0.62 us  [body(): lengths_row(doc_lengths, place, shards)]
    ppermute x7 -> x6, waiting for transfers between devices: 2.6 us -> 2.37 us  [summed_round(): lax.ppermute(value, axes, [(s, s ^ m) for s in range(count)])]
  transfers between devices with their start and end apart: 11 -> 11, of which waited for: 5 -> 4; matrix products, arithmetic and copies ran while one was open for 0% -> 2% of each run, Pallas kernels for 28% -> 28%
where the time goes in v7:
time: 36.1 us; the launch traced here: 35.9 us
  starting transfers between devices  18.2 us (50%)
  Pallas kernels  11.7 us (32%)
  waiting for transfers between devices  3.92 us (11%)
  between operations  1.38 us (4%)
  other arithmetic  0.63 us (2%)
    ppermute x4, starting transfers between devices, rotated(): lax.ppermute(value, axis, [(s, (s + steps) % count) for s in range(count)])  8.82 us
    ppermute x6, starting transfers between devices, summed_round(): lax.ppermute(value, axes, [(s, s ^ m) for s in range(count)])  6.4 us
    pallas_call x1, Pallas kernels, body(): pl.pallas_call(functools.partial(own_kernel, kv_heads), out_shape=[shape(...  5.69 us
    ppermute x1, starting transfers between devices, body(): lax.ppermute(doc_lengths, axes, [(s, s ^ low) for s in range(shards)])  3 us
    ppermute x6, waiting for transfers between devices, summed_round(): lax.ppermute(value, axes, [(s, s ^ m) for s in range(count)])  2.37 us
    pallas_call x1, Pallas kernels, body(): pl.pallas_call(first_kernel, out_shape=shape((kv_heads, blocks, 8, lanes)...  2.26 us
    pallas_call x1, Pallas kernels, body(): pl.pallas_call(functools.partial(fetch_kernel, len(arrays)), out_shape=[s...  1.72 us
    ppermute x4, waiting for transfers between devices, rotated(): lax.ppermute(value, axis, [(s, (s + steps) % count) for s in range(count)])  1.55 us
  transfers between devices with their start and end apart: 11, of which 4 were waited for; matrix products, arithmetic and copies ran while one was open for 2% of the time, Pallas kernels for 28%

profile of v7, /device:TPU:0, one launch (start us, length us, event | category | flops | bytes accessed | tf_op | source)
XLA Modules:
  0.0 35.9 jit_solution(6688983601328862015)
XLA Ops:
  0.6 3.0 %collective-permute-start = (s32[1]{0:T(128)}, s32[1]{0:T(128)}, u32[]{:S(2)}, u32[]{:S(2)}) collective-permute-start(s32[1]{0:T(128)} %param.9), channel_id=1, source_target_pairs={{0,4},{1,5},{2,6},{3,7},{4,0},{5,1},{6,2},{7,3},{8,12},{9,13},{10,... | collective-permute-start | bytes 20 | tf_op jit(solution)/shard_map/ppermute | solution.py:283
  3.6 0.1 collective-permute-start.7
  3.7 3.0 %collective-permute-start.8 = (bf16[512,256]{1,0:T(8,128)(2,1)}, bf16[512,256]{1,0:T(8,128)(2,1)S(1)}, u32[]{:S(2)}, u32[]{:S(2)}) collective-permute-start(bf16[512,256]{1,0:T(8,128)(2,1)} %refs_3_.1), channel_id=1, source_target_pairs={{0,4},{4,8},{8,12},{12,16},{16,20},{20,24},{24,28},{28,0},{1,5},{5... | collective-permute-start | bytes 786440 | tf_op jit(solution)/shard_map/ppermute | solution.py:25
  7.3 0.0 collective-permute-done
  7.3 0.6 %fusion = s32[1,32]{1,0:T(1,128)S(1)} fusion(s32[]{:T(128)} %bitcast.2, s32[]{:T(128)S(6)} %xor.3, s32[]{:T(128)} %bitcast.3, s32[]{:T(128)S(6)} %add.32), kind=kLoop, calls=%fused_computation.2 | loop fusion | flops 160 | bytes 144 | tf_op jit(solution)/shard_map/add | solution.py:284
  8.0 0.2 collective-permute-start.3
  8.2 1.5 %collective-permute-start.2 = (s32[1,32]{1,0:T(1,128)S(1)}, s32[1,32]{1,0:T(1,128)S(1)}, u32[]{:S(2)}, u32[]{:S(2)}) collective-permute-start(s32[1,32]{1,0:T(1,128)S(1)} %fusion), channel_id=1, source_target_pairs={{0,2},{1,3},{2,0},{3,1},{4,6},{5,7},{6,4},{7,5},{8,10},{9,11},{10,... | collective-permute-start | bytes 392 | tf_op jit(solution)/shard_map/ppermute | solution.py:39
  9.6 0.3 collective-permute-start.1
  9.9 1.1 %collective-permute-done.3 = s32[1,32]{1,0:T(1,128)S(1)} collective-permute-done((s32[1,32]{1,0:T(1,128)S(1)}, s32[1,32]{1,0:T(1,128)S(1)}, u32[]{:S(2)}, u32[]{:S(2)}) %collective-permute-start.3) | collective-permute-done | bytes 160 | tf_op jit(solution)/shard_map/ppermute | solution.py:39
  11.0 0.7 %collective-permute-done.2 = s32[1,32]{1,0:T(1,128)S(1)} collective-permute-done((s32[1,32]{1,0:T(1,128)S(1)}, s32[1,32]{1,0:T(1,128)S(1)}, u32[]{:S(2)}, u32[]{:S(2)}) %collective-permute-start.2) | collective-permute-done | bytes 160 | tf_op jit(solution)/shard_map/ppermute | solution.py:39
  11.7 2.3 %collective-permute-start.6 = (s32[1,32]{1,0:T(1,128)S(1)}, s32[1,32]{1,0:T(1,128)S(1)}, u32[]{:S(2)}, u32[]{:S(2)}) collective-permute-start(s32[1,32]{1,0:T(1,128)S(1)} %add_add_fusion.1.after_ref), channel_id=1, source_target_pairs={{0,24},{1,25},{2,26},{3,27},{4,28},{5,29},{6,30},{7,31},{8,16},{9,... | collective-permute-start | bytes 392 | tf_op jit(solution)/shard_map/ppermute | solution.py:39
  14.0 0.8 %collective-permute-start.5 = (s32[1,32]{1,0:T(1,128)S(1)}, s32[1,32]{1,0:T(1,128)S(1)}, u32[]{:S(2)}, u32[]{:S(2)}) collective-permute-start(s32[1,32]{1,0:T(1,128)S(1)} %add_add_fusion.1.after_ref), channel_id=1, source_target_pairs={{0,16},{1,17},{2,18},{3,19},{4,20},{5,21},{6,22},{7,23},{8,24},{9,... | collective-permute-start | bytes 392 | tf_op jit(solution)/shard_map/ppermute | solution.py:39
  14.8 1.3 %collective-permute-start.4 = (s32[1,32]{1,0:T(1,128)S(1)}, s32[1,32]{1,0:T(1,128)S(1)}, u32[]{:S(2)}, u32[]{:S(2)}) collective-permute-start(s32[1,32]{1,0:T(1,128)S(1)} %add_add_fusion.1.after_ref), channel_id=1, source_target_pairs={{0,8},{1,9},{2,10},{3,11},{4,12},{5,13},{6,14},{7,15},{8,0},{9,1},... | collective-permute-start | bytes 392 | tf_op jit(solution)/shard_map/ppermute | solution.py:39
  16.2 1.7 %fetch.1 = (bf16[512,1024]{1,0:T(8,128)(2,1)S(1)}, bf16[512,1024]{1,0:T(8,128)(2,1)S(1)}, bf16[512,256]{1,0:T(8,128)(2,1)S(1)}, bf16[512,256]{1,0:T(8,128)(2,1)S(1)}) custom-call(s32[1,32]{1,0:T(1,128)S(1)} %add_add_fusion.1.after_ref, bf16[512,1024]{1,0:T(8,128)(2,1)} %refs_0_.1, bf16[512,1024]{1,0:T(8,128)(2,1)} %refs_1_.1, bf16[512,256]{1,0:T(8,128)(2,1)} %refs_2_.1, ...), custom_call_target="tpu_custom_call" | custom-call | tf_op jit(solution)/shard_map/fetch/pallas_call | solution.py:303
  17.9 0.0 collective-permute-done.6
  17.9 0.6 %collective-permute-done.5 = s32[1,32]{1,0:T(1,128)S(1)} collective-permute-done((s32[1,32]{1,0:T(1,128)S(1)}, s32[1,32]{1,0:T(1,128)S(1)}, u32[]{:S(2)}, u32[]{:S(2)}) %collective-permute-start.5) | collective-permute-done | bytes 160 | tf_op jit(solution)/shard_map/ppermute | solution.py:39
  18.5 2.3 %first_sums.1.refs_4_.refs_7_ = f32[2,4,8,512]{3,2,1,0:T(8,128)S(1)} custom-call(s32[1]{0:T(128)} %bitcast.first_ref.refs_0_, s32[1,32]{1,0:T(1,128)S(1)} %add_add_fusion.len_ref, bf16[512,1024]{1,0:T(8,128)(2,1)S(1)} %get-tuple-element.20.q_ref.refs_0_.refs_2_, bf16[512,1024]{1,0:T(8,128)(2,1)S(1)} %get-tuple-element.21.g_ref.refs_1_.refs_3_, ...), custom_call_target="tpu_custom_call" | custom-call | tf_op jit(solution)/shard_map/first_sums/pallas_call | solution.py:312
  20.8 0.8 %prev_grads.2 = (bf16[512,256]{1,0:T(8,128)(2,1)S(1)}, f32[4,8,512]{2,1,0:T(8,128)S(1)}, f32[4,128,512]{2,1,0:T(8,128)S(1)}, s32[1]{0:T(128)}, s32[1,512]{1,0:T(1,128)S(1)}) custom-call(s32[1]{0:T(128)} %bitcast.first_ref.refs_0_, s32[1,32]{1,0:T(1,128)S(1)} %add_add_fusion.len_ref, bf16[512,256]{1,0:T(8,128)(2,1)S(1)} %collective-permute-done.7.pk_ref, ...), custom_call_target="tpu_custom_call" | custom-call | tf_op jit(solution)/shard_map/prev_grads/pallas_call | solution.py:321
  21.6 3.0 %collective-permute-start.9 = (bf16[512,256]{1,0:T(8,128)(2,1)S(1)}, bf16[512,256]{1,0:T(8,128)(2,1)S(1)}, u32[]{:S(2)}, u32[]{:S(2)}) collective-permute-start(bf16[512,256]{1,0:T(8,128)(2,1)S(1)} %get-tuple-element.33), channel_id=1, source_target_pairs={{0,28},{4,0},{8,4},{12,8},{16,12},{20,16},{24,20},{28,24},{1,29},{... | collective-permute-start | bytes 786440 | tf_op jit(solution)/shard_map/ppermute | solution.py:25
  24.5 0.3 prev_grads.3
  24.9 2.8 %collective-permute-start.10 = (bf16[512,256]{1,0:T(8,128)(2,1)S(1)}, bf16[512,256]{1,0:T(8,128)(2,1)S(1)}, u32[]{:S(2)}, u32[]{:S(2)}) collective-permute-start(bf16[512,256]{1,0:T(8,128)(2,1)S(1)} %get-tuple-element.34), channel_id=1, source_target_pairs={{0,28},{4,0},{8,4},{12,8},{16,12},{20,16},{24,20},{28,24},{1,29},{... | collective-permute-start | bytes 786440 | tf_op jit(solution)/shard_map/ppermute | solution.py:25
  27.7 5.7 %own_grads.1 = (bf16[512,1024]{1,0:T(8,128)(2,1)}, f32[512,256]{1,0:T(8,128)S(1)}, f32[512,256]{1,0:T(8,128)S(1)}) custom-call(s32[1]{0:T(128)} %bitcast.first_ref.refs_0_, s32[1]{0:T(128)} %get-tuple-element.24.refs_1_, bf16[512,1024]{1,0:T(8,128)(2,1)S(1)} %get-tuple-element.20.q_ref.refs_0_.refs_2_, ...), custom_call_target="tpu_custom_call" | custom-call | tf_op jit(solution)/shard_map/own_grads/pallas_call | solution.py:343
  33.4 1.5 %collective-permute-done.10.refs_3_ = bf16[512,256]{1,0:T(8,128)(2,1)S(1)} collective-permute-done((bf16[512,256]{1,0:T(8,128)(2,1)S(1)}, bf16[512,256]{1,0:T(8,128)(2,1)S(1)}, u32[]{:S(2)}, u32[]{:S(2)}) %collective-permute-start.10) | collective-permute-done | bytes 262176 | tf_op jit(solution)/shard_map/ppermute | solution.py:25
  35.0 0.9 %sums.1 = (bf16[512,256]{1,0:T(8,128)(2,1)}, bf16[512,256]{1,0:T(8,128)(2,1)}) custom-call(f32[512,256]{1,0:T(8,128)S(1)} %get-tuple-element.31.refs_0_, f32[512,256]{1,0:T(8,128)S(1)} %get-tuple-element.32.refs_1_, bf16[512,256]{1,0:T(8,128)(2,1)S(1)} %collective-permute-done.9.refs_2_, bf16[512,256]{1,0:T(8,128)(2,1)S(1)} %collective-permute-done.10.refs_3_), custom_call_target="tpu_custom_call" | custom-call | tf_op jit(solution)/shard_map/sums/pallas_call | solution.py:356
  (7 shorter events, 0.0 us)
Async XLA Ops:
  0.6 6.7 %collective-permute-start = (s32[1]{0:T(128)}, s32[1]{0:T(128)}, u32[]{:S(2)}, u32[]{:S(2)}) collective-permute-start(s32[1]{0:T(128)} %param.9), channel_id=1, source_target_pairs={{0,4},{1,5},{2,6},{3,7},{4,0},{5,1},{6,2},{7,3},{8,12},{9,13},{10,... | collective-permute-start | bytes 20 | tf_op jit(solution)/shard_map/ppermute | solution.py:283
  3.6 17.1 %collective-permute-start.7 = (bf16[512,256]{1,0:T(8,128)(2,1)}, bf16[512,256]{1,0:T(8,128)(2,1)S(1)}, u32[]{:S(2)}, u32[]{:S(2)}) collective-permute-start(bf16[512,256]{1,0:T(8,128)(2,1)} %refs_2_.1), channel_id=1, source_target_pairs={{0,4},{4,8},{8,12},{12,16},{16,20},{20,24},{24,28},{28,0},{1,5},{5... | collective-permute-start | bytes 786440 | tf_op jit(solution)/shard_map/ppermute | solution.py:25
  3.7 17.1 %collective-permute-start.8 = (bf16[512,256]{1,0:T(8,128)(2,1)}, bf16[512,256]{1,0:T(8,128)(2,1)S(1)}, u32[]{:S(2)}, u32[]{:S(2)}) collective-permute-start(bf16[512,256]{1,0:T(8,128)(2,1)} %refs_3_.1), channel_id=1, source_target_pairs={{0,4},{4,8},{8,12},{12,16},{16,20},{20,24},{24,28},{28,0},{1,5},{5... | collective-permute-start | bytes 786440 | tf_op jit(solution)/shard_map/ppermute | solution.py:25
  8.0 3.0 %collective-permute-start.3 = (s32[1,32]{1,0:T(1,128)S(1)}, s32[1,32]{1,0:T(1,128)S(1)}, u32[]{:S(2)}, u32[]{:S(2)}) collective-permute-start(s32[1,32]{1,0:T(1,128)S(1)} %fusion), channel_id=1, source_target_pairs={{0,3},{1,2},{2,1},{3,0},{4,7},{5,6},{6,5},{7,4},{8,11},{9,10},{10,... | collective-permute-start | bytes 392 | tf_op jit(solution)/shard_map/ppermute | solution.py:39
  8.2 3.5 %collective-permute-start.2 = (s32[1,32]{1,0:T(1,128)S(1)}, s32[1,32]{1,0:T(1,128)S(1)}, u32[]{:S(2)}, u32[]{:S(2)}) collective-permute-start(s32[1,32]{1,0:T(1,128)S(1)} %fusion), channel_id=1, source_target_pairs={{0,2},{1,3},{2,0},{3,1},{4,6},{5,7},{6,4},{7,5},{8,10},{9,11},{10,... | collective-permute-start | bytes 392 | tf_op jit(solution)/shard_map/ppermute | solution.py:39
  9.6 2.1 %collective-permute-start.1 = (s32[1,32]{1,0:T(1,128)S(1)}, s32[1,32]{1,0:T(1,128)S(1)}, u32[]{:S(2)}, u32[]{:S(2)}) collective-permute-start(s32[1,32]{1,0:T(1,128)S(1)} %fusion), channel_id=1, source_target_pairs={{0,1},{1,0},{2,3},{3,2},{4,5},{5,4},{6,7},{7,6},{8,9},{9,8},{10,11... | collective-permute-start | bytes 392 | tf_op jit(solution)/shard_map/ppermute | solution.py:39
  11.7 6.2 %collective-permute-start.6 = (s32[1,32]{1,0:T(1,128)S(1)}, s32[1,32]{1,0:T(1,128)S(1)}, u32[]{:S(2)}, u32[]{:S(2)}) collective-permute-start(s32[1,32]{1,0:T(1,128)S(1)} %add_add_fusion.1.after_ref), channel_id=1, source_target_pairs={{0,24},{1,25},{2,26},{3,27},{4,28},{5,29},{6,30},{7,31},{8,16},{9,... | collective-permute-start | bytes 392 | tf_op jit(solution)/shard_map/ppermute | solution.py:39
  14.0 4.5 %collective-permute-start.5 = (s32[1,32]{1,0:T(1,128)S(1)}, s32[1,32]{1,0:T(1,128)S(1)}, u32[]{:S(2)}, u32[]{:S(2)}) collective-permute-start(s32[1,32]{1,0:T(1,128)S(1)} %add_add_fusion.1.after_ref), channel_id=1, source_target_pairs={{0,16},{1,17},{2,18},{3,19},{4,20},{5,21},{6,22},{7,23},{8,24},{9,... | collective-permute-start | bytes 392 | tf_op jit(solution)/shard_map/ppermute | solution.py:39
  14.8 3.7 %collective-permute-start.4 = (s32[1,32]{1,0:T(1,128)S(1)}, s32[1,32]{1,0:T(1,128)S(1)}, u32[]{:S(2)}, u32[]{:S(2)}) collective-permute-start(s32[1,32]{1,0:T(1,128)S(1)} %add_add_fusion.1.after_ref), channel_id=1, source_target_pairs={{0,8},{1,9},{2,10},{3,11},{4,12},{5,13},{6,14},{7,15},{8,0},{9,1},... | collective-permute-start | bytes 392 | tf_op jit(solution)/shard_map/ppermute | solution.py:39
  21.6 11.8 %collective-permute-start.9 = (bf16[512,256]{1,0:T(8,128)(2,1)S(1)}, bf16[512,256]{1,0:T(8,128)(2,1)S(1)}, u32[]{:S(2)}, u32[]{:S(2)}) collective-permute-start(bf16[512,256]{1,0:T(8,128)(2,1)S(1)} %get-tuple-element.33), channel_id=1, source_target_pairs={{0,28},{4,0},{8,4},{12,8},{16,12},{20,16},{24,20},{28,24},{1,29},{... | collective-permute-start | bytes 786440 | tf_op jit(solution)/shard_map/ppermute | solution.py:25
  24.9 10.1 %collective-permute-start.10 = (bf16[512,256]{1,0:T(8,128)(2,1)S(1)}, bf16[512,256]{1,0:T(8,128)(2,1)S(1)}, u32[]{:S(2)}, u32[]{:S(2)}) collective-permute-start(bf16[512,256]{1,0:T(8,128)(2,1)S(1)} %get-tuple-element.34), channel_id=1, source_target_pairs={{0,28},{4,0},{8,4},{12,8},{16,12},{20,16},{24,20},{28,24},{1,29},{... | collective-permute-start | bytes 786440 | tf_op jit(solution)/shard_map/ppermute | solution.py:25

commit v8 on v6

--- a/solution.py
+++ b/solution.py
@@ -262,13 +262,11 @@
         copy.wait()
 
 
-def sum_kernel(kv_heads, *refs):
-    keep, back = refs[:kv_heads], refs[kv_heads : 2 * kv_heads]
-    dk_ref, dv_ref = refs[2 * kv_heads :]
-    for g in range(kv_heads):
-        total = keep[g][...] + back[g][...].astype(jnp.float32)
-        dk_ref[:, column(g)] = total[:, :HEAD_WIDTH].astype(jnp.bfloat16)
-        dv_ref[:, column(g)] = total[:, HEAD_WIDTH:].astype(jnp.bfloat16)
+def sum_kernel(keep_ref, back_ref, *refs):
+    dk_ref, dv_ref = refs[-2:]
+    total = keep_ref[...] + back_ref[...].astype(jnp.float32)
+    dk_ref[...] = total[:, :HEAD_WIDTH].astype(jnp.bfloat16)
+    dv_ref[...] = total[:, HEAD_WIDTH:].astype(jnp.bfloat16)
 
 
 def body(queries, keys, values, output_gradient, doc_lengths):
@@ -351,12 +349,20 @@
         compiler_params=params,
         name="own_grads",
     )(first, reach, *fetched, start, first_stats, *stats)
-    key_gradient, value_gradient = pl.pallas_call(
-        functools.partial(sum_kernel, kv_heads),
-        out_shape=[shape(keys.shape, jnp.bfloat16)] * 2,
-        compiler_params=params,
-        name="sums",
-    )(*keeps, *backs)
+    sums = []
+    for g in range(kv_heads):
+        whole = pl.BlockSpec(pair.shape, lambda n: (0, 0))
+        sums = pl.pallas_call(
+            sum_kernel,
+            grid=(1,),
+            out_shape=[shape(keys.shape, jnp.bfloat16)] * 2,
+            in_specs=[whole] * 2 + [pl.BlockSpec(memory_space=pl.ANY)] * len(sums),
+            out_specs=[pl.BlockSpec((rows, HEAD_WIDTH), lambda n, g=g: (0, g))] * 2,
+            input_output_aliases={2: 0, 3: 1} if sums else {},
+            compiler_params=params,
+            name="sums",
+        )(keeps[g], backs[g], *sums)
+    key_gradient, value_gradient = sums
     return (grad_queries, key_gradient, value_gradient)
 
 

time: 35.7 us -> 36 us (level)
  waiting for transfers between devices: 4.07 us -> 2.86 us
  starting transfers between devices: 18.4 us -> 19.6 us
  Pallas kernels: 11.7 us -> 12.3 us
    ppermute x4, waiting for transfers between devices: 1.47 us -> 0.26 us  [rotated(): lax.ppermute(value, axis, [(s, (s + steps) % count) for s in range(count)])]
    ppermute x4, starting transfers between devices: 9.01 us -> 10.2 us  [rotated(): lax.ppermute(value, axis, [(s, (s + steps) % count) for s in range(count)])]
    pallas_call x1 -> x2, Pallas kernels: 0.9 us -> 1.51 us  [body(): pl.pallas_call(sum_kernel, grid=(1,), out_shape=[shape(keys.shape, jnp.bf...]
  transfers between devices with their start and end apart: 11 -> 11, of which waited for: 5 -> 4; matrix products, arithmetic and copies ran while one was open for 0% -> 0% of each run, Pallas kernels for 28% -> 30%
where the time goes in v8:
time: 36 us; the launch traced here: 36.2 us
  starting transfers between devices  19.6 us (54%)
  Pallas kernels  12.3 us (34%)
  waiting for transfers between devices  2.86 us (8%)
  between operations  1.37 us (4%)
    ppermute x4, starting transfers between devices, rotated(): lax.ppermute(value, axis, [(s, (s + steps) % count) for s in range(count)])  10.2 us
    ppermute x7, starting transfers between devices, summed_round(): lax.ppermute(value, axes, [(s, s ^ m) for s in range(count)])  9.4 us
    pallas_call x1, Pallas kernels, body(): pl.pallas_call(functools.partial(own_kernel, kv_heads), out_shape=[shape(...  5.69 us
    ppermute x7, waiting for transfers between devices, summed_round(): lax.ppermute(value, axes, [(s, s ^ m) for s in range(count)])  2.6 us
    pallas_call x1, Pallas kernels, body(): pl.pallas_call(first_kernel, out_shape=shape((kv_heads, blocks, 8, lanes)...  2.26 us
    pallas_call x1, Pallas kernels, body(): pl.pallas_call(functools.partial(fetch_kernel, len(arrays)), out_shape=[s...  1.72 us
    pallas_call x2, Pallas kernels, body(): pl.pallas_call(sum_kernel, grid=(1,), out_shape=[shape(keys.shape, jnp.bf...  1.51 us
    pallas_call x1, Pallas kernels, body(): pl.pallas_call(functools.partial(prev_kernel, 0), out_shape=per_head + [s...  0.79 us
  transfers between devices with their start and end apart: 11, of which 4 were waited for; matrix products, arithmetic and copies ran while one was open for 0% of the time, Pallas kernels for 30%

profile of v8, /device:TPU:0, one launch (start us, length us, event | category | flops | bytes accessed | tf_op | source)
XLA Modules:
  0.0 36.2 jit_solution(14352740800426075996)
XLA Ops:
  1.3 3.0 %collective-permute-start = (s32[1,32]{1,0:T(1,128)S(1)}, s32[1,32]{1,0:T(1,128)S(1)}, u32[]{:S(2)}, u32[]{:S(2)}) collective-permute-start(s32[1,32]{1,0:T(1,128)S(1)} %compare_select_fusion), channel_id=1, source_target_pairs={{0,4},{1,5},{2,6},{3,7},{4,0},{5,1},{6,2},{7,3},{8,12},{9,13},{10,... | collective-permute-start | bytes 392 | tf_op jit(solution)/shard_map/ppermute | solution.py:39
  4.3 0.1 collective-permute-start.7
  4.4 3.0 %collective-permute-start.8 = (bf16[512,256]{1,0:T(8,128)(2,1)}, bf16[512,256]{1,0:T(8,128)(2,1)S(1)}, u32[]{:S(2)}, u32[]{:S(2)}) collective-permute-start(bf16[512,256]{1,0:T(8,128)(2,1)} %refs_3_.1), channel_id=1, source_target_pairs={{0,4},{4,8},{8,12},{12,16},{16,20},{20,24},{24,28},{28,0},{1,5},{5... | collective-permute-start | bytes 786440 | tf_op jit(solution)/shard_map/ppermute | solution.py:25
  7.3 0.2 collective-permute-start.3
  7.5 1.5 %collective-permute-start.2 = (s32[1,32]{1,0:T(1,128)S(1)}, s32[1,32]{1,0:T(1,128)S(1)}, u32[]{:S(2)}, u32[]{:S(2)}) collective-permute-start(s32[1,32]{1,0:T(1,128)S(1)} %fusion), channel_id=1, source_target_pairs={{0,2},{1,3},{2,0},{3,1},{4,6},{5,7},{6,4},{7,5},{8,10},{9,11},{10,... | collective-permute-start | bytes 392 | tf_op jit(solution)/shard_map/ppermute | solution.py:39
  9.0 0.3 collective-permute-start.1
  9.3 1.1 %collective-permute-done.3 = s32[1,32]{1,0:T(1,128)S(1)} collective-permute-done((s32[1,32]{1,0:T(1,128)S(1)}, s32[1,32]{1,0:T(1,128)S(1)}, u32[]{:S(2)}, u32[]{:S(2)}) %collective-permute-start.3) | collective-permute-done | bytes 160 | tf_op jit(solution)/shard_map/ppermute | solution.py:39
  10.4 0.7 %collective-permute-done.2 = s32[1,32]{1,0:T(1,128)S(1)} collective-permute-done((s32[1,32]{1,0:T(1,128)S(1)}, s32[1,32]{1,0:T(1,128)S(1)}, u32[]{:S(2)}, u32[]{:S(2)}) %collective-permute-start.2) | collective-permute-done | bytes 160 | tf_op jit(solution)/shard_map/ppermute | solution.py:39
  11.1 0.0 collective-permute-done.1
  11.1 2.6 %collective-permute-start.6 = (s32[1,32]{1,0:T(1,128)S(1)}, s32[1,32]{1,0:T(1,128)S(1)}, u32[]{:S(2)}, u32[]{:S(2)}) collective-permute-start(s32[1,32]{1,0:T(1,128)S(1)} %add_add_fusion.1.after_ref), channel_id=1, source_target_pairs={{0,24},{1,25},{2,26},{3,27},{4,28},{5,29},{6,30},{7,31},{8,16},{9,... | collective-permute-start | bytes 392 | tf_op jit(solution)/shard_map/ppermute | solution.py:39
  13.6 0.6 %collective-permute-start.5 = (s32[1,32]{1,0:T(1,128)S(1)}, s32[1,32]{1,0:T(1,128)S(1)}, u32[]{:S(2)}, u32[]{:S(2)}) collective-permute-start(s32[1,32]{1,0:T(1,128)S(1)} %add_add_fusion.1.after_ref), channel_id=1, source_target_pairs={{0,16},{1,17},{2,18},{3,19},{4,20},{5,21},{6,22},{7,23},{8,24},{9,... | collective-permute-start | bytes 392 | tf_op jit(solution)/shard_map/ppermute | solution.py:39
  14.2 1.3 %collective-permute-start.4 = (s32[1,32]{1,0:T(1,128)S(1)}, s32[1,32]{1,0:T(1,128)S(1)}, u32[]{:S(2)}, u32[]{:S(2)}) collective-permute-start(s32[1,32]{1,0:T(1,128)S(1)} %add_add_fusion.1.after_ref), channel_id=1, source_target_pairs={{0,8},{1,9},{2,10},{3,11},{4,12},{5,13},{6,14},{7,15},{8,0},{9,1},... | collective-permute-start | bytes 392 | tf_op jit(solution)/shard_map/ppermute | solution.py:39
  15.6 1.7 %fetch.1 = (bf16[512,1024]{1,0:T(8,128)(2,1)S(1)}, bf16[512,1024]{1,0:T(8,128)(2,1)S(1)}, bf16[512,256]{1,0:T(8,128)(2,1)S(1)}, bf16[512,256]{1,0:T(8,128)(2,1)S(1)}) custom-call(s32[1,32]{1,0:T(1,128)S(1)} %add_add_fusion.1.after_ref, bf16[512,1024]{1,0:T(8,128)(2,1)} %refs_0_.1, bf16[512,1024]{1,0:T(8,128)(2,1)} %refs_1_.1, bf16[512,256]{1,0:T(8,128)(2,1)} %refs_2_.1, ...), custom_call_target="tpu_custom_call" | custom-call | tf_op jit(solution)/shard_map/fetch/pallas_call | solution.py:299
  17.3 0.8 %collective-permute-done.5 = s32[1,32]{1,0:T(1,128)S(1)} collective-permute-done((s32[1,32]{1,0:T(1,128)S(1)}, s32[1,32]{1,0:T(1,128)S(1)}, u32[]{:S(2)}, u32[]{:S(2)}) %collective-permute-start.5) | collective-permute-done | bytes 160 | tf_op jit(solution)/shard_map/ppermute | solution.py:39
  18.1 0.0 collective-permute-done.4
  18.1 2.3 %first_sums.1.refs_4_.refs_7_ = f32[2,4,8,512]{3,2,1,0:T(8,128)S(1)} custom-call(s32[1]{0:T(128)} %bitcast.first_ref.refs_0_, s32[1,32]{1,0:T(1,128)S(1)} %add_add_fusion.len_ref, bf16[512,1024]{1,0:T(8,128)(2,1)S(1)} %get-tuple-element.22.q_ref.refs_0_.refs_2_, bf16[512,1024]{1,0:T(8,128)(2,1)S(1)} %get-tuple-element.23.g_ref.refs_1_.refs_3_, ...), custom_call_target="tpu_custom_call" | custom-call | tf_op jit(solution)/shard_map/first_sums/pallas_call | solution.py:308
  20.4 0.3 collective-permute-done.8.pv_ref
  20.6 0.8 %prev_grads.2 = (bf16[512,256]{1,0:T(8,128)(2,1)S(1)}, f32[4,8,512]{2,1,0:T(8,128)S(1)}, f32[4,128,512]{2,1,0:T(8,128)S(1)}, s32[1]{0:T(128)}, s32[1,512]{1,0:T(1,128)S(1)}) custom-call(s32[1]{0:T(128)} %bitcast.first_ref.refs_0_, s32[1,32]{1,0:T(1,128)S(1)} %add_add_fusion.len_ref, bf16[512,256]{1,0:T(8,128)(2,1)S(1)} %collective-permute-done.7.pk_ref, ...), custom_call_target="tpu_custom_call" | custom-call | tf_op jit(solution)/shard_map/prev_grads/pallas_call | solution.py:317
  21.4 3.2 %collective-permute-start.10 = (bf16[512,256]{1,0:T(8,128)(2,1)S(1)}, bf16[512,256]{1,0:T(8,128)(2,1)S(1)}, u32[]{:S(2)}, u32[]{:S(2)}) collective-permute-start(bf16[512,256]{1,0:T(8,128)(2,1)S(1)} %get-tuple-element.36), channel_id=1, source_target_pairs={{0,28},{4,0},{8,4},{12,8},{16,12},{20,16},{24,20},{28,24},{1,29},{... | collective-permute-start | bytes 786440 | tf_op jit(solution)/shard_map/ppermute | solution.py:25
  24.6 0.3 prev_grads.3
  24.9 4.0 %collective-permute-start.9 = (bf16[512,256]{1,0:T(8,128)(2,1)S(1)}, bf16[512,256]{1,0:T(8,128)(2,1)S(1)}, u32[]{:S(2)}, u32[]{:S(2)}) collective-permute-start(bf16[512,256]{1,0:T(8,128)(2,1)S(1)} %get-tuple-element.34), channel_id=1, source_target_pairs={{0,28},{4,0},{8,4},{12,8},{16,12},{20,16},{24,20},{28,24},{1,29},{... | collective-permute-start | bytes 786440 | tf_op jit(solution)/shard_map/ppermute | solution.py:25
  28.9 5.7 %own_grads.1 = (bf16[512,1024]{1,0:T(8,128)(2,1)}, f32[512,256]{1,0:T(8,128)S(1)}, f32[512,256]{1,0:T(8,128)S(1)}) custom-call(s32[1]{0:T(128)} %bitcast.first_ref.refs_0_, s32[1]{0:T(128)} %get-tuple-element.26.refs_1_, bf16[512,1024]{1,0:T(8,128)(2,1)S(1)} %get-tuple-element.22.q_ref.refs_0_.refs_2_, ...), custom_call_target="tpu_custom_call" | custom-call | tf_op jit(solution)/shard_map/own_grads/pallas_call | solution.py:339
  34.7 0.8 %sums.2 = (bf16[512,256]{1,0:T(8,128)(2,1)}, bf16[512,256]{1,0:T(8,128)(2,1)}) custom-call(f32[512,256]{1,0:T(8,128)S(1)} %get-tuple-element.35.keep_ref, bf16[512,256]{1,0:T(8,128)(2,1)S(1)} %collective-permute-done.10.back_ref), custom_call_target="tpu_custom_call" | custom-call | tf_op jit(solution)/shard_map/sums/pallas_call | solution.py:355
  35.4 0.8 %sums.3 = (bf16[512,256]{1,0:T(8,128)(2,1)}, bf16[512,256]{1,0:T(8,128)(2,1)}) custom-call(f32[512,256]{1,0:T(8,128)S(1)} %get-tuple-element.33.keep_ref, bf16[512,256]{1,0:T(8,128)(2,1)S(1)} %collective-permute-done.9.back_ref, bf16[512,256]{1,0:T(8,128)(2,1)} %get-tuple-element.37.refs_0_, ...), custom_call_target="tpu_custom_call", output_to_operand_aliasing={{0}: (2, {}), {1}: (3, {})} | custom-call | tf_op jit(solution)/shard_map/sums/pallas_call | solution.py:355
  (9 shorter events, 0.0 us)
Async XLA Ops:
  1.3 6.0 %collective-permute-start = (s32[1,32]{1,0:T(1,128)S(1)}, s32[1,32]{1,0:T(1,128)S(1)}, u32[]{:S(2)}, u32[]{:S(2)}) collective-permute-start(s32[1,32]{1,0:T(1,128)S(1)} %compare_select_fusion), channel_id=1, source_target_pairs={{0,4},{1,5},{2,6},{3,7},{4,0},{5,1},{6,2},{7,3},{8,12},{9,13},{10,... | collective-permute-start | bytes 392 | tf_op jit(solution)/shard_map/ppermute | solution.py:39
  4.3 16.1 %collective-permute-start.7 = (bf16[512,256]{1,0:T(8,128)(2,1)}, bf16[512,256]{1,0:T(8,128)(2,1)S(1)}, u32[]{:S(2)}, u32[]{:S(2)}) collective-permute-start(bf16[512,256]{1,0:T(8,128)(2,1)} %refs_2_.1), channel_id=1, source_target_pairs={{0,4},{4,8},{8,12},{12,16},{16,20},{20,24},{24,28},{28,0},{1,5},{5... | collective-permute-start | bytes 786440 | tf_op jit(solution)/shard_map/ppermute | solution.py:25
  4.4 16.3 %collective-permute-start.8 = (bf16[512,256]{1,0:T(8,128)(2,1)}, bf16[512,256]{1,0:T(8,128)(2,1)S(1)}, u32[]{:S(2)}, u32[]{:S(2)}) collective-permute-start(bf16[512,256]{1,0:T(8,128)(2,1)} %refs_3_.1), channel_id=1, source_target_pairs={{0,4},{4,8},{8,12},{12,16},{16,20},{20,24},{24,28},{28,0},{1,5},{5... | collective-permute-start | bytes 786440 | tf_op jit(solution)/shard_map/ppermute | solution.py:25
  7.3 3.0 %collective-permute-start.3 = (s32[1,32]{1,0:T(1,128)S(1)}, s32[1,32]{1,0:T(1,128)S(1)}, u32[]{:S(2)}, u32[]{:S(2)}) collective-permute-start(s32[1,32]{1,0:T(1,128)S(1)} %fusion), channel_id=1, source_target_pairs={{0,3},{1,2},{2,1},{3,0},{4,7},{5,6},{6,5},{7,4},{8,11},{9,10},{10,... | collective-permute-start | bytes 392 | tf_op jit(solution)/shard_map/ppermute | solution.py:39
  7.5 3.5 %collective-permute-start.2 = (s32[1,32]{1,0:T(1,128)S(1)}, s32[1,32]{1,0:T(1,128)S(1)}, u32[]{:S(2)}, u32[]{:S(2)}) collective-permute-start(s32[1,32]{1,0:T(1,128)S(1)} %fusion), channel_id=1, source_target_pairs={{0,2},{1,3},{2,0},{3,1},{4,6},{5,7},{6,4},{7,5},{8,10},{9,11},{10,... | collective-permute-start | bytes 392 | tf_op jit(solution)/shard_map/ppermute | solution.py:39
  9.0 2.1 %collective-permute-start.1 = (s32[1,32]{1,0:T(1,128)S(1)}, s32[1,32]{1,0:T(1,128)S(1)}, u32[]{:S(2)}, u32[]{:S(2)}) collective-permute-start(s32[1,32]{1,0:T(1,128)S(1)} %fusion), channel_id=1, source_target_pairs={{0,1},{1,0},{2,3},{3,2},{4,5},{5,4},{6,7},{7,6},{8,9},{9,8},{10,11... | collective-permute-start | bytes 392 | tf_op jit(solution)/shard_map/ppermute | solution.py:39
  11.1 6.2 %collective-permute-start.6 = (s32[1,32]{1,0:T(1,128)S(1)}, s32[1,32]{1,0:T(1,128)S(1)}, u32[]{:S(2)}, u32[]{:S(2)}) collective-permute-start(s32[1,32]{1,0:T(1,128)S(1)} %add_add_fusion.1.after_ref), channel_id=1, source_target_pairs={{0,24},{1,25},{2,26},{3,27},{4,28},{5,29},{6,30},{7,31},{8,16},{9,... | collective-permute-start | bytes 392 | tf_op jit(solution)/shard_map/ppermute | solution.py:39
  13.6 4.4 %collective-permute-start.5 = (s32[1,32]{1,0:T(1,128)S(1)}, s32[1,32]{1,0:T(1,128)S(1)}, u32[]{:S(2)}, u32[]{:S(2)}) collective-permute-start(s32[1,32]{1,0:T(1,128)S(1)} %add_add_fusion.1.after_ref), channel_id=1, source_target_pairs={{0,16},{1,17},{2,18},{3,19},{4,20},{5,21},{6,22},{7,23},{8,24},{9,... | collective-permute-start | bytes 392 | tf_op jit(solution)/shard_map/ppermute | solution.py:39
  14.2 3.9 %collective-permute-start.4 = (s32[1,32]{1,0:T(1,128)S(1)}, s32[1,32]{1,0:T(1,128)S(1)}, u32[]{:S(2)}, u32[]{:S(2)}) collective-permute-start(s32[1,32]{1,0:T(1,128)S(1)} %add_add_fusion.1.after_ref), channel_id=1, source_target_pairs={{0,8},{1,9},{2,10},{3,11},{4,12},{5,13},{6,14},{7,15},{8,0},{9,1},... | collective-permute-start | bytes 392 | tf_op jit(solution)/shard_map/ppermute | solution.py:39
  21.4 13.2 %collective-permute-start.10 = (bf16[512,256]{1,0:T(8,128)(2,1)S(1)}, bf16[512,256]{1,0:T(8,128)(2,1)S(1)}, u32[]{:S(2)}, u32[]{:S(2)}) collective-permute-start(bf16[512,256]{1,0:T(8,128)(2,1)S(1)} %get-tuple-element.36), channel_id=1, source_target_pairs={{0,28},{4,0},{8,4},{12,8},{16,12},{20,16},{24,20},{28,24},{1,29},{... | collective-permute-start | bytes 786440 | tf_op jit(solution)/shard_map/ppermute | solution.py:25
  24.9 10.5 %collective-permute-start.9 = (bf16[512,256]{1,0:T(8,128)(2,1)S(1)}, bf16[512,256]{1,0:T(8,128)(2,1)S(1)}, u32[]{:S(2)}, u32[]{:S(2)}) collective-permute-start(bf16[512,256]{1,0:T(8,128)(2,1)S(1)} %get-tuple-element.34), channel_id=1, source_target_pairs={{0,28},{4,0},{8,4},{12,8},{16,12},{20,16},{24,20},{28,24},{1,29},{... | collective-permute-start | bytes 786440 | tf_op jit(solution)/shard_map/ppermute | solution.py:25
